TPU v7x, 32 devices: a whole 2x2x4 slice. The times are simulated.
32 devices in a mesh: lat: 8 (over z, y), lon: 4 (over x, core).
Axes of the slice: x: 2, y: 2, z: 4, core: 2. Of those that a mesh axis runs over, the one named last changes fastest.
Arguments:
- state: float32 [5, 24, 8, 8, 2880], P(None, 'lat', None, None, 'lon'), may hold values from -6 to 6
- courant_x: float32 [24, 8, 8, 2880], P('lat', None, None, 'lon'), may hold values from -4 to 4
- courant_y: float32 [24, 8, 8, 2880], P('lat', None, None, 'lon'), may hold values from -4 to 4
- block_of_slot: int32 [24], P('lat'), may hold values from 0 to 23, as said below
- face_source: int32 [24, 2], P('lat'), may hold values from -1 to 23, as said below
- cutoff: int32 [192], replicated, may hold values from 0 to 256, as said below
Outputs:
- new_state: float32 [5, 24, 8, 8, 2880], P(None, 'lat', None, None, 'lon')
Inputs may be any that keep to these rules, and one draw needn't show every extreme that they name: `block_of_slot`: each block number appears once. The polar blocks are the first and the last 4 block numbers; the 3 slots of one index of lat hold at most 2 polar blocks, and some index holds 2. `face_source`: entry 0 of slot s is the slot holding block block_of_slot[s] - 1 and entry 1 the slot holding block block_of_slot[s] + 1; -1 where that block does not exist. Rows of polar blocks have a cutoff of 1 or more; all other rows have 0.
All inputs are finite; a program needn't handle non-finite values.
Results may differ from a plain program's by a relative error of at most 0.00005.
Values sent between devices are 32-bit elements; how exact they have to be, the bound alone decides.
No kernel may reach another device: no remote copies, remote signals or barrier semaphores. Data moves between devices by JAX's collectives and lax.ppermute only.
A program may use at most 64 MiB of HBM per device.

v0:
```python
import functools
import math

import jax
import jax.numpy as jnp
import numpy as np
from jax import lax
from jax.experimental import pallas as pl
from jax.experimental.pallas import tpu as pltpu
from jax.sharding import PartitionSpec as P

NLON = 2880
KCUT = 256
LANES = 128
MIB = 1024 * 1024
BF16 = jnp.bfloat16
F32 = jnp.float32


def phases(columns):
    wavenumber = np.arange(KCUT, dtype=np.int64)
    return (columns[:, None] * wavenumber[None, :] % NLON).astype(np.float64) * (
        2.0 * math.pi / NLON
    )


def basis_tables(width):
    phase = phases(np.arange(width, dtype=np.int64))
    table = np.concatenate([np.cos(phase), np.sin(phase)], axis=1).astype(np.float32)
    high = table.astype(jnp.bfloat16)
    low = (table - high.astype(np.float32)).astype(jnp.bfloat16)
    forward = (jnp.asarray(high), jnp.asarray(low))
    inverse = (
        jnp.asarray(np.ascontiguousarray(high.T)),
        jnp.asarray(np.ascontiguousarray(low.T)),
    )
    return forward, inverse


def turn_table(lon, width):
    phase = phases(np.arange(lon, dtype=np.int64) * width)
    table = np.concatenate([np.cos(phase), np.sin(phase)], axis=1).astype(np.float32)
    return jnp.asarray(table[:, None, :])


def split_dot(rows, high, low, axis=0):
    rows_high = rows.astype(BF16)
    rows_low = (rows - rows_high.astype(F32)).astype(BF16)
    dot = functools.partial(
        lax.dot_general,
        dimension_numbers=(((1,), (axis,)), ((), ())),
        preferred_element_type=F32,
    )
    return dot(rows_high, high) + (dot(rows_low, high) + dot(rows_high, low))


def turned(spec, turn, sign):
    real, imag = spec[:, :KCUT], spec[:, KCUT:]
    cos, sin = turn[:, :KCUT], turn[:, KCUT:] * sign
    return jnp.concatenate([real * cos - imag * sin, imag * cos + real * sin], axis=1)


def row_weights(cut):
    column = lax.broadcasted_iota(jnp.int32, (1, 2 * KCUT), 1)
    wavenumber = jnp.where(column >= KCUT, column - KCUT, column)
    scale = jnp.where(wavenumber == 0, 1.0 / NLON, 2.0 / NLON).astype(F32)
    return jnp.where(wavenumber < cut, scale, 0.0)


def pick_slots(block_ref, cutoff_ref, rows):
    polar1 = cutoff_ref[block_ref[1] * rows] > 0
    polar2 = cutoff_ref[block_ref[2] * rows] > 0
    rest = jnp.where(polar2, jnp.where(polar1, 0, 1), 2)
    return jnp.where(rest == 0, 1, 0), jnp.where(rest == 2, 1, 2), rest


def mine_first(pair, core):
    a, b = pair
    return jnp.where(core == 0, a, b), jnp.where(core == 0, b, a)


def vmem(count):
    return [pl.BlockSpec(memory_space=pltpu.VMEM)] * count


def smem(count):
    return [pl.BlockSpec(memory_space=pltpu.SMEM)] * count


def edge_kernel(lane_last, head_ref, tail_ref, wind_ref, west_ref, east_ref):
    fields, slots, rows = head_ref.shape[:3]
    lane = lax.broadcasted_iota(jnp.int32, (8, LANES), 1)
    for s in range(slots):
        west = jnp.zeros((8, LANES), F32)
        east = jnp.zeros((8, LANES), F32)
        for r in range(rows):
            for f in range(fields):
                here = lane == f * rows + r
                west = jnp.where(here, tail_ref[f, s, r, :, lane_last : lane_last + 1], west)
                east = jnp.where(here, head_ref[f, s, r, :, 0:1], east)
            here = lane == fields * rows + r
            west = jnp.where(here, wind_ref[s, r, :, lane_last : lane_last + 1], west)
        west_ref[s] = west
        east_ref[s] = east


def edges(state, courant_x):
    fields, slots, rows, levels, width = state.shape
    last = (width - 1) // LANES
    out = jax.ShapeDtypeStruct((slots, levels, LANES), F32)
    return pl.pallas_call(
        functools.partial(edge_kernel, (width - 1) % LANES),
        grid=(1,),
        in_specs=[
            pl.BlockSpec((fields, slots, rows, levels, LANES), lambda i: (0, 0, 0, 0, 0)),
            pl.BlockSpec((fields, slots, rows, levels, LANES), lambda i: (0, 0, 0, 0, last)),
            pl.BlockSpec((slots, rows, levels, LANES), lambda i: (0, 0, 0, last)),
        ],
        out_specs=[pl.BlockSpec((slots, levels, LANES), lambda i: (0, 0, 0))] * 2,
        out_shape=[out, out],
        cost_estimate=pl.CostEstimate(flops=10**5, bytes_accessed=1200000, transcendentals=0),
        name="edges",
    )(state, state, courant_x)


PIECE = 200
BACK = 184


def tile_of(slab, t, width):
    part = slab[:, t * LANES : min((t + 1) * LANES, width)]
    if part.shape[1] < LANES:
        part = jnp.concatenate([part, jnp.zeros((8, LANES - part.shape[1]), F32)], axis=1)
    return part


def pack_kernel(width, first_ref, last_ref, wind_ref, block_ref, out_ref):
    fields, slots = first_ref.shape[:2]
    tiles = -(-width // LANES)

    def put(row, tile):
        out_ref[pl.ds(row, 8, stride=PIECE), :] = tile

    for j in range(slots):
        half = wind_ref[j, 0] * 0.5
        for t in range(tiles):
            row = {0: 192 + 2 * j, 1: 193 + 2 * j, 2: 64 * j + 62, 3: 64 * j + 63}.get(
                t, 64 * j + 26 + t
            )
            put(row, tile_of(half, t, width))
        for f in range(fields):
            north = last_ref[f, j, 0] * half
            south = first_ref[f, j, 0]
            for t in range(tiles):
                put(64 * j + f * tiles + t, tile_of(north, t, width))
                put(64 * j + 32 + f * tiles + t, tile_of(south, t, width))
    lane = lax.broadcasted_iota(jnp.int32, (8, LANES), 1)
    table = jnp.zeros((8, LANES), F32)
    for j in range(slots):
        table = jnp.where(lane == j, block_ref[j].astype(F32), table)
    put(198, table)
    put(199, table)


def pack(state, courant_y, block):
    fields, slots, rows, levels, width = state.shape
    return pl.pallas_call(
        functools.partial(pack_kernel, width),
        grid=(1,),
        in_specs=[
            pl.BlockSpec((fields, slots, 1, levels, width), lambda i: (0, 0, 0, 0, 0)),
            pl.BlockSpec((fields, slots, 1, levels, width), lambda i: (0, 0, rows - 1, 0, 0)),
            pl.BlockSpec((slots, 1, levels, width), lambda i: (0, rows - 1, 0, 0)),
            pl.BlockSpec(memory_space=pltpu.SMEM),
        ],
        out_specs=pl.BlockSpec((levels * PIECE, LANES), lambda i: (0, 0)),
        out_shape=jax.ShapeDtypeStruct((levels * PIECE, LANES), F32),
        cost_estimate=pl.CostEstimate(flops=10**5, bytes_accessed=1700000, transcendentals=0),
        name="pack",
    )(state, state, courant_y, block)


def face_kernel(
    got_ref, cutoff_ref, later_in_ref, out_ref, later_ref, face_ref, table_ref, slot_ref, sem
):
    del later_in_ref, later_ref
    parts = got_ref.shape[0]
    slots = face_ref.shape[0] // parts
    count = parts * slots
    copy = pltpu.make_async_copy(got_ref.at[:, 192:200, :], table_ref, sem)
    copy.start()
    copy.wait()
    blocks = [table_ref[s // slots, 6, s % slots].astype(jnp.int32) for s in range(count)]
    slot_ref[0] = -1
    slot_ref[count + 1] = -1
    for s in range(count):
        slot_ref[blocks[s] + 1] = s
    for s in range(count):
        src, j = divmod(s, slots)
        south = slot_ref[blocks[s] + 2]
        safe = jnp.maximum(south, 0)
        from_src = lax.div(safe, slots)
        from_slot = safe - from_src * slots
        half = jnp.concatenate(
            [
                got_ref[src, 192 + 2 * j : 194 + 2 * j, :],
                got_ref[src, 64 * j + 62 : 64 * j + 64, :],
                got_ref[src, 64 * j + 30 : 64 * j + 32, :],
            ],
            axis=0,
        )
        half = jnp.concatenate([half] * 5 + [half[:2]], axis=0)
        other = got_ref[from_src, pl.ds(pl.multiple_of(64 * from_slot + 32, 32), 32), :]
        face = got_ref[src, 64 * j : 64 * j + 32, :] + half * other
        face_ref[s] = jnp.where(south >= 0, face, 0.0)
    for d in range(parts):
        first, second, rest = pick_slots(blocks[slots * d : slots * d + slots], cutoff_ref, 8)
        for i, slot in enumerate((first, second, rest)):
            row = 60 * i
            block = jnp.where(
                slot == 0,
                blocks[slots * d],
                jnp.where(slot == 1, blocks[slots * d + 1], blocks[slots * d + 2]),
            )
            north = slot_ref[block]
            out_ref[d, row : row + 30] = jnp.where(
                north >= 0, face_ref[jnp.maximum(north, 0), :30], 0.0
            )
            out_ref[d, row + 30 : row + 60] = face_ref[slots * d + slot, :30]
        out_ref[d, 180:184] = jnp.zeros((4, LANES), F32)


def faces_of_pieces(got, slots, cutoff, later):
    parts = got.shape[0]
    return pl.pallas_call(
        face_kernel,
        in_specs=vmem(1) + smem(1) + [pl.BlockSpec(memory_space=pl.ANY)],
        out_specs=vmem(1) + [pl.BlockSpec(memory_space=pl.ANY)],
        out_shape=[
            jax.ShapeDtypeStruct((parts, BACK, LANES), F32),
            jax.ShapeDtypeStruct(later.shape, F32),
        ],
        input_output_aliases={2: 1},
        scratch_shapes=[
            pltpu.VMEM((parts * slots, 32, LANES), F32),
            pltpu.SMEM((parts, 8, LANES), F32),
            pltpu.SMEM((parts * slots + 2,), jnp.int32),
            pltpu.SemaphoreType.DMA(()),
        ],
        cost_estimate=pl.CostEstimate(flops=10**5, bytes_accessed=1600000, transcendentals=0),
        name="faces",
    )(got, cutoff, later)


def to_pieces(units, parts):
    count, levels, width = units.shape
    groups = math.gcd(parts, levels)
    chunks = parts // groups
    span = -(-width // chunks)
    units = jnp.pad(units, ((0, 0), (0, 0), (0, span * chunks - width)))
    units = units.reshape(count, groups, levels // groups, chunks, span)
    return units.transpose(1, 3, 0, 2, 4).reshape(parts, count, levels // groups * span)


def from_pieces(pieces, levels, width):
    parts, count, _ = pieces.shape
    groups = math.gcd(parts, levels)
    chunks = parts // groups
    span = -(-width // chunks)
    pieces = pieces.reshape(groups, chunks, count, levels // groups, span)
    return pieces.transpose(2, 0, 3, 1, 4).reshape(count, levels, chunks * span)[:, :, :width]


def exchange_faces(state, courant_y, face_source):
    fields, slots, rows, levels, width = state.shape
    lat = lax.axis_size("lat")
    count = 2 * fields + 1
    first = state[:, :, 0].transpose(1, 0, 2, 3)
    last = state[:, :, rows - 1].transpose(1, 0, 2, 3)
    half = courant_y[:, rows - 1][:, None] * 0.5
    units = jnp.concatenate([first, last * half, half], axis=1)
    sent = to_pieces(units.reshape(slots * count, levels, width), lat)
    span = sent.shape[2]
    table = jnp.pad(
        face_source.astype(F32).reshape(1, slots * 2), ((0, 0), (0, span - slots * 2))
    )
    sent = jnp.concatenate([sent, jnp.broadcast_to(table[None], (lat, 1, span))], axis=1)
    got = lax.all_to_all(sent, "lat", 0, 0, tiled=True)
    indices = got[:, slots * count, : slots * 2].reshape(lat * slots, 2).astype(jnp.int32)
    data = got[:, : slots * count].reshape(lat * slots, count, span)
    north, south = indices[:, 0], indices[:, 1]
    face = data[:, fields : 2 * fields] + data[:, 2 * fields :] * data[
        jnp.maximum(south, 0), :fields
    ]
    face = jnp.where((south >= 0)[:, None, None], face, 0.0)
    face_north = jnp.where((north >= 0)[:, None, None], face[jnp.maximum(north, 0)], 0.0)
    back = jnp.concatenate([face_north, face], axis=1).reshape(lat, slots * 2 * fields, span)
    back = lax.all_to_all(back, "lat", 0, 0, tiled=True)
    return from_pieces(back, levels, width).reshape(slots, 2, fields, levels, width)


def tendency_kernel(
    state_ref,
    cx_ref,
    cy_ref,
    west_ref,
    east_ref,
    high_ref,
    low_ref,
    turn_ref,
    place_ref,
    block_ref,
    cutoff_ref,
    out_ref,
    mine_ref,
    other_ref,
    tend_ref,
    base_ref,
    sem,
):
    fields, slots, rows, levels, width = state_ref.shape

    def streamed(s):
        return pltpu.make_async_copy(base_ref.at[:, s], out_ref.at[:, s], sem.at[s])


    tiles = -(-width // LANES)
    lane = lax.broadcasted_iota(jnp.int32, (levels, LANES), 1)
    head, tail, last = lane == 0, lane == LANES - 1, lane == (width - 1) % LANES

    def load(ref, *index):
        out = []
        for t in range(tiles):
            part = ref[index + (slice(None), slice(t * LANES, min((t + 1) * LANES, width)))]
            if part.shape[1] < LANES:
                pad = jnp.zeros((levels, LANES - part.shape[1]), F32)
                part = jnp.concatenate([part, pad], axis=1)
            out.append(part)
        return out

    def one_slot(s, carry):
        west, east = west_ref[s], east_ref[s]
        for f in range(fields):
            above = None
            now = load(state_ref, f, s, 0)
            for r in range(rows):
                column = f * rows + r
                left = [pltpu.roll(x, LANES - 1, 1) for x in now]
                left = [
                    jnp.where(tail, left[t + 1], left[t])
                    if t + 1 < tiles
                    else jnp.where(last, east[:, column : column + 1], left[t])
                    for t in range(tiles)
                ]
                half = [x * 0.5 for x in load(cx_ref, s, r)]
                flux = [h * (x + y) for h, x, y in zip(half, now, left)]
                wind = west[:, fields * rows + r : fields * rows + r + 1] * 0.5
                first = wind * (west[:, column : column + 1] + now[0])
                right = [pltpu.roll(x, 1, 1) for x in flux]
                right = [jnp.where(head, y, x) for x, y in zip(right, [first] + right[:-1])]
                change = [x - y for x, y in zip(right, flux)]
                if above is not None:
                    change = [x + y for x, y in zip(change, above)]
                if r + 1 < rows:
                    later = load(state_ref, f, s, r + 1)
                    half = load(cy_ref, s, r)
                    above = [h * 0.5 * (x + y) for h, x, y in zip(half, now, later)]
                    change = [x - y for x, y in zip(change, above)]
                for t in range(tiles):
                    stop = min((t + 1) * LANES, width)
                    base = now[t] + change[t]
                    tend_ref[f, s, r, :, t * LANES : stop] = change[t][:, : stop - t * LANES]
                    base_ref[f, s, r, :, t * LANES : stop] = base[:, : stop - t * LANES]
                now = later
        streamed(s).start()
        return carry

    lax.fori_loop(0, slots, one_slot, 0)
    turn = turn_ref[place_ref[0]]
    first, second, _ = pick_slots(block_ref, cutoff_ref, rows)
    mine, other = mine_first((first, second), place_ref[1])
    for slot, spec_ref in ((other, other_ref), (mine, mine_ref)):
        spec = split_dot(
            tend_ref[:, slot].reshape(fields * rows * levels, width), high_ref[...], low_ref[...]
        )
        spec_ref[...] = turned(spec, turn, 1.0)
    for s in range(slots):
        streamed(s).wait()


def local_tendency(state, courant_x, courant_y, west, east, forward, turn, place, block, cutoff):
    fields, slots, rows, levels, width = state.shape
    count = fields * rows * levels
    spec = jax.ShapeDtypeStruct((count, 2 * KCUT), F32)
    return pl.pallas_call(
        tendency_kernel,
        in_specs=vmem(8) + smem(3),
        out_specs=[pl.BlockSpec(memory_space=pl.ANY)] + vmem(2),
        out_shape=[jax.ShapeDtypeStruct(state.shape, F32), spec, spec],
        scratch_shapes=[
            pltpu.VMEM(state.shape, F32),
            pltpu.VMEM(state.shape, F32),
            pltpu.SemaphoreType.DMA((slots,)),
        ],
        compiler_params=pltpu.CompilerParams(vmem_limit_bytes=50 * MIB),
        cost_estimate=pl.CostEstimate(
            flops=6 * count * 2 * KCUT * width * 2, bytes_accessed=9 * 10**6, transcendentals=0
        ),
        name="tendency",
    )(state, courant_x, courant_y, west, east, *forward, turn, place, block, cutoff)


def chosen_slot(i, place_ref, block_ref, cutoff_ref, rows):
    first, second, _ = pick_slots(block_ref, cutoff_ref, rows)
    return jnp.where(i == place_ref[1], first, second)


def main_kernel(
    place_ref,
    block_ref,
    cutoff_ref,
    state_ref,
    base_ref,
    mine_ref,
    away_ref,
    high_ref,
    low_ref,
    turn_ref,
    after_ref,
    out_ref,
    token_ref,
):
    fields, _, rows, levels, width = state_ref.shape
    del after_ref
    token_ref[...] = jnp.zeros_like(token_ref)
    i = pl.program_id(0)
    turn = turn_ref[place_ref[0]]
    slot = chosen_slot(i, place_ref, block_ref, cutoff_ref, rows)
    spec = turned(jnp.where(i == 0, mine_ref[...], away_ref[...]), turn, -1.0)
    spec = spec.reshape(fields, rows, levels, 2 * KCUT)
    cuts = [cutoff_ref[block_ref[slot] * rows + r] for r in range(rows)]
    spec = jnp.concatenate(
        [spec[:, r : r + 1] * row_weights(cuts[r]) for r in range(rows)], axis=1
    )
    smooth = split_dot(
        spec.reshape(fields * rows * levels, 2 * KCUT), high_ref[...], low_ref[...]
    ).reshape(fields, rows, levels, width)
    for r in range(rows):
        out_ref[:, 0, r] = jnp.where(
            cuts[r] > 0, state_ref[:, 0, r] + smooth[:, r], base_ref[:, 0, r]
        )


def main_part(after, state, base, mine, away, inverse, turn, place, block, cutoff):
    fields, slots, rows, levels, width = state.shape
    slot_block = pl.BlockSpec(
        (fields, 1, rows, levels, width),
        lambda i, *scalars: (0, chosen_slot(i, *scalars, rows), 0, 0, 0),
    )
    return pl.pallas_call(
        main_kernel,
        grid_spec=pltpu.PrefetchScalarGridSpec(
            num_scalar_prefetch=3,
            grid=(2,),
            in_specs=[slot_block, slot_block] + vmem(6),
            out_specs=[slot_block, pl.BlockSpec((1, 2 * KCUT), lambda i, *scalars: (0, 0))],
        ),
        out_shape=[
            jax.ShapeDtypeStruct(state.shape, F32),
            jax.ShapeDtypeStruct((1, 2 * KCUT), F32),
        ],
        input_output_aliases={4: 0},
        compiler_params=pltpu.CompilerParams(vmem_limit_bytes=50 * MIB),
        cost_estimate=pl.CostEstimate(
            flops=12 * mine.shape[0] * 2 * KCUT * width,
            bytes_accessed=6 * 10**6,
            transcendentals=0,
        ),
        name="main",
    )(place, block, cutoff, state, base, mine, away, *inverse, turn, after)


def unpack(ref, base, stride, put, fields, width):
    tiles = -(-width // LANES)
    for f in range(fields):
        for t in range(tiles):
            tile = ref[pl.ds(base + f * tiles + t, 8, stride=stride), :]
            stop = min((t + 1) * LANES, width)
            put(f, t * LANES, stop, tile[:, : stop - t * LANES])


def rim_kernel(
    packed,
    got_ref,
    high_ref,
    low_ref,
    turn_ref,
    place_ref,
    faces_ref,
    mine_ref,
    other_ref,
    token_ref,
):
    _, _, fields, levels, width = faces_ref.shape
    token_ref[...] = jnp.zeros_like(token_ref)
    if packed:
        for i in range(2):
            for side in range(2):

                def put(f, start, stop, tile, i=i, side=side):
                    faces_ref[i, side, f, :, start:stop] = tile

                unpack(got_ref, 60 * i + 30 * side, BACK, put, fields, width)
    else:
        faces_ref[...] = got_ref[...]
    turn = turn_ref[place_ref[0]]
    core = place_ref[1]
    both = jnp.concatenate(
        [part for i in (core, 1 - core) for part in (faces_ref[i, 0], -faces_ref[i, 1])], axis=0
    ).reshape(4 * fields * levels, width)
    spec = turned(split_dot(both, high_ref[...], low_ref[...], axis=1), turn, 1.0)
    mine_ref[...] = spec[: 2 * fields * levels]
    other_ref[...] = spec[2 * fields * levels :]


def rim_spectra(got, shape, inverse, turn, place):
    _, _, fields, levels, width = shape
    spec = jax.ShapeDtypeStruct((2 * fields * levels, 2 * KCUT), F32)
    return pl.pallas_call(
        functools.partial(rim_kernel, got.ndim == 2),
        in_specs=vmem(4) + smem(1),
        out_specs=vmem(4),
        out_shape=[
            jax.ShapeDtypeStruct(shape, F32),
            spec,
            spec,
            jax.ShapeDtypeStruct((8, LANES), F32),
        ],
        compiler_params=pltpu.CompilerParams(vmem_limit_bytes=50 * MIB),
        cost_estimate=pl.CostEstimate(
            flops=24 * fields * levels * 2 * KCUT * width,
            bytes_accessed=3 * 10**6,
            transcendentals=0,
        ),
        name="rim_spectra",
    )(got, *inverse, turn, place)


def final_kernel(
    packed,
    main_ref,
    pair_ref,
    back_ref,
    mine_ref,
    away_ref,
    high_ref,
    low_ref,
    turn_ref,
    place_ref,
    block_ref,
    cutoff_ref,
    out_ref,
    smooth_ref,
):
    fields, slots, _, levels, width = main_ref.shape
    rows = 8
    side = pl.program_id(0)
    row = side * (rows - 1)
    turn = turn_ref[place_ref[0]]
    core = place_ref[1]
    first, second, rest = pick_slots(block_ref, cutoff_ref, rows)
    mine, other = mine_first((first, second), core)
    count = fields * levels

    @pl.when(side == 0)
    def _():
        spec = [
            turned(ref[j * count : (j + 1) * count], turn, -1.0)
            * row_weights(cutoff_ref[block_ref[slot] * rows + j * (rows - 1)])
            for slot, ref in ((mine, mine_ref), (other, away_ref))
            for j in range(2)
        ]
        smooth = split_dot(jnp.concatenate(spec, axis=0), high_ref[...], low_ref[...])
        smooth_ref[...] = smooth.reshape(2, 2, fields, levels, width)

    sign = jnp.where(side == 0, 1.0, -1.0).astype(F32)
    if packed:

        def put(f, start, stop, tile):
            old = main_ref[f, rest, 0, :, start:stop]
            out_ref[f, rest, 0, :, start:stop] = old + tile * sign

        unpack(back_ref, 120 + 30 * side, BACK, put, fields, width)
    else:
        out_ref[:, rest, 0] = main_ref[:, rest, 0] + back_ref[side] * sign
    cuts = [cutoff_ref[block_ref[slot] * rows + row] for slot in (mine, other)]
    for i, (slot, order) in enumerate(((mine, core), (other, 1 - core))):
        out_ref[:, slot, 0] = main_ref[:, slot, 0] + jnp.where(
            cuts[i] > 0, smooth_ref[i, side], pair_ref[order, side] * sign
        )


def final_part(main, pair, back, mine, away, inverse, turn, place, block, cutoff):
    fields, slots, rows, levels, width = main.shape
    block_spec = pl.BlockSpec(
        (fields, slots, 1, levels, width), lambda i: (0, 0, i * (rows - 1), 0, 0)
    )
    return pl.pallas_call(
        functools.partial(final_kernel, back.ndim == 2),
        grid=(2,),
        in_specs=[block_spec] + vmem(7) + smem(3),
        out_specs=block_spec,
        scratch_shapes=[pltpu.VMEM((2, 2, fields, levels, width), F32)],
        out_shape=jax.ShapeDtypeStruct(main.shape, F32),
        input_output_aliases={0: 0},
        compiler_params=pltpu.CompilerParams(vmem_limit_bytes=50 * MIB),
        cost_estimate=pl.CostEstimate(
            flops=12 * mine.shape[0] * 2 * KCUT * width,
            bytes_accessed=4 * 10**6,
            transcendentals=0,
        ),
        name="final",
    )(main, pair, back, mine, away, *inverse, turn, place, block, cutoff)


def swap(array, bit):
    size = lax.axis_size("lon")
    return lax.ppermute(array, "lon", [(i, i ^ bit) for i in range(size)])


def lon_sum(mine, other, last=None):
    total = mine + swap(other, 1)
    bit = 2
    while bit < lax.axis_size("lon"):
        total = total + swap(total, bit)
        bit *= 2
    if last is not None:
        total = total + last
    return total, swap(total, 1)


def shards(state, courant_x, courant_y, block_of_slot, face_source, cutoff):
    fields, slots, rows, levels, width = state.shape
    lat, lon = lax.axis_size("lat"), lax.axis_size("lon")
    lon_index = lax.axis_index("lon")
    place = jnp.stack([lon_index, lon_index % 2]).astype(jnp.int32)
    forward, inverse = basis_tables(width)
    turn = turn_table(lon, width)
    tables = (turn, place, block_of_slot, cutoff)

    packed = lat == levels == 8 and -(-width // LANES) * fields == 30
    if packed:
        sent = pack(state, courant_y, block_of_slot).reshape(lat, PIECE, LANES)
        got = lax.all_to_all(sent, "lat", 0, 0, tiled=True)

    west, east = edges(state, courant_x)
    west = lax.ppermute(west, "lon", [(i, (i + 1) % lon) for i in range(lon)])
    east = lax.ppermute(east, "lon", [((i + 1) % lon, i) for i in range(lon)])
    base, mine, other = local_tendency(
        state, courant_x, courant_y, west, east, forward, *tables
    )
    if packed:
        back, mine = faces_of_pieces(got, slots, cutoff, mine)
        back = lax.all_to_all(back, "lat", 0, 0, tiled=True)
        pair = rest = back.reshape(lat * BACK, LANES)
    else:
        faces = exchange_faces(state, courant_y, face_source)
        picked = pick_slots(block_of_slot, cutoff, rows)
        pair, rest = faces[jnp.stack(picked[:2])], faces[picked[2]]
    total, away = lon_sum(mine, other)
    shape = (2, 2, fields, levels, width)
    pair, rim_mine, rim_other, token = rim_spectra(pair, shape, inverse, turn, place)
    main, token = main_part(token, state, base, total, away, inverse, *tables)
    rim_total, rim_away = lon_sum(rim_mine, rim_other, token)
    return final_part(main, pair, rest, rim_total, rim_away, inverse, *tables)


def solution(mesh):
    placed = (
        P(None, "lat", None, None, "lon"),
        P("lat", None, None, "lon"),
        P("lat", None, None, "lon"),
        P("lat"),
        P("lat", None),
        P(),
    )
    return jax.shard_map(
        shards,
        mesh=mesh,
        in_specs=placed,
        out_specs=P(None, "lat", None, None, "lon"),
        check_vma=False,
    )
```

profile of v0, /device:TPU:0, one launch (start us, length us, event | category | flops | bytes accessed | tf_op | source)
XLA Modules:
  0.0 73.4 jit_solution(10324576732789078328)
XLA Ops:
  0.0 2.2 %pack.1 = f32[1600,128]{1,0:T(8,128)} custom-call(f32[5,3,8,8,720]{4,3,2,1,0:T(8,128)} %state_ref.3, f32[5,3,8,8,720]{4,3,2,1,0:T(8,128)} %state_ref.3, f32[3,8,8,720]{3,2,1,0:T(8,128)} %wind_ref.3, s32[3]{0:T(128)} %block_ref.7), custom_call_target="tpu_custom_call" | custom-call | flops 100000 | bytes 1700000 | tf_op jit(solution)/shard_map/pack/pallas_call | solution.py:167
  2.2 7.3 %all-to-all-start = ((f32[8,200,128]{2,1,0:T(8,128)}), f32[8,200,128]{2,1,0:T(8,128)}, u32[]{:S(2)}, u32[]{:S(2)}) async-start(f32[8,200,128]{2,1,0:T(8,128)} %bitcast.8), calls=%async_computation | async-start | bytes 1638400 | tf_op jit(solution)/shard_map/all_to_all | solution.py:654
  9.5 0.0 copy-start.5
  9.5 0.0 copy-start.6
  9.5 0.0 copy-start.7
  9.6 2.4 %edges.1 = (f32[3,8,128]{2,1,0:T(8,128)}, f32[3,8,128]{2,1,0:T(8,128)}) custom-call(f32[5,3,8,8,720]{4,3,2,1,0:T(8,128)} %state_ref.3, f32[5,3,8,8,720]{4,3,2,1,0:T(8,128)} %state_ref.3, f32[3,8,8,720]{3,2,1,0:T(8,128)} %cx_ref.1), custom_call_target="tpu_custom_call" | custom-call | flops 100000 | bytes 1200000 | tf_op jit(solution)/shard_map/edges/pallas_call | solution.py:111
  12.0 1.7 %collective-permute-start.1 = (f32[3,8,128]{2,1,0:T(8,128)}, f32[3,8,128]{2,1,0:T(8,128)S(1)}, u32[]{:S(2)}, u32[]{:S(2)}) collective-permute-start(f32[3,8,128]{2,1,0:T(8,128)} %get-tuple-element.19), channel_id=1, source_target_pairs={{1,0},{2,1},{3,2},{0,3},{5,4},{6,5},{7,6},{4,7},{9,8},{10,9},{11,1... | collective-permute-start | bytes 36872 | tf_op jit(solution)/shard_map/ppermute | solution.py:658
  13.7 0.1 pad_add_fusion.place_ref
  13.8 1.5 %collective-permute-done.west_ref = f32[3,8,128]{2,1,0:T(8,128)S(1)} collective-permute-done((f32[3,8,128]{2,1,0:T(8,128)}, f32[3,8,128]{2,1,0:T(8,128)S(1)}, u32[]{:S(2)}, u32[]{:S(2)}) %collective-permute-start) | collective-permute-done | bytes 12320 | tf_op jit(solution)/shard_map/ppermute | solution.py:657
  15.3 0.0 collective-permute-done.1.east_ref
  15.4 12.6 %tendency.1 = (f32[5,3,8,8,720]{4,3,2,1,0:T(8,128)}, f32[320,512]{1,0:T(8,128)S(1)}, f32[320,512]{1,0:T(8,128)}) custom-call(f32[5,3,8,8,720]{4,3,2,1,0:T(8,128)} %state_ref.3, f32[3,8,8,720]{3,2,1,0:T(8,128)S(1)} %copy-done.3, f32[3,8,8,720]{3,2,1,0:T(8,128)S(1)} %copy-done.4, f32[3,8,128]{2,1,0:T(8,128)S(1)} %collective-permute-done.west_ref, ...), custom_call_target="tpu_custom_call" | custom-call | flops 1415577600 | bytes 9000000 | tf_op jit(solution)/shard_map/tendency/pallas_call | solution.py:395
  28.0 0.8 %copy-done.2 = f32[320,512]{1,0:T(8,128)} copy-done((f32[320,512]{1,0:T(8,128)}, f32[320,512]{1,0:T(8,128)S(1)}, u32[]{:S(2)}) %copy-start.2) | copy-done | bytes 655384
  28.8 2.0 %collective-permute-start.2 = (f32[320,512]{1,0:T(8,128)}, f32[320,512]{1,0:T(8,128)S(1)}, u32[]{:S(2)}, u32[]{:S(2)}) collective-permute-start(f32[320,512]{1,0:T(8,128)} %get-tuple-element.23), channel_id=1, source_target_pairs={{0,1},{1,0},{2,3},{3,2},{4,5},{5,4},{6,7},{7,6},{8,9},{9,8},{10,11... | collective-permute-start | bytes 1966088 | tf_op jit(solution)/shard_map/ppermute | solution.py:628
  30.8 3.5 %faces.1 = (f32[8,184,128]{2,1,0:T(8,128)}, f32[320,512]{1,0:T(8,128)}) custom-call(f32[8,200,128]{2,1,0:T(8,128)} %all-to-all-done.got_ref, s32[192]{0:T(256)} %cutoff_ref.7, f32[320,512]{1,0:T(8,128)} %copy-done.2), custom_call_target="tpu_custom_call", output_to_operand_aliasing={{1}: (2, {})} | custom-call | flops 100000 | bytes 1600000 | tf_op jit(solution)/shard_map/faces/pallas_call | solution.py:235
  34.3 0.0 copy-start
  34.3 0.0 copy-start.1
  34.4 6.1 %all-to-all-start.1 = ((f32[8,184,128]{2,1,0:T(8,128)}), f32[8,184,128]{2,1,0:T(8,128)S(1)}, u32[]{:S(2)}, u32[]{:S(2)}) async-start(f32[8,184,128]{2,1,0:T(8,128)} %get-tuple-element.24), calls=%async_computation.1 | async-start | bytes 1507328 | tf_op jit(solution)/shard_map/all_to_all | solution.py:664
  40.5 1.2 %add.27 = f32[320,512]{1,0:T(8,128)S(1)} add(f32[320,512]{1,0:T(8,128)} %get-tuple-element.22, f32[320,512]{1,0:T(8,128)S(1)} %collective-permute-done.2) | non-fusion elementwise | flops 163840 | bytes 1966080 | tf_op jit(solution)/shard_map/add | solution.py:632
  41.7 0.6 collective-permute-start.3
  42.3 15.8 %collective-permute-done.3 = f32[320,512]{1,0:T(8,128)S(1)} collective-permute-done((f32[320,512]{1,0:T(8,128)S(1)}, f32[320,512]{1,0:T(8,128)S(1)}, u32[]{:S(2)}, u32[]{:S(2)}) %collective-permute-start.3) | collective-permute-done | bytes 655392 | tf_op jit(solution)/shard_map/ppermute | solution.py:628
  58.1 0.1 add.28.mine_ref
  58.2 0.1 collective-permute-start.4
  58.3 1.8 %all-to-all-done.1 = f32[8,184,128]{2,1,0:T(8,128)S(1)} async-done(((f32[8,184,128]{2,1,0:T(8,128)}), f32[8,184,128]{2,1,0:T(8,128)S(1)}, u32[]{:S(2)}, u32[]{:S(2)}) %all-to-all-start.1) | async-done | bytes 753696 | tf_op jit(solution)/shard_map/all_to_all | solution.py:664
  60.1 1.5 %rim_spectra.1 = (f32[2,2,5,8,720]{4,3,2,1,0:T(8,128)S(1)}, f32[80,512]{1,0:T(8,128)S(1)}, f32[80,512]{1,0:T(8,128)S(1)}, f32[8,128]{1,0:T(8,128)S(1)}) custom-call(f32[1472,128]{1,0:T(8,128)S(1)} %bitcast.5, bf16[512,720]{1,0:T(8,128)(2,1)S(1)} %copy-done.1, bf16[512,720]{1,0:T(8,128)(2,1)S(1)} %copy-done, f32[4,1,512]{2,1,0:T(1,128)S(1)} %copy-done.7, ...), custom_call_target="tpu_custom_call" | custom-call | flops 353894400 | bytes 3000000 | tf_op jit(solution)/shard_map/rim_spectra/pallas_call | solution.py:529
  61.6 0.1 collective-permute-start.5
  61.7 1.4 %collective-permute-done.5 = f32[80,512]{1,0:T(8,128)S(1)} collective-permute-done((f32[80,512]{1,0:T(8,128)S(1)}, f32[80,512]{1,0:T(8,128)S(1)}, u32[]{:S(2)}, u32[]{:S(2)}) %collective-permute-start.5) | collective-permute-done | bytes 163872 | tf_op jit(solution)/shard_map/ppermute | solution.py:628
  63.1 0.6 collective-permute-start.6
  63.7 5.4 %main.1 = (f32[5,3,8,8,720]{4,3,2,1,0:T(8,128)}, f32[1,512]{1,0:T(1,128)S(1)}) custom-call(s32[2]{0:T(128)S(1)} %pad_add_fusion.place_ref, s32[3]{0:T(128)S(1)} %copy-done.10, s32[192]{0:T(256)S(1)} %copy-done.9, f32[5,3,8,8,720]{4,3,2,1,0:T(8,128)} %state_ref.3, f32[5,3,8,8,720]{4,3,2,1,0:T(8,128)} %get-tuple-element.20.base_ref, ...), custom_call_target="tpu_custom_call", output_to_operand_aliasing={{0}: (4, {})} | custom-call | flops 1415577600 | bytes 6000000 | tf_op jit(solution)/shard_map/main/pallas_call | solution.py:460
  69.1 0.3 collective-permute-done.6
  69.5 0.1 collective-permute-start.7
  69.5 1.4 %collective-permute-done.7.away_ref = f32[80,512]{1,0:T(8,128)S(1)} collective-permute-done((f32[80,512]{1,0:T(8,128)S(1)}, f32[80,512]{1,0:T(8,128)S(1)}, u32[]{:S(2)}, u32[]{:S(2)}) %collective-permute-start.7) | collective-permute-done | bytes 163872 | tf_op jit(solution)/shard_map/ppermute | solution.py:628
  70.9 2.5 %final.1 = f32[5,3,8,8,720]{4,3,2,1,0:T(8,128)} custom-call(f32[5,3,8,8,720]{4,3,2,1,0:T(8,128)} %get-tuple-element.26.main_ref, f32[2,2,5,8,720]{4,3,2,1,0:T(8,128)S(1)} %get-tuple-element.27.pair_ref, f32[1472,128]{1,0:T(8,128)S(1)} %bitcast.6, f32[80,512]{1,0:T(8,128)S(1)} %add_add_fusion.mine_ref, ...), custom_call_target="tpu_custom_call", output_to_operand_aliasing={{}: (0, {})} | custom-call | flops 353894400 | bytes 4000000 | tf_op jit(solution)/shard_map/final/pallas_call | solution.py:608
  (22 shorter events, 0.1 us)
Async XLA Ops:
  2.2 28.6 %all-to-all-start = ((f32[8,200,128]{2,1,0:T(8,128)}), f32[8,200,128]{2,1,0:T(8,128)}, u32[]{:S(2)}, u32[]{:S(2)}) async-start(f32[8,200,128]{2,1,0:T(8,128)} %bitcast.8), calls=%async_computation | async-start | bytes 1638400 | tf_op jit(solution)/shard_map/all_to_all | solution.py:654
  9.5 5.8 %copy-start.3 = (f32[3,8,8,720]{3,2,1,0:T(8,128)S(1)}, f32[3,8,8,720]{3,2,1,0:T(8,128)}, u32[]{:S(2)}) copy-start(f32[3,8,8,720]{3,2,1,0:T(8,128)} %cx_ref.1) | copy-start | bytes 1658884
  9.5 5.8 %copy-start.4 = (f32[3,8,8,720]{3,2,1,0:T(8,128)S(1)}, f32[3,8,8,720]{3,2,1,0:T(8,128)}, u32[]{:S(2)}) copy-start(f32[3,8,8,720]{3,2,1,0:T(8,128)} %wind_ref.3) | copy-start | bytes 1658884
  9.5 5.8 %copy-start.5 = (bf16[720,512]{1,0:T(8,128)(2,1)S(1)}, bf16[720,512]{1,0:T(8,128)(2,1)}, u32[]{:S(2)}) copy-start(bf16[720,512]{1,0:T(8,128)(2,1)} %constant.28.clone.low_ref) | copy-start | bytes 2211844
  9.5 5.8 %copy-start.6 = (bf16[720,512]{1,0:T(8,128)(2,1)S(1)}, bf16[720,512]{1,0:T(8,128)(2,1)}, u32[]{:S(2)}) copy-start(bf16[720,512]{1,0:T(8,128)(2,1)} %constant.27.clone.high_ref) | copy-start | bytes 2211844
  9.5 5.8 %copy-start.7 = (f32[4,1,512]{2,1,0:T(1,128)S(1)}, f32[4,1,512]{2,1,0:T(1,128)}, u32[]{:S(2)}) copy-start(f32[4,1,512]{2,1,0:T(1,128)} %constant.31.clone.turn_ref) | copy-start | bytes 24580
  9.5 5.8 %copy-start.8 = (s32[192]{0:T(256)S(1)}, s32[192]{0:T(256)}, u32[]{:S(2)}) copy-start(s32[192]{0:T(256)} %cutoff_ref.7) | copy-start | bytes 2308
  9.6 5.8 %copy-start.10 = (s32[3]{0:T(128)S(1)}, s32[3]{0:T(128)}, u32[]{:S(2)}) copy-start(s32[3]{0:T(128)} %block_ref.7) | copy-start | bytes 40
  11.9 3.3 %collective-permute-start = (f32[3,8,128]{2,1,0:T(8,128)}, f32[3,8,128]{2,1,0:T(8,128)S(1)}, u32[]{:S(2)}, u32[]{:S(2)}) collective-permute-start(f32[3,8,128]{2,1,0:T(8,128)} %get-tuple-element.18), channel_id=1, source_target_pairs={{0,1},{1,2},{2,3},{3,0},{4,5},{5,6},{6,7},{7,4},{8,9},{9,10},{10,1... | collective-permute-start | bytes 36872 | tf_op jit(solution)/shard_map/ppermute | solution.py:657
  12.0 3.4 %collective-permute-start.1 = (f32[3,8,128]{2,1,0:T(8,128)}, f32[3,8,128]{2,1,0:T(8,128)S(1)}, u32[]{:S(2)}, u32[]{:S(2)}) collective-permute-start(f32[3,8,128]{2,1,0:T(8,128)} %get-tuple-element.19), channel_id=1, source_target_pairs={{1,0},{2,1},{3,2},{0,3},{5,4},{6,5},{7,6},{4,7},{9,8},{10,9},{11,1... | collective-permute-start | bytes 36872 | tf_op jit(solution)/shard_map/ppermute | solution.py:658
  28.0 0.9 %copy-start.2 = (f32[320,512]{1,0:T(8,128)}, f32[320,512]{1,0:T(8,128)S(1)}, u32[]{:S(2)}) copy-start(f32[320,512]{1,0:T(8,128)S(1)} %get-tuple-element.21.later_in_ref) | copy-start | bytes 1966084
  28.8 11.6 %collective-permute-start.2 = (f32[320,512]{1,0:T(8,128)}, f32[320,512]{1,0:T(8,128)S(1)}, u32[]{:S(2)}, u32[]{:S(2)}) collective-permute-start(f32[320,512]{1,0:T(8,128)} %get-tuple-element.23), channel_id=1, source_target_pairs={{0,1},{1,0},{2,3},{3,2},{4,5},{5,4},{6,7},{7,6},{8,9},{9,8},{10,11... | collective-permute-start | bytes 1966088 | tf_op jit(solution)/shard_map/ppermute | solution.py:628
  34.3 25.8 %copy-start = (bf16[512,720]{1,0:T(8,128)(2,1)S(1)}, bf16[512,720]{1,0:T(8,128)(2,1)}, u32[]{:S(2)}) copy-start(bf16[512,720]{1,0:T(8,128)(2,1)} %constant.30.clone.low_ref) | copy-start | bytes 2211844
  34.3 25.8 %copy-start.1 = (bf16[512,720]{1,0:T(8,128)(2,1)S(1)}, bf16[512,720]{1,0:T(8,128)(2,1)}, u32[]{:S(2)}) copy-start(bf16[512,720]{1,0:T(8,128)(2,1)} %constant.29.clone.high_ref) | copy-start | bytes 2211844
  34.4 25.8 %all-to-all-start.1 = ((f32[8,184,128]{2,1,0:T(8,128)}), f32[8,184,128]{2,1,0:T(8,128)S(1)}, u32[]{:S(2)}, u32[]{:S(2)}) async-start(f32[8,184,128]{2,1,0:T(8,128)} %get-tuple-element.24), calls=%async_computation.1 | async-start | bytes 1507328 | tf_op jit(solution)/shard_map/all_to_all | solution.py:664
  40.5 23.2 %copy-start.9 = (s32[192]{0:T(256)S(1)}, s32[192]{0:T(256)}, u32[]{:S(2)}) copy-start(s32[192]{0:T(256)} %cutoff_ref.7) | copy-start | bytes 2308
  41.7 16.4 %collective-permute-start.3 = (f32[320,512]{1,0:T(8,128)S(1)}, f32[320,512]{1,0:T(8,128)S(1)}, u32[]{:S(2)}, u32[]{:S(2)}) collective-permute-start(f32[320,512]{1,0:T(8,128)S(1)} %add.27), channel_id=1, source_target_pairs={{0,2},{1,3},{2,0},{3,1},{4,6},{5,7},{6,4},{7,5},{8,10},{9,11},{10,... | collective-permute-start | bytes 1966088 | tf_op jit(solution)/shard_map/ppermute | solution.py:628
  58.2 5.5 %collective-permute-start.4 = (f32[320,512]{1,0:T(8,128)S(1)}, f32[320,512]{1,0:T(8,128)}, u32[]{:S(2)}, u32[]{:S(2)}) collective-permute-start(f32[320,512]{1,0:T(8,128)S(1)} %add.28.mine_ref), channel_id=1, source_target_pairs={{0,1},{1,0},{2,3},{3,2},{4,5},{5,4},{6,7},{7,6},{8,9},{9,8},{10,11... | collective-permute-start | bytes 1966088 | tf_op jit(solution)/shard_map/ppermute | solution.py:628
  61.6 1.5 %collective-permute-start.5 = (f32[80,512]{1,0:T(8,128)S(1)}, f32[80,512]{1,0:T(8,128)S(1)}, u32[]{:S(2)}, u32[]{:S(2)}) collective-permute-start(f32[80,512]{1,0:T(8,128)S(1)} %get-tuple-element.29), channel_id=1, source_target_pairs={{0,1},{1,0},{2,3},{3,2},{4,5},{5,4},{6,7},{7,6},{8,9},{9,8},{10,11... | collective-permute-start | bytes 491528 | tf_op jit(solution)/shard_map/ppermute | solution.py:628
  63.1 6.3 %collective-permute-start.6 = (f32[80,512]{1,0:T(8,128)S(1)}, f32[80,512]{1,0:T(8,128)S(1)}, u32[]{:S(2)}, u32[]{:S(2)}) collective-permute-start(f32[80,512]{1,0:T(8,128)S(1)} %add.29), channel_id=1, source_target_pairs={{0,2},{1,3},{2,0},{3,1},{4,6},{5,7},{6,4},{7,5},{8,10},{9,11},{10,... | collective-permute-start | bytes 491528 | tf_op jit(solution)/shard_map/ppermute | solution.py:628
  69.5 1.5 %collective-permute-start.7 = (f32[80,512]{1,0:T(8,128)S(1)}, f32[80,512]{1,0:T(8,128)S(1)}, u32[]{:S(2)}, u32[]{:S(2)}) collective-permute-start(f32[80,512]{1,0:T(8,128)S(1)} %add_add_fusion.mine_ref), channel_id=1, source_target_pairs={{0,1},{1,0},{2,3},{3,2},{4,5},{5,4},{6,7},{7,6},{8,9},{9,8},{10,11... | collective-permute-start | bytes 491528 | tf_op jit(solution)/shard_map/ppermute | solution.py:628
where the time goes:
time: 73.8 us; the launch traced here: 73.4 us
  Pallas kernels  30 us (41%)
  waiting for transfers between devices  22.3 us (30%)
  starting transfers between devices  18.6 us (25%)
  other arithmetic  1.4 us (2%)
  local copies, waits for them, and re-layouts  0.91 us (1%)
    ppermute x6, waiting for transfers between devices, swap(): return lax.ppermute(array, 'lon', [(i, i ^ bit) for i in range(size)])  18.9 us
    pallas_call x1, Pallas kernels, local_tendency(): pl.pallas_call(tendency_kernel, in_specs=vmem(8) + smem(3), out_specs=[pl...  12.6 us
    all_to_all x1, starting transfers between devices, shards(): got = lax.all_to_all(sent, 'lat', 0, 0, tiled=True)  7.28 us
    all_to_all x1, starting transfers between devices, shards(): back = lax.all_to_all(back, 'lat', 0, 0, tiled=True)  6.12 us
    pallas_call x1, Pallas kernels, main_part(): pl.pallas_call(main_kernel, grid_spec=pltpu.PrefetchScalarGridSpec(num_sc...  5.36 us
    pallas_call x1, Pallas kernels, faces_of_pieces(): pl.pallas_call(face_kernel, in_specs=vmem(1) + smem(1) + [pl.BlockSpec(me...  3.49 us
    ppermute x6, starting transfers between devices, swap(): return lax.ppermute(array, 'lon', [(i, i ^ bit) for i in range(size)])  3.4 us
    pallas_call x1, Pallas kernels, final_part(): pl.pallas_call(functools.partial(final_kernel, back.ndim == 2), grid=(2,)...  2.5 us
  transfers between devices with their start and end apart: 10, of which 6 were waited for; matrix products, arithmetic and copies ran while one was open for 2% of the time, Pallas kernels for 35%

commit v1 on v0

--- a/solution.py
+++ b/solution.py
@@ -134,67 +134,129 @@
     return part
 
 
-def pack_kernel(width, first_ref, last_ref, wind_ref, block_ref, out_ref):
-    fields, slots = first_ref.shape[:2]
+def pack_kernel(
+    state_ref,
+    wind_ref,
+    block_ref,
+    out_ref,
+    first_ref,
+    last_ref,
+    half_ref,
+    sent_ref,
+    in_sem,
+    out_sem,
+):
+    fields, slots, rows, levels, width = state_ref.shape
     tiles = -(-width // LANES)
 
+    def incoming(j):
+        return (
+            pltpu.make_async_copy(state_ref.at[:, j, 0], first_ref.at[j], in_sem.at[j, 0]),
+            pltpu.make_async_copy(state_ref.at[:, j, rows - 1], last_ref.at[j], in_sem.at[j, 1]),
+            pltpu.make_async_copy(wind_ref.at[j, rows - 1], half_ref.at[j], in_sem.at[j, 2]),
+        )
+
+    def outgoing(j, p):
+        part = pl.ds(p * PIECE + 64 * j, 64 if j < slots else PIECE - 64 * slots)
+        return pltpu.make_async_copy(sent_ref.at[part], out_ref.at[part], out_sem.at[j, p])
+
     def put(row, tile):
-        out_ref[pl.ds(row, 8, stride=PIECE), :] = tile
+        sent_ref[pl.ds(row, 8, stride=PIECE), :] = tile
 
     for j in range(slots):
-        half = wind_ref[j, 0] * 0.5
+        for copy in incoming(j):
+            copy.start()
+    for j in range(slots):
+        for copy in incoming(j):
+            copy.wait()
+        half = half_ref[j] * 0.5
         for t in range(tiles):
             row = {0: 192 + 2 * j, 1: 193 + 2 * j, 2: 64 * j + 62, 3: 64 * j + 63}.get(
                 t, 64 * j + 26 + t
             )
             put(row, tile_of(half, t, width))
         for f in range(fields):
-            north = last_ref[f, j, 0] * half
-            south = first_ref[f, j, 0]
+            north = last_ref[j, f] * half
+            south = first_ref[j, f]
             for t in range(tiles):
                 put(64 * j + f * tiles + t, tile_of(north, t, width))
                 put(64 * j + 32 + f * tiles + t, tile_of(south, t, width))
+        for p in range(levels):
+            outgoing(j, p).start()
     lane = lax.broadcasted_iota(jnp.int32, (8, LANES), 1)
     table = jnp.zeros((8, LANES), F32)
     for j in range(slots):
         table = jnp.where(lane == j, block_ref[j].astype(F32), table)
     put(198, table)
     put(199, table)
+    for p in range(levels):
+        outgoing(slots, p).start()
+    for j in range(slots + 1):
+        for p in range(levels):
+            outgoing(j, p).wait()
+
+
+def anywhere(count):
+    return [pl.BlockSpec(memory_space=pl.ANY)] * count
 
 
 def pack(state, courant_y, block):
     fields, slots, rows, levels, width = state.shape
     return pl.pallas_call(
-        functools.partial(pack_kernel, width),
-        grid=(1,),
-        in_specs=[
-            pl.BlockSpec((fields, slots, 1, levels, width), lambda i: (0, 0, 0, 0, 0)),
-            pl.BlockSpec((fields, slots, 1, levels, width), lambda i: (0, 0, rows - 1, 0, 0)),
-            pl.BlockSpec((slots, 1, levels, width), lambda i: (0, rows - 1, 0, 0)),
-            pl.BlockSpec(memory_space=pltpu.SMEM),
+        pack_kernel,
+        in_specs=anywhere(2) + smem(1),
+        out_specs=anywhere(1)[0],
+        out_shape=jax.ShapeDtypeStruct((levels * PIECE, LANES), F32),
+        scratch_shapes=[
+            pltpu.VMEM((slots, fields, levels, width), F32),
+            pltpu.VMEM((slots, fields, levels, width), F32),
+            pltpu.VMEM((slots, levels, width), F32),
+            pltpu.VMEM((levels * PIECE, LANES), F32),
+            pltpu.SemaphoreType.DMA((slots, 3)),
+            pltpu.SemaphoreType.DMA((slots + 1, levels)),
         ],
-        out_specs=pl.BlockSpec((levels * PIECE, LANES), lambda i: (0, 0)),
-        out_shape=jax.ShapeDtypeStruct((levels * PIECE, LANES), F32),
         cost_estimate=pl.CostEstimate(flops=10**5, bytes_accessed=1700000, transcendentals=0),
         name="pack",
-    )(state, state, courant_y, block)
+    )(state, courant_y, block)
 
 
 def face_kernel(
-    got_ref, cutoff_ref, later_in_ref, out_ref, later_ref, face_ref, table_ref, slot_ref, sem
+    from_ref,
+    cutoff_ref,
+    later_in_ref,
+    to_ref,
+    later_ref,
+    got_ref,
+    out_ref,
+    face_ref,
+    table_ref,
+    slot_ref,
+    sem,
+    in_sem,
+    out_sem,
 ):
     del later_in_ref, later_ref
-    parts = got_ref.shape[0]
+    parts = from_ref.shape[0]
     slots = face_ref.shape[0] // parts
     count = parts * slots
-    copy = pltpu.make_async_copy(got_ref.at[:, 192:200, :], table_ref, sem)
+    copy = pltpu.make_async_copy(from_ref.at[:, 192:200, :], table_ref, sem)
+    incoming = [
+        pltpu.make_async_copy(from_ref.at[d], got_ref.at[d], in_sem.at[d]) for d in range(parts)
+    ]
+    outgoing = [
+        pltpu.make_async_copy(out_ref.at[d], to_ref.at[d], out_sem.at[d]) for d in range(parts)
+    ]
     copy.start()
+    for part in incoming:
+        part.start()
     copy.wait()
     blocks = [table_ref[s // slots, 6, s % slots].astype(jnp.int32) for s in range(count)]
     slot_ref[0] = -1
     slot_ref[count + 1] = -1
     for s in range(count):
         slot_ref[blocks[s] + 1] = s
+    for part in incoming:
+        part.wait()
     for s in range(count):
         src, j = divmod(s, slots)
         south = slot_ref[blocks[s] + 2]
@@ -228,24 +290,31 @@
             )
             out_ref[d, row + 30 : row + 60] = face_ref[slots * d + slot, :30]
         out_ref[d, 180:184] = jnp.zeros((4, LANES), F32)
+        outgoing[d].start()
+    for part in outgoing:
+        part.wait()
 
 
 def faces_of_pieces(got, slots, cutoff, later):
     parts = got.shape[0]
     return pl.pallas_call(
         face_kernel,
-        in_specs=vmem(1) + smem(1) + [pl.BlockSpec(memory_space=pl.ANY)],
-        out_specs=vmem(1) + [pl.BlockSpec(memory_space=pl.ANY)],
+        in_specs=anywhere(1) + smem(1) + anywhere(1),
+        out_specs=anywhere(2),
         out_shape=[
             jax.ShapeDtypeStruct((parts, BACK, LANES), F32),
             jax.ShapeDtypeStruct(later.shape, F32),
         ],
         input_output_aliases={2: 1},
         scratch_shapes=[
+            pltpu.VMEM(got.shape, F32),
+            pltpu.VMEM((parts, BACK, LANES), F32),
             pltpu.VMEM((parts * slots, 32, LANES), F32),
             pltpu.SMEM((parts, 8, LANES), F32),
             pltpu.SMEM((parts * slots + 2,), jnp.int32),
             pltpu.SemaphoreType.DMA(()),
+            pltpu.SemaphoreType.DMA((parts,)),
+            pltpu.SemaphoreType.DMA((parts,)),
         ],
         cost_estimate=pl.CostEstimate(flops=10**5, bytes_accessed=1600000, transcendentals=0),
         name="faces",

time: 73.8 us -> 75.3 us (1.020)
  local copies, waits for them, and re-layouts: 0.91 us -> 1.82 us
    unnamed x22 -> x24, local copies, waits for them, and re-layouts: 0.91 us -> 1.82 us
  transfers between devices with their start and end apart: 10 -> 10, of which waited for: 6 -> 6; matrix products, arithmetic and copies ran while one was open for 2% -> 2% of each run, Pallas kernels for 35% -> 34%
where the time goes in v1:
time: 75.3 us; the launch traced here: 74.9 us
  Pallas kernels  30.7 us (41%)
  waiting for transfers between devices  22.3 us (30%)
  starting transfers between devices  18.5 us (25%)
  local copies, waits for them, and re-layouts  1.82 us (2%)
  other arithmetic  1.4 us (2%)
    ppermute x6, waiting for transfers between devices, swap(): return lax.ppermute(array, 'lon', [(i, i ^ bit) for i in range(size)])  19 us
    pallas_call x1, Pallas kernels, local_tendency(): pl.pallas_call(tendency_kernel, in_specs=vmem(8) + smem(3), out_specs=[pl...  12.6 us
    all_to_all x1, starting transfers between devices, shards(): got = lax.all_to_all(sent, 'lat', 0, 0, tiled=True)  7.29 us
    all_to_all x1, starting transfers between devices, shards(): back = lax.all_to_all(back, 'lat', 0, 0, tiled=True)  6.12 us
    pallas_call x1, Pallas kernels, main_part(): pl.pallas_call(main_kernel, grid_spec=pltpu.PrefetchScalarGridSpec(num_sc...  5.36 us
    pallas_call x1, Pallas kernels, faces_of_pieces(): pl.pallas_call(face_kernel, in_specs=anywhere(1) + smem(1) + anywhere(1),...  3.3 us
    ppermute x6, starting transfers between devices, swap(): return lax.ppermute(array, 'lon', [(i, i ^ bit) for i in range(size)])  3.29 us
    pallas_call x1, Pallas kernels, pack(): pl.pallas_call(pack_kernel, in_specs=anywhere(2) + smem(1), out_specs=any...  3.04 us
  transfers between devices with their start and end apart: 10, of which 6 were waited for; matrix products, arithmetic and copies ran while one was open for 2% of the time, Pallas kernels for 34%

profile of v1, /device:TPU:0, one launch (start us, length us, event | category | flops | bytes accessed | tf_op | source)
XLA Modules:
  0.0 74.9 jit_solution(17054275971968399353)
XLA Ops:
  0.0 3.0 %pack.1 = f32[1600,128]{1,0:T(8,128)} custom-call(f32[5,3,8,8,720]{4,3,2,1,0:T(8,128)} %state_ref.5, f32[3,8,8,720]{3,2,1,0:T(8,128)} %wind_ref.3, s32[3]{0:T(128)} %block_ref.7), custom_call_target="tpu_custom_call" | custom-call | flops 100000 | bytes 1700000 | tf_op jit(solution)/shard_map/pack/pallas_call | solution.py:205
  3.0 7.3 %all-to-all-start = ((f32[8,200,128]{2,1,0:T(8,128)}), f32[8,200,128]{2,1,0:T(8,128)S(1)}, u32[]{:S(2)}, u32[]{:S(2)}) async-start(f32[8,200,128]{2,1,0:T(8,128)} %bitcast.8), calls=%async_computation | async-start | bytes 1638400 | tf_op jit(solution)/shard_map/all_to_all | solution.py:723
  10.4 0.0 copy-start.5
  10.4 0.0 copy-start.6
  10.4 0.0 copy-start.7
  10.4 2.4 %edges.1 = (f32[3,8,128]{2,1,0:T(8,128)}, f32[3,8,128]{2,1,0:T(8,128)}) custom-call(f32[5,3,8,8,720]{4,3,2,1,0:T(8,128)} %state_ref.5, f32[5,3,8,8,720]{4,3,2,1,0:T(8,128)} %state_ref.5, f32[3,8,8,720]{3,2,1,0:T(8,128)} %cx_ref.1), custom_call_target="tpu_custom_call" | custom-call | flops 100000 | bytes 1200000 | tf_op jit(solution)/shard_map/edges/pallas_call | solution.py:111
  12.8 1.7 %collective-permute-start.1 = (f32[3,8,128]{2,1,0:T(8,128)}, f32[3,8,128]{2,1,0:T(8,128)S(1)}, u32[]{:S(2)}, u32[]{:S(2)}) collective-permute-start(f32[3,8,128]{2,1,0:T(8,128)} %get-tuple-element.19), channel_id=1, source_target_pairs={{1,0},{2,1},{3,2},{0,3},{5,4},{6,5},{7,6},{4,7},{9,8},{10,9},{11,1... | collective-permute-start | bytes 36872 | tf_op jit(solution)/shard_map/ppermute | solution.py:727
  14.6 0.1 pad_add_fusion.place_ref
  14.6 1.5 %collective-permute-done.west_ref = f32[3,8,128]{2,1,0:T(8,128)S(1)} collective-permute-done((f32[3,8,128]{2,1,0:T(8,128)}, f32[3,8,128]{2,1,0:T(8,128)S(1)}, u32[]{:S(2)}, u32[]{:S(2)}) %collective-permute-start) | collective-permute-done | bytes 12320 | tf_op jit(solution)/shard_map/ppermute | solution.py:726
  16.1 0.0 collective-permute-done.1.east_ref
  16.2 12.6 %tendency.1 = (f32[5,3,8,8,720]{4,3,2,1,0:T(8,128)}, f32[320,512]{1,0:T(8,128)S(1)}, f32[320,512]{1,0:T(8,128)}) custom-call(f32[5,3,8,8,720]{4,3,2,1,0:T(8,128)} %state_ref.5, f32[3,8,8,720]{3,2,1,0:T(8,128)S(1)} %copy-done.3, f32[3,8,8,720]{3,2,1,0:T(8,128)S(1)} %copy-done.4, f32[3,8,128]{2,1,0:T(8,128)S(1)} %collective-permute-done.west_ref, ...), custom_call_target="tpu_custom_call" | custom-call | flops 1415577600 | bytes 9000000 | tf_op jit(solution)/shard_map/tendency/pallas_call | solution.py:464
  28.9 0.8 %copy-done.2 = f32[320,512]{1,0:T(8,128)} copy-done((f32[320,512]{1,0:T(8,128)}, f32[320,512]{1,0:T(8,128)S(1)}, u32[]{:S(2)}) %copy-start.2) | copy-done | bytes 655384
  29.7 1.9 %collective-permute-start.2 = (f32[320,512]{1,0:T(8,128)}, f32[320,512]{1,0:T(8,128)S(1)}, u32[]{:S(2)}, u32[]{:S(2)}) collective-permute-start(f32[320,512]{1,0:T(8,128)} %get-tuple-element.23), channel_id=1, source_target_pairs={{0,1},{1,0},{2,3},{3,2},{4,5},{5,4},{6,7},{7,6},{8,9},{9,8},{10,11... | collective-permute-start | bytes 1966088 | tf_op jit(solution)/shard_map/ppermute | solution.py:697
  31.6 0.9 %copy-done.11 = f32[8,200,128]{2,1,0:T(8,128)} copy-done((f32[8,200,128]{2,1,0:T(8,128)}, f32[8,200,128]{2,1,0:T(8,128)S(1)}, u32[]{:S(2)}) %copy-start.11) | copy-done | bytes 819224
  32.5 3.3 %faces.1 = (f32[8,184,128]{2,1,0:T(8,128)}, f32[320,512]{1,0:T(8,128)}) custom-call(f32[8,200,128]{2,1,0:T(8,128)} %copy-done.11, s32[192]{0:T(256)} %cutoff_ref.7, f32[320,512]{1,0:T(8,128)} %copy-done.2), custom_call_target="tpu_custom_call", output_to_operand_aliasing={{1}: (2, {})} | custom-call | flops 100000 | bytes 1600000 | tf_op jit(solution)/shard_map/faces/pallas_call | solution.py:300
  35.8 0.0 copy-start
  35.8 6.1 %all-to-all-start.1 = ((f32[8,184,128]{2,1,0:T(8,128)}), f32[8,184,128]{2,1,0:T(8,128)S(1)}, u32[]{:S(2)}, u32[]{:S(2)}) async-start(f32[8,184,128]{2,1,0:T(8,128)} %get-tuple-element.24), calls=%async_computation.1 | async-start | bytes 1507328 | tf_op jit(solution)/shard_map/all_to_all | solution.py:733
  42.0 1.2 %add.27 = f32[320,512]{1,0:T(8,128)S(1)} add(f32[320,512]{1,0:T(8,128)} %get-tuple-element.22, f32[320,512]{1,0:T(8,128)S(1)} %collective-permute-done.2) | non-fusion elementwise | flops 163840 | bytes 1966080 | tf_op jit(solution)/shard_map/add | solution.py:701
  43.1 0.6 collective-permute-start.3
  43.7 15.8 %collective-permute-done.3 = f32[320,512]{1,0:T(8,128)S(1)} collective-permute-done((f32[320,512]{1,0:T(8,128)S(1)}, f32[320,512]{1,0:T(8,128)S(1)}, u32[]{:S(2)}, u32[]{:S(2)}) %collective-permute-start.3) | collective-permute-done | bytes 655392 | tf_op jit(solution)/shard_map/ppermute | solution.py:697
  59.6 0.1 add.28.mine_ref
  59.7 0.1 collective-permute-start.4
  59.8 1.8 %all-to-all-done.1 = f32[8,184,128]{2,1,0:T(8,128)S(1)} async-done(((f32[8,184,128]{2,1,0:T(8,128)}), f32[8,184,128]{2,1,0:T(8,128)S(1)}, u32[]{:S(2)}, u32[]{:S(2)}) %all-to-all-start.1) | async-done | bytes 753696 | tf_op jit(solution)/shard_map/all_to_all | solution.py:733
  61.6 1.5 %rim_spectra.1 = (f32[2,2,5,8,720]{4,3,2,1,0:T(8,128)S(1)}, f32[80,512]{1,0:T(8,128)S(1)}, f32[80,512]{1,0:T(8,128)S(1)}, f32[8,128]{1,0:T(8,128)S(1)}) custom-call(f32[1472,128]{1,0:T(8,128)S(1)} %bitcast.5, bf16[512,720]{1,0:T(8,128)(2,1)S(1)} %copy-done.1, bf16[512,720]{1,0:T(8,128)(2,1)S(1)} %copy-done, f32[4,1,512]{2,1,0:T(1,128)S(1)} %copy-done.7, ...), custom_call_target="tpu_custom_call" | custom-call | flops 353894400 | bytes 3000000 | tf_op jit(solution)/shard_map/rim_spectra/pallas_call | solution.py:598
  63.1 0.1 collective-permute-start.5
  63.2 1.4 %collective-permute-done.5 = f32[80,512]{1,0:T(8,128)S(1)} collective-permute-done((f32[80,512]{1,0:T(8,128)S(1)}, f32[80,512]{1,0:T(8,128)S(1)}, u32[]{:S(2)}, u32[]{:S(2)}) %collective-permute-start.5) | collective-permute-done | bytes 163872 | tf_op jit(solution)/shard_map/ppermute | solution.py:697
  64.6 0.6 collective-permute-start.6
  65.2 5.4 %main.1 = (f32[5,3,8,8,720]{4,3,2,1,0:T(8,128)}, f32[1,512]{1,0:T(1,128)S(1)}) custom-call(s32[2]{0:T(128)S(1)} %pad_add_fusion.place_ref, s32[3]{0:T(128)S(1)} %copy-done.10, s32[192]{0:T(256)S(1)} %copy-done.9, f32[5,3,8,8,720]{4,3,2,1,0:T(8,128)} %state_ref.5, f32[5,3,8,8,720]{4,3,2,1,0:T(8,128)} %get-tuple-element.20.base_ref, ...), custom_call_target="tpu_custom_call", output_to_operand_aliasing={{0}: (4, {})} | custom-call | flops 1415577600 | bytes 6000000 | tf_op jit(solution)/shard_map/main/pallas_call | solution.py:529
  70.5 0.4 collective-permute-done.6
  70.9 0.1 collective-permute-start.7
  71.0 1.4 %collective-permute-done.7.away_ref = f32[80,512]{1,0:T(8,128)S(1)} collective-permute-done((f32[80,512]{1,0:T(8,128)S(1)}, f32[80,512]{1,0:T(8,128)S(1)}, u32[]{:S(2)}, u32[]{:S(2)}) %collective-permute-start.7) | collective-permute-done | bytes 163872 | tf_op jit(solution)/shard_map/ppermute | solution.py:697
  72.4 2.5 %final.1 = f32[5,3,8,8,720]{4,3,2,1,0:T(8,128)} custom-call(f32[5,3,8,8,720]{4,3,2,1,0:T(8,128)} %get-tuple-element.26.main_ref, f32[2,2,5,8,720]{4,3,2,1,0:T(8,128)S(1)} %get-tuple-element.27.pair_ref, f32[1472,128]{1,0:T(8,128)S(1)} %bitcast.6, f32[80,512]{1,0:T(8,128)S(1)} %add_add_fusion.mine_ref, ...), custom_call_target="tpu_custom_call", output_to_operand_aliasing={{}: (0, {})} | custom-call | flops 353894400 | bytes 4000000 | tf_op jit(solution)/shard_map/final/pallas_call | solution.py:677
  (24 shorter events, 0.1 us)
Async XLA Ops:
  3.0 28.5 %all-to-all-start = ((f32[8,200,128]{2,1,0:T(8,128)}), f32[8,200,128]{2,1,0:T(8,128)S(1)}, u32[]{:S(2)}, u32[]{:S(2)}) async-start(f32[8,200,128]{2,1,0:T(8,128)} %bitcast.8), calls=%async_computation | async-start | bytes 1638400 | tf_op jit(solution)/shard_map/all_to_all | solution.py:723
  10.3 5.8 %copy-start.3 = (f32[3,8,8,720]{3,2,1,0:T(8,128)S(1)}, f32[3,8,8,720]{3,2,1,0:T(8,128)}, u32[]{:S(2)}) copy-start(f32[3,8,8,720]{3,2,1,0:T(8,128)} %cx_ref.1) | copy-start | bytes 1658884
  10.3 5.8 %copy-start.4 = (f32[3,8,8,720]{3,2,1,0:T(8,128)S(1)}, f32[3,8,8,720]{3,2,1,0:T(8,128)}, u32[]{:S(2)}) copy-start(f32[3,8,8,720]{3,2,1,0:T(8,128)} %wind_ref.3) | copy-start | bytes 1658884
  10.4 5.8 %copy-start.5 = (bf16[720,512]{1,0:T(8,128)(2,1)S(1)}, bf16[720,512]{1,0:T(8,128)(2,1)}, u32[]{:S(2)}) copy-start(bf16[720,512]{1,0:T(8,128)(2,1)} %constant.28.clone.low_ref) | copy-start | bytes 2211844
  10.4 5.8 %copy-start.6 = (bf16[720,512]{1,0:T(8,128)(2,1)S(1)}, bf16[720,512]{1,0:T(8,128)(2,1)}, u32[]{:S(2)}) copy-start(bf16[720,512]{1,0:T(8,128)(2,1)} %constant.27.clone.high_ref) | copy-start | bytes 2211844
  10.4 5.8 %copy-start.7 = (f32[4,1,512]{2,1,0:T(1,128)S(1)}, f32[4,1,512]{2,1,0:T(1,128)}, u32[]{:S(2)}) copy-start(f32[4,1,512]{2,1,0:T(1,128)} %constant.31.clone.turn_ref) | copy-start | bytes 24580
  10.4 5.8 %copy-start.8 = (s32[192]{0:T(256)S(1)}, s32[192]{0:T(256)}, u32[]{:S(2)}) copy-start(s32[192]{0:T(256)} %cutoff_ref.7) | copy-start | bytes 2308
  10.4 5.8 %copy-start.10 = (s32[3]{0:T(128)S(1)}, s32[3]{0:T(128)}, u32[]{:S(2)}) copy-start(s32[3]{0:T(128)} %block_ref.7) | copy-start | bytes 40
  12.8 3.3 %collective-permute-start = (f32[3,8,128]{2,1,0:T(8,128)}, f32[3,8,128]{2,1,0:T(8,128)S(1)}, u32[]{:S(2)}, u32[]{:S(2)}) collective-permute-start(f32[3,8,128]{2,1,0:T(8,128)} %get-tuple-element.18), channel_id=1, source_target_pairs={{0,1},{1,2},{2,3},{3,0},{4,5},{5,6},{6,7},{7,4},{8,9},{9,10},{10,1... | collective-permute-start | bytes 36872 | tf_op jit(solution)/shard_map/ppermute | solution.py:726
  12.8 3.4 %collective-permute-start.1 = (f32[3,8,128]{2,1,0:T(8,128)}, f32[3,8,128]{2,1,0:T(8,128)S(1)}, u32[]{:S(2)}, u32[]{:S(2)}) collective-permute-start(f32[3,8,128]{2,1,0:T(8,128)} %get-tuple-element.19), channel_id=1, source_target_pairs={{1,0},{2,1},{3,2},{0,3},{5,4},{6,5},{7,6},{4,7},{9,8},{10,9},{11,1... | collective-permute-start | bytes 36872 | tf_op jit(solution)/shard_map/ppermute | solution.py:727
  28.8 0.9 %copy-start.2 = (f32[320,512]{1,0:T(8,128)}, f32[320,512]{1,0:T(8,128)S(1)}, u32[]{:S(2)}) copy-start(f32[320,512]{1,0:T(8,128)S(1)} %get-tuple-element.21.later_in_ref) | copy-start | bytes 1966084
  29.7 12.3 %collective-permute-start.2 = (f32[320,512]{1,0:T(8,128)}, f32[320,512]{1,0:T(8,128)S(1)}, u32[]{:S(2)}, u32[]{:S(2)}) collective-permute-start(f32[320,512]{1,0:T(8,128)} %get-tuple-element.23), channel_id=1, source_target_pairs={{0,1},{1,0},{2,3},{3,2},{4,5},{5,4},{6,7},{7,6},{8,9},{9,8},{10,11... | collective-permute-start | bytes 1966088 | tf_op jit(solution)/shard_map/ppermute | solution.py:697
  31.6 0.9 %copy-start.11 = (f32[8,200,128]{2,1,0:T(8,128)}, f32[8,200,128]{2,1,0:T(8,128)S(1)}, u32[]{:S(2)}) copy-start(f32[8,200,128]{2,1,0:T(8,128)S(1)} %all-to-all-done.from_ref) | copy-start | bytes 2457604
  35.8 25.8 %copy-start = (bf16[512,720]{1,0:T(8,128)(2,1)S(1)}, bf16[512,720]{1,0:T(8,128)(2,1)}, u32[]{:S(2)}) copy-start(bf16[512,720]{1,0:T(8,128)(2,1)} %constant.30.clone.low_ref) | copy-start | bytes 2211844
  35.8 25.8 %copy-start.1 = (bf16[512,720]{1,0:T(8,128)(2,1)S(1)}, bf16[512,720]{1,0:T(8,128)(2,1)}, u32[]{:S(2)}) copy-start(bf16[512,720]{1,0:T(8,128)(2,1)} %constant.29.clone.high_ref) | copy-start | bytes 2211844
  35.8 25.8 %all-to-all-start.1 = ((f32[8,184,128]{2,1,0:T(8,128)}), f32[8,184,128]{2,1,0:T(8,128)S(1)}, u32[]{:S(2)}, u32[]{:S(2)}) async-start(f32[8,184,128]{2,1,0:T(8,128)} %get-tuple-element.24), calls=%async_computation.1 | async-start | bytes 1507328 | tf_op jit(solution)/shard_map/all_to_all | solution.py:733
  42.0 23.2 %copy-start.9 = (s32[192]{0:T(256)S(1)}, s32[192]{0:T(256)}, u32[]{:S(2)}) copy-start(s32[192]{0:T(256)} %cutoff_ref.7) | copy-start | bytes 2308
  43.1 16.4 %collective-permute-start.3 = (f32[320,512]{1,0:T(8,128)S(1)}, f32[320,512]{1,0:T(8,128)S(1)}, u32[]{:S(2)}, u32[]{:S(2)}) collective-permute-start(f32[320,512]{1,0:T(8,128)S(1)} %add.27), channel_id=1, source_target_pairs={{0,2},{1,3},{2,0},{3,1},{4,6},{5,7},{6,4},{7,5},{8,10},{9,11},{10,... | collective-permute-start | bytes 1966088 | tf_op jit(solution)/shard_map/ppermute | solution.py:697
  59.7 5.5 %collective-permute-start.4 = (f32[320,512]{1,0:T(8,128)S(1)}, f32[320,512]{1,0:T(8,128)}, u32[]{:S(2)}, u32[]{:S(2)}) collective-permute-start(f32[320,512]{1,0:T(8,128)S(1)} %add.28.mine_ref), channel_id=1, source_target_pairs={{0,1},{1,0},{2,3},{3,2},{4,5},{5,4},{6,7},{7,6},{8,9},{9,8},{10,11... | collective-permute-start | bytes 1966088 | tf_op jit(solution)/shard_map/ppermute | solution.py:697
  63.1 1.5 %collective-permute-start.5 = (f32[80,512]{1,0:T(8,128)S(1)}, f32[80,512]{1,0:T(8,128)S(1)}, u32[]{:S(2)}, u32[]{:S(2)}) collective-permute-start(f32[80,512]{1,0:T(8,128)S(1)} %get-tuple-element.29), channel_id=1, source_target_pairs={{0,1},{1,0},{2,3},{3,2},{4,5},{5,4},{6,7},{7,6},{8,9},{9,8},{10,11... | collective-permute-start | bytes 491528 | tf_op jit(solution)/shard_map/ppermute | solution.py:697
  64.6 6.3 %collective-permute-start.6 = (f32[80,512]{1,0:T(8,128)S(1)}, f32[80,512]{1,0:T(8,128)S(1)}, u32[]{:S(2)}, u32[]{:S(2)}) collective-permute-start(f32[80,512]{1,0:T(8,128)S(1)} %add.29), channel_id=1, source_target_pairs={{0,2},{1,3},{2,0},{3,1},{4,6},{5,7},{6,4},{7,5},{8,10},{9,11},{10,... | collective-permute-start | bytes 491528 | tf_op jit(solution)/shard_map/ppermute | solution.py:697
  70.9 1.5 %collective-permute-start.7 = (f32[80,512]{1,0:T(8,128)S(1)}, f32[80,512]{1,0:T(8,128)S(1)}, u32[]{:S(2)}, u32[]{:S(2)}) collective-permute-start(f32[80,512]{1,0:T(8,128)S(1)} %add_add_fusion.mine_ref), channel_id=1, source_target_pairs={{0,1},{1,0},{2,3},{3,2},{4,5},{5,4},{6,7},{7,6},{8,9},{9,8},{10,11... | collective-permute-start | bytes 491528 | tf_op jit(solution)/shard_map/ppermute | solution.py:697

commit v2 on v0

--- a/solution.py
+++ b/solution.py
@@ -123,8 +123,10 @@
     )(state, state, courant_x)
 
 
-PIECE = 200
-BACK = 184
+PIECE = 192
+BACK = 176
+TAIL = 80
+SPARE = LANES - TAIL
 
 
 def tile_of(slab, t, width):
@@ -138,28 +140,30 @@
     fields, slots = first_ref.shape[:2]
     tiles = -(-width // LANES)
 
+    lane = lax.broadcasted_iota(jnp.int32, (8, LANES), 1)
+
     def put(row, tile):
         out_ref[pl.ds(row, 8, stride=PIECE), :] = tile
 
+    tails = []
     for j in range(slots):
         half = wind_ref[j, 0] * 0.5
-        for t in range(tiles):
-            row = {0: 192 + 2 * j, 1: 193 + 2 * j, 2: 64 * j + 62, 3: 64 * j + 63}.get(
-                t, 64 * j + 26 + t
-            )
-            put(row, tile_of(half, t, width))
-        for f in range(fields):
-            north = last_ref[f, j, 0] * half
-            south = first_ref[f, j, 0]
-            for t in range(tiles):
-                put(64 * j + f * tiles + t, tile_of(north, t, width))
-                put(64 * j + 32 + f * tiles + t, tile_of(south, t, width))
-    lane = lax.broadcasted_iota(jnp.int32, (8, LANES), 1)
-    table = jnp.zeros((8, LANES), F32)
+        north = [last_ref[f, j, 0] * half for f in range(fields)]
+        south = [first_ref[f, j, 0] for f in range(fields)]
+        for t in range(tiles - 1):
+            put(55 * j + 25 + t, tile_of(half, t, width))
+            for f in range(fields):
+                put(55 * j + t * fields + f, tile_of(north[f], t, width))
+                put(55 * j + 30 + t * fields + f, tile_of(south[f], t, width))
+        tails.append([tile_of(slab, tiles - 1, width) for slab in (*north, half, *south)])
+    for u, (a, b, c) in enumerate(zip(*tails)):
+        put(165 + u, jnp.where(lane < TAIL, a, pltpu.roll(c, TAIL, 1)))
+        put(176 + u, jnp.where(lane < TAIL, b, pltpu.roll(c, LANES - 2 * SPARE, 1)))
+    table = jnp.zeros((8, LANES), jnp.int32)
     for j in range(slots):
-        table = jnp.where(lane == j, block_ref[j].astype(F32), table)
-    put(198, table)
-    put(199, table)
+        table = jnp.where(lane == j, block_ref[j], table)
+    for row in range(187, PIECE):
+        put(row, table.astype(F32))
 
 
 def pack(state, courant_y, block):
@@ -181,53 +185,80 @@
 
 
 def face_kernel(
-    got_ref, cutoff_ref, later_in_ref, out_ref, later_ref, face_ref, table_ref, slot_ref, sem
+    got_ref,
+    cutoff_ref,
+    later_in_ref,
+    out_ref,
+    later_ref,
+    face_ref,
+    south_ref,
+    half_ref,
+    whole_ref,
+    table_ref,
+    slot_ref,
+    sem,
 ):
     del later_in_ref, later_ref
     parts = got_ref.shape[0]
     slots = face_ref.shape[0] // parts
     count = parts * slots
-    copy = pltpu.make_async_copy(got_ref.at[:, 192:200, :], table_ref, sem)
+    whole_ref[...] = got_ref[:, 184:192, :].astype(jnp.int32)
+    copy = pltpu.make_async_copy(whole_ref, table_ref, sem)
     copy.start()
+    lane = lax.broadcasted_iota(jnp.int32, (8, LANES), 1)
+    wide = lax.broadcasted_iota(jnp.int32, (16, LANES), 1)
+    tails = []
+    for s in range(count):
+        src, j = divmod(s, slots)
+        if j < 2:
+            tail = got_ref[src, 165 + 11 * j : 176 + 11 * j, :]
+        else:
+            one = pltpu.roll(got_ref[src, 165:181, :], SPARE, 1)
+            two = pltpu.roll(got_ref[src, 176:192, :], 2 * SPARE, 1)
+            tail = jnp.where(wide < SPARE, one, two)[:11]
+        south_ref[s, :25] = got_ref[src, 55 * j + 30 : 55 * j + 55, :]
+        south_ref[s, 25:30] = tail[6:]
+        face_ref[s, :25] = got_ref[src, 55 * j : 55 * j + 25, :]
+        face_ref[s, 25:30] = tail[:5]
+        half_ref[s, :5] = got_ref[src, 55 * j + 25 : 55 * j + 30, :]
+        half_ref[s, 5:6] = tail[5:6]
     copy.wait()
-    blocks = [table_ref[s // slots, 6, s % slots].astype(jnp.int32) for s in range(count)]
+    blocks = [table_ref[s // slots, 3, s % slots] for s in range(count)]
     slot_ref[0] = -1
     slot_ref[count + 1] = -1
     for s in range(count):
         slot_ref[blocks[s] + 1] = s
     for s in range(count):
-        src, j = divmod(s, slots)
         south = slot_ref[blocks[s] + 2]
-        safe = jnp.maximum(south, 0)
-        from_src = lax.div(safe, slots)
-        from_slot = safe - from_src * slots
         half = jnp.concatenate(
-            [
-                got_ref[src, 192 + 2 * j : 194 + 2 * j, :],
-                got_ref[src, 64 * j + 62 : 64 * j + 64, :],
-                got_ref[src, 64 * j + 30 : 64 * j + 32, :],
-            ],
-            axis=0,
+            [jnp.broadcast_to(half_ref[s, t : t + 1], (5, LANES)) for t in range(6)], axis=0
         )
-        half = jnp.concatenate([half] * 5 + [half[:2]], axis=0)
-        other = got_ref[from_src, pl.ds(pl.multiple_of(64 * from_slot + 32, 32), 32), :]
-        face = got_ref[src, 64 * j : 64 * j + 32, :] + half * other
-        face_ref[s] = jnp.where(south >= 0, face, 0.0)
+        face = face_ref[s, :30] + half * south_ref[jnp.maximum(south, 0), :30]
+        face_ref[s, :30] = jnp.where(south >= 0, face, 0.0)
     for d in range(parts):
         first, second, rest = pick_slots(blocks[slots * d : slots * d + slots], cutoff_ref, 8)
+        tails = []
         for i, slot in enumerate((first, second, rest)):
-            row = 60 * i
             block = jnp.where(
                 slot == 0,
                 blocks[slots * d],
                 jnp.where(slot == 1, blocks[slots * d + 1], blocks[slots * d + 2]),
             )
             north = slot_ref[block]
-            out_ref[d, row : row + 30] = jnp.where(
-                north >= 0, face_ref[jnp.maximum(north, 0), :30], 0.0
-            )
-            out_ref[d, row + 30 : row + 60] = face_ref[slots * d + slot, :30]
-        out_ref[d, 180:184] = jnp.zeros((4, LANES), F32)
+            for q, face, there in (
+                (2 * i, jnp.maximum(north, 0), north >= 0),
+                (2 * i + 1, slots * d + slot, None),
+            ):
+                rows, tail = face_ref[face, :25], face_ref[face, 24:32]
+                if there is not None:
+                    rows, tail = jnp.where(there, rows, 0.0), jnp.where(there, tail, 0.0)
+                out_ref[d, 25 * q : 25 * q + 25] = rows
+                tails.append(tail)
+        for q in range(4):
+            rest_tail = pltpu.roll(tails[4 + q % 2], TAIL if q < 2 else LANES - 2 * SPARE, 1)
+            tail = jnp.where(lane < TAIL, tails[q], rest_tail)
+            out_ref[d, 150 + 5 * q : 155 + 5 * q] = tail[1:6]
+        out_ref[d, 170:BACK] = jnp.zeros((BACK - 170, LANES), F32)
 
 
 def faces_of_pieces(got, slots, cutoff, later):
@@ -243,7 +274,10 @@
         input_output_aliases={2: 1},
         scratch_shapes=[
             pltpu.VMEM((parts * slots, 32, LANES), F32),
-            pltpu.SMEM((parts, 8, LANES), F32),
+            pltpu.VMEM((parts * slots, 32, LANES), F32),
+            pltpu.VMEM((parts * slots, 8, LANES), F32),
+            pltpu.VMEM((parts, 8, LANES), jnp.int32),
+            pltpu.SMEM((parts, 8, LANES), jnp.int32),
             pltpu.SMEM((parts * slots + 2,), jnp.int32),
             pltpu.SemaphoreType.DMA(()),
         ],
@@ -480,13 +514,21 @@
     )(place, block, cutoff, state, base, mine, away, *inverse, turn, after)
 
 
-def unpack(ref, base, stride, put, fields, width):
+def unpack(ref, full, tail, spare, put, fields, width):
     tiles = -(-width // LANES)
+    lane = lax.broadcasted_iota(jnp.int32, (8, LANES), 1)
+
+    def load(row):
+        return ref[pl.ds(row, 8, stride=BACK), :]
+
     for f in range(fields):
-        for t in range(tiles):
-            tile = ref[pl.ds(base + f * tiles + t, 8, stride=stride), :]
-            stop = min((t + 1) * LANES, width)
-            put(f, t * LANES, stop, tile[:, : stop - t * LANES])
+        for t in range(tiles - 1):
+            put(f, t * LANES, (t + 1) * LANES, load(full + t * fields + f))
+        tile = load(tail + f)
+        if spare is not None:
+            other = pltpu.roll(load(spare + f), 2 * SPARE, 1)
+            tile = jnp.where(lane < SPARE, pltpu.roll(tile, SPARE, 1), other)
+        put(f, (tiles - 1) * LANES, width, tile[:, :TAIL])
 
 
 def rim_kernel(
@@ -510,7 +552,8 @@
                 def put(f, start, stop, tile, i=i, side=side):
                     faces_ref[i, side, f, :, start:stop] = tile
 
-                unpack(got_ref, 60 * i + 30 * side, BACK, put, fields, width)
+                q = 2 * i + side
+                unpack(got_ref, 25 * q, 150 + 5 * q, None, put, fields, width)
     else:
         faces_ref[...] = got_ref[...]
     turn = turn_ref[place_ref[0]]
@@ -590,7 +633,9 @@
             old = main_ref[f, rest, 0, :, start:stop]
             out_ref[f, rest, 0, :, start:stop] = old + tile * sign
 
-        unpack(back_ref, 120 + 30 * side, BACK, put, fields, width)
+        unpack(
+            back_ref, 100 + 25 * side, 150 + 5 * side, 160 + 5 * side, put, fields, width
+        )
     else:
         out_ref[:, rest, 0] = main_ref[:, rest, 0] + back_ref[side] * sign
     cuts = [cutoff_ref[block_ref[slot] * rows + row] for slot in (mine, other)]
@@ -648,7 +693,7 @@
     turn = turn_table(lon, width)
     tables = (turn, place, block_of_slot, cutoff)
 
-    packed = lat == levels == 8 and -(-width // LANES) * fields == 30
+    packed = lat == levels == 8 and width == 5 * LANES + TAIL and fields == 5
     if packed:
         sent = pack(state, courant_y, block_of_slot).reshape(lat, PIECE, LANES)
         got = lax.all_to_all(sent, "lat", 0, 0, tiled=True)

time: 73.8 us -> 74.2 us (level)
  local copies, waits for them, and re-layouts: 0.91 us -> 1.79 us
    unnamed x22 -> x24, local copies, waits for them, and re-layouts: 0.91 us -> 1.79 us
  transfers between devices with their start and end apart: 10 -> 10, of which waited for: 6 -> 6; matrix products, arithmetic and copies ran while one was open for 2% -> 2% of each run, Pallas kernels for 35% -> 34%
where the time goes in v2:
time: 74.2 us; the launch traced here: 73.8 us
  Pallas kernels  30.4 us (41%)
  waiting for transfers between devices  21.6 us (29%)
  starting transfers between devices  18.4 us (25%)
  local copies, waits for them, and re-layouts  1.79 us (2%)
  other arithmetic  1.4 us (2%)
    ppermute x6, waiting for transfers between devices, swap(): return lax.ppermute(array, 'lon', [(i, i ^ bit) for i in range(size)])  18.9 us
    pallas_call x1, Pallas kernels, local_tendency(): pl.pallas_call(tendency_kernel, in_specs=vmem(8) + smem(3), out_specs=[pl...  12.6 us
    all_to_all x1, starting transfers between devices, shards(): got = lax.all_to_all(sent, 'lat', 0, 0, tiled=True)  7.28 us
    all_to_all x1, starting transfers between devices, shards(): back = lax.all_to_all(back, 'lat', 0, 0, tiled=True)  6.12 us
    pallas_call x1, Pallas kernels, main_part(): pl.pallas_call(main_kernel, grid_spec=pltpu.PrefetchScalarGridSpec(num_sc...  5.36 us
    pallas_call x1, Pallas kernels, faces_of_pieces(): pl.pallas_call(face_kernel, in_specs=vmem(1) + smem(1) + [pl.BlockSpec(me...  3.41 us
    ppermute x6, starting transfers between devices, swap(): return lax.ppermute(array, 'lon', [(i, i ^ bit) for i in range(size)])  3.3 us
    pallas_call x1, Pallas kernels, final_part(): pl.pallas_call(functools.partial(final_kernel, back.ndim == 2), grid=(2,)...  2.57 us
  transfers between devices with their start and end apart: 10, of which 6 were waited for; matrix products, arithmetic and copies ran while one was open for 2% of the time, Pallas kernels for 34%

profile of v2, /device:TPU:0, one launch (start us, length us, event | category | flops | bytes accessed | tf_op | source)
XLA Modules:
  0.0 73.8 jit_solution(10769691991552582599)
XLA Ops:
  0.0 2.5 %pack.1 = f32[1536,128]{1,0:T(8,128)} custom-call(f32[5,3,8,8,720]{4,3,2,1,0:T(8,128)} %state_ref.3, f32[5,3,8,8,720]{4,3,2,1,0:T(8,128)} %state_ref.3, f32[3,8,8,720]{3,2,1,0:T(8,128)} %wind_ref.3, s32[3]{0:T(128)} %block_ref.7), custom_call_target="tpu_custom_call" | custom-call | flops 100000 | bytes 1700000 | tf_op jit(solution)/shard_map/pack/pallas_call | solution.py:171
  2.5 7.3 %all-to-all-start = ((f32[8,192,128]{2,1,0:T(8,128)}), f32[8,192,128]{2,1,0:T(8,128)S(1)}, u32[]{:S(2)}, u32[]{:S(2)}) async-start(f32[8,192,128]{2,1,0:T(8,128)} %bitcast.8), calls=%async_computation | async-start | bytes 1572864 | tf_op jit(solution)/shard_map/all_to_all | solution.py:699
  9.8 0.0 copy-start.5
  9.8 0.0 copy-start.6
  9.8 0.0 copy-start.7
  9.8 2.4 %edges.1 = (f32[3,8,128]{2,1,0:T(8,128)}, f32[3,8,128]{2,1,0:T(8,128)}) custom-call(f32[5,3,8,8,720]{4,3,2,1,0:T(8,128)} %state_ref.3, f32[5,3,8,8,720]{4,3,2,1,0:T(8,128)} %state_ref.3, f32[3,8,8,720]{3,2,1,0:T(8,128)} %cx_ref.1), custom_call_target="tpu_custom_call" | custom-call | flops 100000 | bytes 1200000 | tf_op jit(solution)/shard_map/edges/pallas_call | solution.py:111
  12.2 1.7 %collective-permute-start.1 = (f32[3,8,128]{2,1,0:T(8,128)}, f32[3,8,128]{2,1,0:T(8,128)S(1)}, u32[]{:S(2)}, u32[]{:S(2)}) collective-permute-start(f32[3,8,128]{2,1,0:T(8,128)} %get-tuple-element.19), channel_id=1, source_target_pairs={{1,0},{2,1},{3,2},{0,3},{5,4},{6,5},{7,6},{4,7},{9,8},{10,9},{11,1... | collective-permute-start | bytes 36872 | tf_op jit(solution)/shard_map/ppermute | solution.py:703
  14.0 0.1 pad_add_fusion.place_ref
  14.1 1.5 %collective-permute-done.west_ref = f32[3,8,128]{2,1,0:T(8,128)S(1)} collective-permute-done((f32[3,8,128]{2,1,0:T(8,128)}, f32[3,8,128]{2,1,0:T(8,128)S(1)}, u32[]{:S(2)}, u32[]{:S(2)}) %collective-permute-start) | collective-permute-done | bytes 12320 | tf_op jit(solution)/shard_map/ppermute | solution.py:702
  15.6 0.0 collective-permute-done.1.east_ref
  15.6 12.6 %tendency.1 = (f32[5,3,8,8,720]{4,3,2,1,0:T(8,128)}, f32[320,512]{1,0:T(8,128)S(1)}, f32[320,512]{1,0:T(8,128)}) custom-call(f32[5,3,8,8,720]{4,3,2,1,0:T(8,128)} %state_ref.3, f32[3,8,8,720]{3,2,1,0:T(8,128)S(1)} %copy-done.4, f32[3,8,8,720]{3,2,1,0:T(8,128)S(1)} %copy-done.3, f32[3,8,128]{2,1,0:T(8,128)S(1)} %collective-permute-done.west_ref, ...), custom_call_target="tpu_custom_call" | custom-call | flops 1415577600 | bytes 9000000 | tf_op jit(solution)/shard_map/tendency/pallas_call | solution.py:429
  28.3 0.8 %copy-done.2 = f32[320,512]{1,0:T(8,128)} copy-done((f32[320,512]{1,0:T(8,128)}, f32[320,512]{1,0:T(8,128)S(1)}, u32[]{:S(2)}) %copy-start.2) | copy-done | bytes 655384
  29.1 1.9 %collective-permute-start.2 = (f32[320,512]{1,0:T(8,128)}, f32[320,512]{1,0:T(8,128)S(1)}, u32[]{:S(2)}, u32[]{:S(2)}) collective-permute-start(f32[320,512]{1,0:T(8,128)} %get-tuple-element.23), channel_id=1, source_target_pairs={{0,1},{1,0},{2,3},{3,2},{4,5},{5,4},{6,7},{7,6},{8,9},{9,8},{10,11... | collective-permute-start | bytes 1966088 | tf_op jit(solution)/shard_map/ppermute | solution.py:673
  31.0 0.9 %copy-done.11 = f32[8,192,128]{2,1,0:T(8,128)} copy-done((f32[8,192,128]{2,1,0:T(8,128)}, f32[8,192,128]{2,1,0:T(8,128)S(1)}, u32[]{:S(2)}) %copy-start.11) | copy-done | bytes 786456
  31.9 3.4 %faces.1 = (f32[8,176,128]{2,1,0:T(8,128)}, f32[320,512]{1,0:T(8,128)}) custom-call(f32[8,192,128]{2,1,0:T(8,128)} %copy-done.11, s32[192]{0:T(256)} %cutoff_ref.7, f32[320,512]{1,0:T(8,128)} %copy-done.2), custom_call_target="tpu_custom_call", output_to_operand_aliasing={{1}: (2, {})} | custom-call | flops 100000 | bytes 1600000 | tf_op jit(solution)/shard_map/faces/pallas_call | solution.py:266
  35.3 0.0 copy-start
  35.3 6.1 %all-to-all-start.1 = ((f32[8,176,128]{2,1,0:T(8,128)}), f32[8,176,128]{2,1,0:T(8,128)S(1)}, u32[]{:S(2)}, u32[]{:S(2)}) async-start(f32[8,176,128]{2,1,0:T(8,128)} %get-tuple-element.24), calls=%async_computation.1 | async-start | bytes 1441792 | tf_op jit(solution)/shard_map/all_to_all | solution.py:709
  41.5 1.2 %add.27 = f32[320,512]{1,0:T(8,128)S(1)} add(f32[320,512]{1,0:T(8,128)} %get-tuple-element.22, f32[320,512]{1,0:T(8,128)S(1)} %collective-permute-done.2) | non-fusion elementwise | flops 163840 | bytes 1966080 | tf_op jit(solution)/shard_map/add | solution.py:677
  42.6 0.6 collective-permute-start.3
  43.3 15.8 %collective-permute-done.3 = f32[320,512]{1,0:T(8,128)S(1)} collective-permute-done((f32[320,512]{1,0:T(8,128)S(1)}, f32[320,512]{1,0:T(8,128)S(1)}, u32[]{:S(2)}, u32[]{:S(2)}) %collective-permute-start.3) | collective-permute-done | bytes 655392 | tf_op jit(solution)/shard_map/ppermute | solution.py:673
  59.1 0.1 add.28.mine_ref
  59.2 0.1 collective-permute-start.4
  59.3 1.1 %all-to-all-done.1 = f32[8,176,128]{2,1,0:T(8,128)S(1)} async-done(((f32[8,176,128]{2,1,0:T(8,128)}), f32[8,176,128]{2,1,0:T(8,128)S(1)}, u32[]{:S(2)}, u32[]{:S(2)}) %all-to-all-start.1) | async-done | bytes 720928 | tf_op jit(solution)/shard_map/all_to_all | solution.py:709
  60.4 1.6 %rim_spectra.1 = (f32[2,2,5,8,720]{4,3,2,1,0:T(8,128)S(1)}, f32[80,512]{1,0:T(8,128)S(1)}, f32[80,512]{1,0:T(8,128)S(1)}, f32[8,128]{1,0:T(8,128)S(1)}) custom-call(f32[1408,128]{1,0:T(8,128)S(1)} %bitcast.5, bf16[512,720]{1,0:T(8,128)(2,1)S(1)} %copy-done.1, bf16[512,720]{1,0:T(8,128)(2,1)S(1)} %copy-done, f32[4,1,512]{2,1,0:T(1,128)S(1)} %copy-done.7, ...), custom_call_target="tpu_custom_call" | custom-call | flops 353894400 | bytes 3000000 | tf_op jit(solution)/shard_map/rim_spectra/pallas_call | solution.py:572
  61.9 0.1 collective-permute-start.5
  62.0 1.4 %collective-permute-done.5 = f32[80,512]{1,0:T(8,128)S(1)} collective-permute-done((f32[80,512]{1,0:T(8,128)S(1)}, f32[80,512]{1,0:T(8,128)S(1)}, u32[]{:S(2)}, u32[]{:S(2)}) %collective-permute-start.5) | collective-permute-done | bytes 163872 | tf_op jit(solution)/shard_map/ppermute | solution.py:673
  63.4 0.6 collective-permute-start.6
  64.0 5.4 %main.1 = (f32[5,3,8,8,720]{4,3,2,1,0:T(8,128)}, f32[1,512]{1,0:T(1,128)S(1)}) custom-call(s32[2]{0:T(128)S(1)} %pad_add_fusion.place_ref, s32[3]{0:T(128)S(1)} %copy-done.10, s32[192]{0:T(256)S(1)} %copy-done.9, f32[5,3,8,8,720]{4,3,2,1,0:T(8,128)} %state_ref.3, f32[5,3,8,8,720]{4,3,2,1,0:T(8,128)} %get-tuple-element.20.base_ref, ...), custom_call_target="tpu_custom_call", output_to_operand_aliasing={{0}: (4, {})} | custom-call | flops 1415577600 | bytes 6000000 | tf_op jit(solution)/shard_map/main/pallas_call | solution.py:494
  69.4 0.3 collective-permute-done.6
  69.8 0.1 collective-permute-start.7
  69.9 1.4 %collective-permute-done.7.away_ref = f32[80,512]{1,0:T(8,128)S(1)} collective-permute-done((f32[80,512]{1,0:T(8,128)S(1)}, f32[80,512]{1,0:T(8,128)S(1)}, u32[]{:S(2)}, u32[]{:S(2)}) %collective-permute-start.7) | collective-permute-done | bytes 163872 | tf_op jit(solution)/shard_map/ppermute | solution.py:673
  71.2 2.6 %final.1 = f32[5,3,8,8,720]{4,3,2,1,0:T(8,128)} custom-call(f32[5,3,8,8,720]{4,3,2,1,0:T(8,128)} %get-tuple-element.26.main_ref, f32[2,2,5,8,720]{4,3,2,1,0:T(8,128)S(1)} %get-tuple-element.27.pair_ref, f32[1408,128]{1,0:T(8,128)S(1)} %bitcast.6, f32[80,512]{1,0:T(8,128)S(1)} %add_add_fusion.mine_ref, ...), custom_call_target="tpu_custom_call", output_to_operand_aliasing={{}: (0, {})} | custom-call | flops 353894400 | bytes 4000000 | tf_op jit(solution)/shard_map/final/pallas_call | solution.py:653
  (24 shorter events, 0.1 us)
Async XLA Ops:
  2.5 28.5 %all-to-all-start = ((f32[8,192,128]{2,1,0:T(8,128)}), f32[8,192,128]{2,1,0:T(8,128)S(1)}, u32[]{:S(2)}, u32[]{:S(2)}) async-start(f32[8,192,128]{2,1,0:T(8,128)} %bitcast.8), calls=%async_computation | async-start | bytes 1572864 | tf_op jit(solution)/shard_map/all_to_all | solution.py:699
  9.8 5.8 %copy-start.3 = (f32[3,8,8,720]{3,2,1,0:T(8,128)S(1)}, f32[3,8,8,720]{3,2,1,0:T(8,128)}, u32[]{:S(2)}) copy-start(f32[3,8,8,720]{3,2,1,0:T(8,128)} %wind_ref.3) | copy-start | bytes 1658884
  9.8 5.8 %copy-start.4 = (f32[3,8,8,720]{3,2,1,0:T(8,128)S(1)}, f32[3,8,8,720]{3,2,1,0:T(8,128)}, u32[]{:S(2)}) copy-start(f32[3,8,8,720]{3,2,1,0:T(8,128)} %cx_ref.1) | copy-start | bytes 1658884
  9.8 5.8 %copy-start.5 = (bf16[720,512]{1,0:T(8,128)(2,1)S(1)}, bf16[720,512]{1,0:T(8,128)(2,1)}, u32[]{:S(2)}) copy-start(bf16[720,512]{1,0:T(8,128)(2,1)} %constant.28.clone.low_ref) | copy-start | bytes 2211844
  9.8 5.8 %copy-start.6 = (bf16[720,512]{1,0:T(8,128)(2,1)S(1)}, bf16[720,512]{1,0:T(8,128)(2,1)}, u32[]{:S(2)}) copy-start(bf16[720,512]{1,0:T(8,128)(2,1)} %constant.27.clone.high_ref) | copy-start | bytes 2211844
  9.8 5.8 %copy-start.7 = (f32[4,1,512]{2,1,0:T(1,128)S(1)}, f32[4,1,512]{2,1,0:T(1,128)}, u32[]{:S(2)}) copy-start(f32[4,1,512]{2,1,0:T(1,128)} %constant.31.clone.turn_ref) | copy-start | bytes 24580
  9.8 5.8 %copy-start.8 = (s32[192]{0:T(256)S(1)}, s32[192]{0:T(256)}, u32[]{:S(2)}) copy-start(s32[192]{0:T(256)} %cutoff_ref.7) | copy-start | bytes 2308
  9.8 5.8 %copy-start.10 = (s32[3]{0:T(128)S(1)}, s32[3]{0:T(128)}, u32[]{:S(2)}) copy-start(s32[3]{0:T(128)} %block_ref.7) | copy-start | bytes 40
  12.2 3.3 %collective-permute-start = (f32[3,8,128]{2,1,0:T(8,128)}, f32[3,8,128]{2,1,0:T(8,128)S(1)}, u32[]{:S(2)}, u32[]{:S(2)}) collective-permute-start(f32[3,8,128]{2,1,0:T(8,128)} %get-tuple-element.18), channel_id=1, source_target_pairs={{0,1},{1,2},{2,3},{3,0},{4,5},{5,6},{6,7},{7,4},{8,9},{9,10},{10,1... | collective-permute-start | bytes 36872 | tf_op jit(solution)/shard_map/ppermute | solution.py:702
  12.2 3.4 %collective-permute-start.1 = (f32[3,8,128]{2,1,0:T(8,128)}, f32[3,8,128]{2,1,0:T(8,128)S(1)}, u32[]{:S(2)}, u32[]{:S(2)}) collective-permute-start(f32[3,8,128]{2,1,0:T(8,128)} %get-tuple-element.19), channel_id=1, source_target_pairs={{1,0},{2,1},{3,2},{0,3},{5,4},{6,5},{7,6},{4,7},{9,8},{10,9},{11,1... | collective-permute-start | bytes 36872 | tf_op jit(solution)/shard_map/ppermute | solution.py:703
  28.3 0.8 %copy-start.2 = (f32[320,512]{1,0:T(8,128)}, f32[320,512]{1,0:T(8,128)S(1)}, u32[]{:S(2)}) copy-start(f32[320,512]{1,0:T(8,128)S(1)} %get-tuple-element.21.later_in_ref) | copy-start | bytes 1966084
  29.1 12.3 %collective-permute-start.2 = (f32[320,512]{1,0:T(8,128)}, f32[320,512]{1,0:T(8,128)S(1)}, u32[]{:S(2)}, u32[]{:S(2)}) collective-permute-start(f32[320,512]{1,0:T(8,128)} %get-tuple-element.23), channel_id=1, source_target_pairs={{0,1},{1,0},{2,3},{3,2},{4,5},{5,4},{6,7},{7,6},{8,9},{9,8},{10,11... | collective-permute-start | bytes 1966088 | tf_op jit(solution)/shard_map/ppermute | solution.py:673
  31.0 0.9 %copy-start.11 = (f32[8,192,128]{2,1,0:T(8,128)}, f32[8,192,128]{2,1,0:T(8,128)S(1)}, u32[]{:S(2)}) copy-start(f32[8,192,128]{2,1,0:T(8,128)S(1)} %all-to-all-done.got_ref) | copy-start | bytes 2359300
  35.3 25.1 %copy-start = (bf16[512,720]{1,0:T(8,128)(2,1)S(1)}, bf16[512,720]{1,0:T(8,128)(2,1)}, u32[]{:S(2)}) copy-start(bf16[512,720]{1,0:T(8,128)(2,1)} %constant.30.clone.low_ref) | copy-start | bytes 2211844
  35.3 25.1 %copy-start.1 = (bf16[512,720]{1,0:T(8,128)(2,1)S(1)}, bf16[512,720]{1,0:T(8,128)(2,1)}, u32[]{:S(2)}) copy-start(bf16[512,720]{1,0:T(8,128)(2,1)} %constant.29.clone.high_ref) | copy-start | bytes 2211844
  35.3 25.0 %all-to-all-start.1 = ((f32[8,176,128]{2,1,0:T(8,128)}), f32[8,176,128]{2,1,0:T(8,128)S(1)}, u32[]{:S(2)}, u32[]{:S(2)}) async-start(f32[8,176,128]{2,1,0:T(8,128)} %get-tuple-element.24), calls=%async_computation.1 | async-start | bytes 1441792 | tf_op jit(solution)/shard_map/all_to_all | solution.py:709
  41.5 22.6 %copy-start.9 = (s32[192]{0:T(256)S(1)}, s32[192]{0:T(256)}, u32[]{:S(2)}) copy-start(s32[192]{0:T(256)} %cutoff_ref.7) | copy-start | bytes 2308
  42.6 16.4 %collective-permute-start.3 = (f32[320,512]{1,0:T(8,128)S(1)}, f32[320,512]{1,0:T(8,128)S(1)}, u32[]{:S(2)}, u32[]{:S(2)}) collective-permute-start(f32[320,512]{1,0:T(8,128)S(1)} %add.27), channel_id=1, source_target_pairs={{0,2},{1,3},{2,0},{3,1},{4,6},{5,7},{6,4},{7,5},{8,10},{9,11},{10,... | collective-permute-start | bytes 1966088 | tf_op jit(solution)/shard_map/ppermute | solution.py:673
  59.2 4.9 %collective-permute-start.4 = (f32[320,512]{1,0:T(8,128)S(1)}, f32[320,512]{1,0:T(8,128)}, u32[]{:S(2)}, u32[]{:S(2)}) collective-permute-start(f32[320,512]{1,0:T(8,128)S(1)} %add.28.mine_ref), channel_id=1, source_target_pairs={{0,1},{1,0},{2,3},{3,2},{4,5},{5,4},{6,7},{7,6},{8,9},{9,8},{10,11... | collective-permute-start | bytes 1966088 | tf_op jit(solution)/shard_map/ppermute | solution.py:673
  61.9 1.5 %collective-permute-start.5 = (f32[80,512]{1,0:T(8,128)S(1)}, f32[80,512]{1,0:T(8,128)S(1)}, u32[]{:S(2)}, u32[]{:S(2)}) collective-permute-start(f32[80,512]{1,0:T(8,128)S(1)} %get-tuple-element.29), channel_id=1, source_target_pairs={{0,1},{1,0},{2,3},{3,2},{4,5},{5,4},{6,7},{7,6},{8,9},{9,8},{10,11... | collective-permute-start | bytes 491528 | tf_op jit(solution)/shard_map/ppermute | solution.py:673
  63.4 6.3 %collective-permute-start.6 = (f32[80,512]{1,0:T(8,128)S(1)}, f32[80,512]{1,0:T(8,128)S(1)}, u32[]{:S(2)}, u32[]{:S(2)}) collective-permute-start(f32[80,512]{1,0:T(8,128)S(1)} %add.29), channel_id=1, source_target_pairs={{0,2},{1,3},{2,0},{3,1},{4,6},{5,7},{6,4},{7,5},{8,10},{9,11},{10,... | collective-permute-start | bytes 491528 | tf_op jit(solution)/shard_map/ppermute | solution.py:673
  69.8 1.5 %collective-permute-start.7 = (f32[80,512]{1,0:T(8,128)S(1)}, f32[80,512]{1,0:T(8,128)S(1)}, u32[]{:S(2)}, u32[]{:S(2)}) collective-permute-start(f32[80,512]{1,0:T(8,128)S(1)} %add_add_fusion.mine_ref), channel_id=1, source_target_pairs={{0,1},{1,0},{2,3},{3,2},{4,5},{5,4},{6,7},{7,6},{8,9},{9,8},{10,11... | collective-permute-start | bytes 491528 | tf_op jit(solution)/shard_map/ppermute | solution.py:673

commit v3 on v2

--- a/solution.py
+++ b/solution.py
@@ -281,6 +281,7 @@
             pltpu.SMEM((parts * slots + 2,), jnp.int32),
             pltpu.SemaphoreType.DMA(()),
         ],
+        compiler_params=pltpu.CompilerParams(vmem_limit_bytes=16 * MIB),
         cost_estimate=pl.CostEstimate(flops=10**5, bytes_accessed=1600000, transcendentals=0),
         name="faces",
     )(got, cutoff, later)

time: 74.2 us -> 74.1 us (level)
  Pallas kernels: 30.4 us -> 28.8 us
  local copies, waits for them, and re-layouts: 1.79 us -> 3.13 us
    pallas_call x1, Pallas kernels: 3.41 us -> 1.95 us  [faces_of_pieces(): pl.pallas_call(face_kernel, in_specs=vmem(1) + smem(1) + [pl.BlockSpec(me...]
    unnamed x24 -> x20, local copies, waits for them, and re-layouts: 1.79 us -> 3.13 us
  transfers between devices with their start and end apart: 10 -> 10, of which waited for: 6 -> 6; matrix products, arithmetic and copies ran while one was open for 2% -> 2% of each run, Pallas kernels for 34% -> 32%
where the time goes in v3:
time: 74.1 us; the launch traced here: 73.6 us
  Pallas kernels  28.8 us (39%)
  waiting for transfers between devices  21.6 us (29%)
  starting transfers between devices  18.5 us (25%)
  local copies, waits for them, and re-layouts  3.13 us (4%)
  other arithmetic  1.45 us (2%)
    ppermute x6, waiting for transfers between devices, swap(): return lax.ppermute(array, 'lon', [(i, i ^ bit) for i in range(size)])  19 us
    pallas_call x1, Pallas kernels, local_tendency(): pl.pallas_call(tendency_kernel, in_specs=vmem(8) + smem(3), out_specs=[pl...  12.6 us
    all_to_all x1, starting transfers between devices, shards(): got = lax.all_to_all(sent, 'lat', 0, 0, tiled=True)  7.28 us
    all_to_all x1, starting transfers between devices, shards(): back = lax.all_to_all(back, 'lat', 0, 0, tiled=True)  6.12 us
    pallas_call x1, Pallas kernels, main_part(): pl.pallas_call(main_kernel, grid_spec=pltpu.PrefetchScalarGridSpec(num_sc...  5.36 us
    ppermute x6, starting transfers between devices, swap(): return lax.ppermute(array, 'lon', [(i, i ^ bit) for i in range(size)])  3.36 us
    unnamed x20, local copies, waits for them, and re-layouts  3.13 us
    pallas_call x1, Pallas kernels, final_part(): pl.pallas_call(functools.partial(final_kernel, back.ndim == 2), grid=(2,)...  2.58 us
  transfers between devices with their start and end apart: 10, of which 6 were waited for; matrix products, arithmetic and copies ran while one was open for 2% of the time, Pallas kernels for 32%

profile of v3, /device:TPU:0, one launch (start us, length us, event | category | flops | bytes accessed | tf_op | source)
XLA Modules:
  0.0 73.6 jit_solution(17821709942777351811)
XLA Ops:
  0.0 2.5 %pack.1 = f32[1536,128]{1,0:T(8,128)} custom-call(f32[5,3,8,8,720]{4,3,2,1,0:T(8,128)} %state_ref.3, f32[5,3,8,8,720]{4,3,2,1,0:T(8,128)} %state_ref.3, f32[3,8,8,720]{3,2,1,0:T(8,128)} %wind_ref.3, s32[3]{0:T(128)} %block_ref.7), custom_call_target="tpu_custom_call" | custom-call | flops 100000 | bytes 1700000 | tf_op jit(solution)/shard_map/pack/pallas_call | solution.py:171
  2.5 7.3 %all-to-all-start = ((f32[8,192,128]{2,1,0:T(8,128)}), f32[8,192,128]{2,1,0:T(8,128)S(1)}, u32[]{:S(2)}, u32[]{:S(2)}) async-start(f32[8,192,128]{2,1,0:T(8,128)} %bitcast.8), calls=%async_computation | async-start | bytes 1572864 | tf_op jit(solution)/shard_map/all_to_all | solution.py:700
  9.8 0.0 copy-start.7
  9.8 0.0 copy-start.8
  9.8 2.3 %edges.1 = (f32[3,8,128]{2,1,0:T(8,128)}, f32[3,8,128]{2,1,0:T(8,128)}) custom-call(f32[5,3,8,8,720]{4,3,2,1,0:T(8,128)} %state_ref.3, f32[5,3,8,8,720]{4,3,2,1,0:T(8,128)} %state_ref.3, f32[3,8,8,720]{3,2,1,0:T(8,128)} %cx_ref.1), custom_call_target="tpu_custom_call" | custom-call | flops 100000 | bytes 1200000 | tf_op jit(solution)/shard_map/edges/pallas_call | solution.py:111
  12.1 1.7 %collective-permute-start.1 = (f32[3,8,128]{2,1,0:T(8,128)}, f32[3,8,128]{2,1,0:T(8,128)S(1)}, u32[]{:S(2)}, u32[]{:S(2)}) collective-permute-start(f32[3,8,128]{2,1,0:T(8,128)} %get-tuple-element.19), channel_id=1, source_target_pairs={{1,0},{2,1},{3,2},{0,3},{5,4},{6,5},{7,6},{4,7},{9,8},{10,9},{11,1... | collective-permute-start | bytes 36872 | tf_op jit(solution)/shard_map/ppermute | solution.py:704
  13.9 0.1 pad_add_fusion.place_ref
  14.0 1.5 %collective-permute-done.west_ref = f32[3,8,128]{2,1,0:T(8,128)S(1)} collective-permute-done((f32[3,8,128]{2,1,0:T(8,128)}, f32[3,8,128]{2,1,0:T(8,128)S(1)}, u32[]{:S(2)}, u32[]{:S(2)}) %collective-permute-start) | collective-permute-done | bytes 12320 | tf_op jit(solution)/shard_map/ppermute | solution.py:703
  15.5 0.0 collective-permute-done.1.east_ref
  15.5 0.0 copy-start.4
  15.5 1.1 %copy-done.4 = bf16[720,512]{1,0:T(8,128)(2,1)S(1)} copy-done((bf16[720,512]{1,0:T(8,128)(2,1)S(1)}, bf16[720,512]{1,0:T(8,128)(2,1)}, u32[]{:S(2)}) %copy-start.4) | copy-done | bytes 737304
  16.6 1.1 %copy-done.5 = bf16[720,512]{1,0:T(8,128)(2,1)S(1)} copy-done((bf16[720,512]{1,0:T(8,128)(2,1)S(1)}, bf16[720,512]{1,0:T(8,128)(2,1)}, u32[]{:S(2)}) %copy-start.5) | copy-done | bytes 737304
  17.8 12.6 %tendency.1 = (f32[5,3,8,8,720]{4,3,2,1,0:T(8,128)}, f32[320,512]{1,0:T(8,128)S(1)}, f32[320,512]{1,0:T(8,128)}) custom-call(f32[5,3,8,8,720]{4,3,2,1,0:T(8,128)} %state_ref.3, f32[3,8,8,720]{3,2,1,0:T(8,128)S(1)} %copy-done.3, f32[3,8,8,720]{3,2,1,0:T(8,128)S(1)} %copy-done.2, f32[3,8,128]{2,1,0:T(8,128)S(1)} %collective-permute-done.west_ref, ...), custom_call_target="tpu_custom_call" | custom-call | flops 1415577600 | bytes 9000000 | tf_op jit(solution)/shard_map/tendency/pallas_call | solution.py:430
  30.4 1.9 %collective-permute-start.2 = (f32[320,512]{1,0:T(8,128)}, f32[320,512]{1,0:T(8,128)}, u32[]{:S(2)}, u32[]{:S(2)}) collective-permute-start(f32[320,512]{1,0:T(8,128)} %get-tuple-element.23), channel_id=1, source_target_pairs={{0,1},{1,0},{2,3},{3,2},{4,5},{5,4},{6,7},{7,6},{8,9},{9,8},{10,11... | collective-permute-start | bytes 1966088 | tf_op jit(solution)/shard_map/ppermute | solution.py:674
  32.3 2.0 %faces.1 = (f32[8,176,128]{2,1,0:T(8,128)S(1)}, f32[320,512]{1,0:T(8,128)S(1)}) custom-call(f32[8,192,128]{2,1,0:T(8,128)S(1)} %all-to-all-done.got_ref, s32[192]{0:T(256)S(1)} %copy-done.8, f32[320,512]{1,0:T(8,128)S(1)} %get-tuple-element.21.later_in_ref), custom_call_target="tpu_custom_call", output_to_operand_aliasing={{1}: (2, {})} | custom-call | flops 100000 | bytes 1600000 | tf_op jit(solution)/shard_map/faces/pallas_call | solution.py:266
  34.3 0.9 %copy-done.6 = f32[8,176,128]{2,1,0:T(8,128)} copy-done((f32[8,176,128]{2,1,0:T(8,128)}, f32[8,176,128]{2,1,0:T(8,128)S(1)}, u32[]{:S(2)}) %copy-start.6) | copy-done | bytes 720920
  35.1 6.1 %all-to-all-start.1 = ((f32[8,176,128]{2,1,0:T(8,128)}), f32[8,176,128]{2,1,0:T(8,128)S(1)}, u32[]{:S(2)}, u32[]{:S(2)}) async-start(f32[8,176,128]{2,1,0:T(8,128)} %copy-done.6), calls=%async_computation.1 | async-start | bytes 1441792 | tf_op jit(solution)/shard_map/all_to_all | solution.py:710
  41.3 1.2 %add.27 = f32[320,512]{1,0:T(8,128)S(1)} add(f32[320,512]{1,0:T(8,128)S(1)} %get-tuple-element.22, f32[320,512]{1,0:T(8,128)} %collective-permute-done.2) | non-fusion elementwise | flops 163840 | bytes 1966080 | tf_op jit(solution)/shard_map/add | solution.py:678
  42.5 0.6 collective-permute-start.3
  43.1 15.8 %collective-permute-done.3 = f32[320,512]{1,0:T(8,128)S(1)} collective-permute-done((f32[320,512]{1,0:T(8,128)S(1)}, f32[320,512]{1,0:T(8,128)S(1)}, u32[]{:S(2)}, u32[]{:S(2)}) %collective-permute-start.3) | collective-permute-done | bytes 655392 | tf_op jit(solution)/shard_map/ppermute | solution.py:674
  58.9 0.1 add.28.mine_ref
  59.0 0.1 collective-permute-start.4
  59.1 1.1 %all-to-all-done.1 = f32[8,176,128]{2,1,0:T(8,128)S(1)} async-done(((f32[8,176,128]{2,1,0:T(8,128)}), f32[8,176,128]{2,1,0:T(8,128)S(1)}, u32[]{:S(2)}, u32[]{:S(2)}) %all-to-all-start.1) | async-done | bytes 720928 | tf_op jit(solution)/shard_map/all_to_all | solution.py:710
  60.2 1.6 %rim_spectra.1 = (f32[2,2,5,8,720]{4,3,2,1,0:T(8,128)S(1)}, f32[80,512]{1,0:T(8,128)S(1)}, f32[80,512]{1,0:T(8,128)S(1)}, f32[8,128]{1,0:T(8,128)S(1)}) custom-call(f32[1408,128]{1,0:T(8,128)S(1)} %bitcast.5, bf16[512,720]{1,0:T(8,128)(2,1)S(1)} %copy-done.1, bf16[512,720]{1,0:T(8,128)(2,1)S(1)} %copy-done, f32[4,1,512]{2,1,0:T(1,128)S(1)} %copy-done.7, ...), custom_call_target="tpu_custom_call" | custom-call | flops 353894400 | bytes 3000000 | tf_op jit(solution)/shard_map/rim_spectra/pallas_call | solution.py:573
  61.8 0.1 collective-permute-start.5
  61.8 1.4 %collective-permute-done.5 = f32[80,512]{1,0:T(8,128)S(1)} collective-permute-done((f32[80,512]{1,0:T(8,128)S(1)}, f32[80,512]{1,0:T(8,128)S(1)}, u32[]{:S(2)}, u32[]{:S(2)}) %collective-permute-start.5) | collective-permute-done | bytes 163872 | tf_op jit(solution)/shard_map/ppermute | solution.py:674
  63.3 0.6 collective-permute-start.6
  63.9 5.4 %main.1 = (f32[5,3,8,8,720]{4,3,2,1,0:T(8,128)}, f32[1,512]{1,0:T(1,128)S(1)}) custom-call(s32[2]{0:T(128)S(1)} %pad_add_fusion.place_ref, s32[3]{0:T(128)S(1)} %copy-done.9, s32[192]{0:T(256)S(1)} %copy-done.8, f32[5,3,8,8,720]{4,3,2,1,0:T(8,128)} %state_ref.3, f32[5,3,8,8,720]{4,3,2,1,0:T(8,128)} %get-tuple-element.20.base_ref, ...), custom_call_target="tpu_custom_call", output_to_operand_aliasing={{0}: (4, {})} | custom-call | flops 1415577600 | bytes 6000000 | tf_op jit(solution)/shard_map/main/pallas_call | solution.py:495
  69.2 0.4 collective-permute-done.6
  69.6 0.1 collective-permute-start.7
  69.7 1.4 %collective-permute-done.7.away_ref = f32[80,512]{1,0:T(8,128)S(1)} collective-permute-done((f32[80,512]{1,0:T(8,128)S(1)}, f32[80,512]{1,0:T(8,128)S(1)}, u32[]{:S(2)}, u32[]{:S(2)}) %collective-permute-start.7) | collective-permute-done | bytes 163872 | tf_op jit(solution)/shard_map/ppermute | solution.py:674
  71.1 2.6 %final.1 = f32[5,3,8,8,720]{4,3,2,1,0:T(8,128)} custom-call(f32[5,3,8,8,720]{4,3,2,1,0:T(8,128)} %get-tuple-element.26.main_ref, f32[2,2,5,8,720]{4,3,2,1,0:T(8,128)S(1)} %get-tuple-element.27.pair_ref, f32[1408,128]{1,0:T(8,128)S(1)} %bitcast.6, f32[80,512]{1,0:T(8,128)S(1)} %add_add_fusion.mine_ref, ...), custom_call_target="tpu_custom_call", output_to_operand_aliasing={{}: (0, {})} | custom-call | flops 353894400 | bytes 4000000 | tf_op jit(solution)/shard_map/final/pallas_call | solution.py:654
  (20 shorter events, 0.1 us)
Async XLA Ops:
  2.5 29.8 %all-to-all-start = ((f32[8,192,128]{2,1,0:T(8,128)}), f32[8,192,128]{2,1,0:T(8,128)S(1)}, u32[]{:S(2)}, u32[]{:S(2)}) async-start(f32[8,192,128]{2,1,0:T(8,128)} %bitcast.8), calls=%async_computation | async-start | bytes 1572864 | tf_op jit(solution)/shard_map/all_to_all | solution.py:700
  9.8 5.7 %copy-start.2 = (f32[3,8,8,720]{3,2,1,0:T(8,128)S(1)}, f32[3,8,8,720]{3,2,1,0:T(8,128)}, u32[]{:S(2)}) copy-start(f32[3,8,8,720]{3,2,1,0:T(8,128)} %wind_ref.3) | copy-start | bytes 1658884
  9.8 5.7 %copy-start.3 = (f32[3,8,8,720]{3,2,1,0:T(8,128)S(1)}, f32[3,8,8,720]{3,2,1,0:T(8,128)}, u32[]{:S(2)}) copy-start(f32[3,8,8,720]{3,2,1,0:T(8,128)} %cx_ref.1) | copy-start | bytes 1658884
  9.8 5.7 %copy-start.7 = (f32[4,1,512]{2,1,0:T(1,128)S(1)}, f32[4,1,512]{2,1,0:T(1,128)}, u32[]{:S(2)}) copy-start(f32[4,1,512]{2,1,0:T(1,128)} %constant.31.clone.turn_ref) | copy-start | bytes 24580
  9.8 5.7 %copy-start.8 = (s32[192]{0:T(256)S(1)}, s32[192]{0:T(256)}, u32[]{:S(2)}) copy-start(s32[192]{0:T(256)} %cutoff_ref.7) | copy-start | bytes 2308
  9.8 5.7 %copy-start.9 = (s32[3]{0:T(128)S(1)}, s32[3]{0:T(128)}, u32[]{:S(2)}) copy-start(s32[3]{0:T(128)} %block_ref.7) | copy-start | bytes 40
  12.1 3.3 %collective-permute-start = (f32[3,8,128]{2,1,0:T(8,128)}, f32[3,8,128]{2,1,0:T(8,128)S(1)}, u32[]{:S(2)}, u32[]{:S(2)}) collective-permute-start(f32[3,8,128]{2,1,0:T(8,128)} %get-tuple-element.18), channel_id=1, source_target_pairs={{0,1},{1,2},{2,3},{3,0},{4,5},{5,6},{6,7},{7,4},{8,9},{9,10},{10,1... | collective-permute-start | bytes 36872 | tf_op jit(solution)/shard_map/ppermute | solution.py:703
  12.1 3.4 %collective-permute-start.1 = (f32[3,8,128]{2,1,0:T(8,128)}, f32[3,8,128]{2,1,0:T(8,128)S(1)}, u32[]{:S(2)}, u32[]{:S(2)}) collective-permute-start(f32[3,8,128]{2,1,0:T(8,128)} %get-tuple-element.19), channel_id=1, source_target_pairs={{1,0},{2,1},{3,2},{0,3},{5,4},{6,5},{7,6},{4,7},{9,8},{10,9},{11,1... | collective-permute-start | bytes 36872 | tf_op jit(solution)/shard_map/ppermute | solution.py:704
  15.5 1.1 %copy-start.4 = (bf16[720,512]{1,0:T(8,128)(2,1)S(1)}, bf16[720,512]{1,0:T(8,128)(2,1)}, u32[]{:S(2)}) copy-start(bf16[720,512]{1,0:T(8,128)(2,1)} %constant.28.clone.low_ref) | copy-start | bytes 2211844
  16.6 1.1 %copy-start.5 = (bf16[720,512]{1,0:T(8,128)(2,1)S(1)}, bf16[720,512]{1,0:T(8,128)(2,1)}, u32[]{:S(2)}) copy-start(bf16[720,512]{1,0:T(8,128)(2,1)} %constant.27.clone.high_ref) | copy-start | bytes 2211844
  30.4 10.9 %collective-permute-start.2 = (f32[320,512]{1,0:T(8,128)}, f32[320,512]{1,0:T(8,128)}, u32[]{:S(2)}, u32[]{:S(2)}) collective-permute-start(f32[320,512]{1,0:T(8,128)} %get-tuple-element.23), channel_id=1, source_target_pairs={{0,1},{1,0},{2,3},{3,2},{4,5},{5,4},{6,7},{7,6},{8,9},{9,8},{10,11... | collective-permute-start | bytes 1966088 | tf_op jit(solution)/shard_map/ppermute | solution.py:674
  34.3 0.9 %copy-start.6 = (f32[8,176,128]{2,1,0:T(8,128)}, f32[8,176,128]{2,1,0:T(8,128)S(1)}, u32[]{:S(2)}) copy-start(f32[8,176,128]{2,1,0:T(8,128)S(1)} %get-tuple-element.24) | copy-start | bytes 2162692
  35.1 25.1 %copy-start = (bf16[512,720]{1,0:T(8,128)(2,1)S(1)}, bf16[512,720]{1,0:T(8,128)(2,1)}, u32[]{:S(2)}) copy-start(bf16[512,720]{1,0:T(8,128)(2,1)} %constant.30.clone.low_ref) | copy-start | bytes 2211844
  35.1 25.1 %copy-start.1 = (bf16[512,720]{1,0:T(8,128)(2,1)S(1)}, bf16[512,720]{1,0:T(8,128)(2,1)}, u32[]{:S(2)}) copy-start(bf16[512,720]{1,0:T(8,128)(2,1)} %constant.29.clone.high_ref) | copy-start | bytes 2211844
  35.1 25.0 %all-to-all-start.1 = ((f32[8,176,128]{2,1,0:T(8,128)}), f32[8,176,128]{2,1,0:T(8,128)S(1)}, u32[]{:S(2)}, u32[]{:S(2)}) async-start(f32[8,176,128]{2,1,0:T(8,128)} %copy-done.6), calls=%async_computation.1 | async-start | bytes 1441792 | tf_op jit(solution)/shard_map/all_to_all | solution.py:710
  42.5 16.4 %collective-permute-start.3 = (f32[320,512]{1,0:T(8,128)S(1)}, f32[320,512]{1,0:T(8,128)S(1)}, u32[]{:S(2)}, u32[]{:S(2)}) collective-permute-start(f32[320,512]{1,0:T(8,128)S(1)} %add.27), channel_id=1, source_target_pairs={{0,2},{1,3},{2,0},{3,1},{4,6},{5,7},{6,4},{7,5},{8,10},{9,11},{10,... | collective-permute-start | bytes 1966088 | tf_op jit(solution)/shard_map/ppermute | solution.py:674
  59.0 4.8 %collective-permute-start.4 = (f32[320,512]{1,0:T(8,128)S(1)}, f32[320,512]{1,0:T(8,128)}, u32[]{:S(2)}, u32[]{:S(2)}) collective-permute-start(f32[320,512]{1,0:T(8,128)S(1)} %add.28.mine_ref), channel_id=1, source_target_pairs={{0,1},{1,0},{2,3},{3,2},{4,5},{5,4},{6,7},{7,6},{8,9},{9,8},{10,11... | collective-permute-start | bytes 1966088 | tf_op jit(solution)/shard_map/ppermute | solution.py:674
  61.8 1.5 %collective-permute-start.5 = (f32[80,512]{1,0:T(8,128)S(1)}, f32[80,512]{1,0:T(8,128)S(1)}, u32[]{:S(2)}, u32[]{:S(2)}) collective-permute-start(f32[80,512]{1,0:T(8,128)S(1)} %get-tuple-element.29), channel_id=1, source_target_pairs={{0,1},{1,0},{2,3},{3,2},{4,5},{5,4},{6,7},{7,6},{8,9},{9,8},{10,11... | collective-permute-start | bytes 491528 | tf_op jit(solution)/shard_map/ppermute | solution.py:674
  63.3 6.3 %collective-permute-start.6 = (f32[80,512]{1,0:T(8,128)S(1)}, f32[80,512]{1,0:T(8,128)S(1)}, u32[]{:S(2)}, u32[]{:S(2)}) collective-permute-start(f32[80,512]{1,0:T(8,128)S(1)} %add.29), channel_id=1, source_target_pairs={{0,2},{1,3},{2,0},{3,1},{4,6},{5,7},{6,4},{7,5},{8,10},{9,11},{10,... | collective-permute-start | bytes 491528 | tf_op jit(solution)/shard_map/ppermute | solution.py:674
  69.6 1.5 %collective-permute-start.7 = (f32[80,512]{1,0:T(8,128)S(1)}, f32[80,512]{1,0:T(8,128)S(1)}, u32[]{:S(2)}, u32[]{:S(2)}) collective-permute-start(f32[80,512]{1,0:T(8,128)S(1)} %add_add_fusion.mine_ref), channel_id=1, source_target_pairs={{0,1},{1,0},{2,3},{3,2},{4,5},{5,4},{6,7},{7,6},{8,9},{9,8},{10,11... | collective-permute-start | bytes 491528 | tf_op jit(solution)/shard_map/ppermute | solution.py:674

commit v4 on v3

--- a/solution.py
+++ b/solution.py
@@ -85,6 +85,10 @@
 
 def smem(count):
     return [pl.BlockSpec(memory_space=pltpu.SMEM)] * count
+
+
+def hbm(count):
+    return [pl.BlockSpec(memory_space=pltpu.HBM)] * count
 
 
 def edge_kernel(lane_last, head_ref, tail_ref, wind_ref, west_ref, east_ref):
@@ -188,8 +192,9 @@
     got_ref,
     cutoff_ref,
     later_in_ref,
+    to_ref,
+    later_ref,
     out_ref,
-    later_ref,
     face_ref,
     south_ref,
     half_ref,
@@ -197,9 +202,13 @@
     table_ref,
     slot_ref,
     sem,
+    out_sem,
 ):
     del later_in_ref, later_ref
     parts = got_ref.shape[0]
+    outgoing = [
+        pltpu.make_async_copy(out_ref.at[d], to_ref.at[d], out_sem.at[d]) for d in range(parts)
+    ]
     slots = face_ref.shape[0] // parts
     count = parts * slots
     whole_ref[...] = got_ref[:, 184:192, :].astype(jnp.int32)
@@ -259,6 +268,9 @@
             tail = jnp.where(lane < TAIL, tails[q], rest_tail)
             out_ref[d, 150 + 5 * q : 155 + 5 * q] = tail[1:6]
         out_ref[d, 170:BACK] = jnp.zeros((BACK - 170, LANES), F32)
+        outgoing[d].start()
+    for part in outgoing:
+        part.wait()
 
 
 def faces_of_pieces(got, slots, cutoff, later):
@@ -266,13 +278,14 @@
     return pl.pallas_call(
         face_kernel,
         in_specs=vmem(1) + smem(1) + [pl.BlockSpec(memory_space=pl.ANY)],
-        out_specs=vmem(1) + [pl.BlockSpec(memory_space=pl.ANY)],
+        out_specs=hbm(1) + [pl.BlockSpec(memory_space=pl.ANY)],
         out_shape=[
             jax.ShapeDtypeStruct((parts, BACK, LANES), F32),
             jax.ShapeDtypeStruct(later.shape, F32),
         ],
         input_output_aliases={2: 1},
         scratch_shapes=[
+            pltpu.VMEM((parts, BACK, LANES), F32),
             pltpu.VMEM((parts * slots, 32, LANES), F32),
             pltpu.VMEM((parts * slots, 32, LANES), F32),
             pltpu.VMEM((parts * slots, 8, LANES), F32),
@@ -280,6 +293,7 @@
             pltpu.SMEM((parts, 8, LANES), jnp.int32),
             pltpu.SMEM((parts * slots + 2,), jnp.int32),
             pltpu.SemaphoreType.DMA(()),
+            pltpu.SemaphoreType.DMA((parts,)),
         ],
         compiler_params=pltpu.CompilerParams(vmem_limit_bytes=16 * MIB),
         cost_estimate=pl.CostEstimate(flops=10**5, bytes_accessed=1600000, transcendentals=0),
@@ -335,13 +349,13 @@
 
 
 def tendency_kernel(
-    state_ref,
-    cx_ref,
-    cy_ref,
+    far_state_ref,
+    far_cx_ref,
+    far_cy_ref,
+    far_high_ref,
+    far_low_ref,
     west_ref,
     east_ref,
-    high_ref,
-    low_ref,
     turn_ref,
     place_ref,
     block_ref,
@@ -349,16 +363,38 @@
     out_ref,
     mine_ref,
     other_ref,
+    state_ref,
+    cx_ref,
+    cy_ref,
+    high_ref,
+    low_ref,
     tend_ref,
     base_ref,
     sem,
+    in_sem,
+    table_sem,
 ):
     fields, slots, rows, levels, width = state_ref.shape
 
     def streamed(s):
         return pltpu.make_async_copy(base_ref.at[:, s], out_ref.at[:, s], sem.at[s])
 
-
+    def incoming(s):
+        return (
+            pltpu.make_async_copy(far_state_ref.at[:, s], state_ref.at[:, s], in_sem.at[s, 0]),
+            pltpu.make_async_copy(far_cx_ref.at[s], cx_ref.at[s], in_sem.at[s, 1]),
+            pltpu.make_async_copy(far_cy_ref.at[s], cy_ref.at[s], in_sem.at[s, 2]),
+        )
+
+    tables = (
+        pltpu.make_async_copy(far_high_ref, high_ref, table_sem.at[0]),
+        pltpu.make_async_copy(far_low_ref, low_ref, table_sem.at[1]),
+    )
+    for s in range(slots):
+        for copy in incoming(s):
+            copy.start()
+    for copy in tables:
+        copy.start()
     tiles = -(-width // LANES)
     lane = lax.broadcasted_iota(jnp.int32, (levels, LANES), 1)
     head, tail, last = lane == 0, lane == LANES - 1, lane == (width - 1) % LANES
@@ -374,6 +410,8 @@
         return out
 
     def one_slot(s, carry):
+        for copy in incoming(s):
+            copy.wait()
         west, east = west_ref[s], east_ref[s]
         for f in range(fields):
             above = None
@@ -411,6 +449,8 @@
         return carry
 
     lax.fori_loop(0, slots, one_slot, 0)
+    for copy in tables:
+        copy.wait()
     turn = turn_ref[place_ref[0]]
     first, second, _ = pick_slots(block_ref, cutoff_ref, rows)
     mine, other = mine_first((first, second), place_ref[1])
@@ -429,20 +469,27 @@
     spec = jax.ShapeDtypeStruct((count, 2 * KCUT), F32)
     return pl.pallas_call(
         tendency_kernel,
-        in_specs=vmem(8) + smem(3),
+        in_specs=hbm(5) + vmem(3) + smem(3),
         out_specs=[pl.BlockSpec(memory_space=pl.ANY)] + vmem(2),
         out_shape=[jax.ShapeDtypeStruct(state.shape, F32), spec, spec],
         scratch_shapes=[
             pltpu.VMEM(state.shape, F32),
+            pltpu.VMEM(courant_x.shape, F32),
+            pltpu.VMEM(courant_y.shape, F32),
+            pltpu.VMEM(forward[0].shape, BF16),
+            pltpu.VMEM(forward[1].shape, BF16),
+            pltpu.VMEM(state.shape, F32),
             pltpu.VMEM(state.shape, F32),
             pltpu.SemaphoreType.DMA((slots,)),
+            pltpu.SemaphoreType.DMA((slots, 3)),
+            pltpu.SemaphoreType.DMA((2,)),
         ],
         compiler_params=pltpu.CompilerParams(vmem_limit_bytes=50 * MIB),
         cost_estimate=pl.CostEstimate(
             flops=6 * count * 2 * KCUT * width * 2, bytes_accessed=9 * 10**6, transcendentals=0
         ),
         name="tendency",
-    )(state, courant_x, courant_y, west, east, *forward, turn, place, block, cutoff)
+    )(state, courant_x, courant_y, *forward, west, east, turn, place, block, cutoff)
 
 
 def chosen_slot(i, place_ref, block_ref, cutoff_ref, rows):

time: 74.1 us -> 76.5 us (1.032)
  Pallas kernels: 28.8 us -> 31.2 us
    pallas_call x1, Pallas kernels: 1.95 us -> 3.42 us  [faces_of_pieces(): pl.pallas_call(face_kernel, in_specs=vmem(1) + smem(1) + [pl.BlockSpec(me...]
    pallas_call x1, Pallas kernels: 12.6 us -> 13.5 us  [local_tendency(): pl.pallas_call(tendency_kernel, in_specs=hbm(5) + vmem(3) + smem(3), out_...]
  transfers between devices with their start and end apart: 10 -> 10, of which waited for: 6 -> 6; matrix products, arithmetic and copies ran while one was open for 2% -> 2% of each run, Pallas kernels for 32% -> 34%
where the time goes in v4:
time: 76.5 us; the launch traced here: 76 us
  Pallas kernels  31.2 us (41%)
  waiting for transfers between devices  21.6 us (28%)
  starting transfers between devices  18.5 us (24%)
  local copies, waits for them, and re-layouts  3.13 us (4%)
  other arithmetic  1.45 us (2%)
    ppermute x6, waiting for transfers between devices, swap(): return lax.ppermute(array, 'lon', [(i, i ^ bit) for i in range(size)])  19 us
    pallas_call x1, Pallas kernels, local_tendency(): pl.pallas_call(tendency_kernel, in_specs=hbm(5) + vmem(3) + smem(3), out_...  13.5 us
    all_to_all x1, starting transfers between devices, shards(): got = lax.all_to_all(sent, 'lat', 0, 0, tiled=True)  7.28 us
    all_to_all x1, starting transfers between devices, shards(): back = lax.all_to_all(back, 'lat', 0, 0, tiled=True)  6.12 us
    pallas_call x1, Pallas kernels, main_part(): pl.pallas_call(main_kernel, grid_spec=pltpu.PrefetchScalarGridSpec(num_sc...  5.35 us
    pallas_call x1, Pallas kernels, faces_of_pieces(): pl.pallas_call(face_kernel, in_specs=vmem(1) + smem(1) + [pl.BlockSpec(me...  3.42 us
    ppermute x6, starting transfers between devices, swap(): return lax.ppermute(array, 'lon', [(i, i ^ bit) for i in range(size)])  3.35 us
    unnamed x20, local copies, waits for them, and re-layouts  3.13 us
  transfers between devices with their start and end apart: 10, of which 6 were waited for; matrix products, arithmetic and copies ran while one was open for 2% of the time, Pallas kernels for 34%

profile of v4, /device:TPU:0, one launch (start us, length us, event | category | flops | bytes accessed | tf_op | source)
XLA Modules:
  0.0 76.0 jit_solution(1799652786661871409)
XLA Ops:
  0.0 2.5 %pack.1 = f32[1536,128]{1,0:T(8,128)} custom-call(f32[5,3,8,8,720]{4,3,2,1,0:T(8,128)} %state_ref.1, f32[5,3,8,8,720]{4,3,2,1,0:T(8,128)} %state_ref.1, f32[3,8,8,720]{3,2,1,0:T(8,128)} %wind_ref.3, s32[3]{0:T(128)} %block_ref.7), custom_call_target="tpu_custom_call" | custom-call | flops 100000 | bytes 1700000 | tf_op jit(solution)/shard_map/pack/pallas_call | solution.py:175
  2.5 7.3 %all-to-all-start = ((f32[8,192,128]{2,1,0:T(8,128)}), f32[8,192,128]{2,1,0:T(8,128)S(1)}, u32[]{:S(2)}, u32[]{:S(2)}) async-start(f32[8,192,128]{2,1,0:T(8,128)} %bitcast.8), calls=%async_computation | async-start | bytes 1572864 | tf_op jit(solution)/shard_map/all_to_all | solution.py:747
  9.8 0.0 copy-start.3
  9.8 0.0 copy-start.7
  9.8 2.3 %edges.1 = (f32[3,8,128]{2,1,0:T(8,128)}, f32[3,8,128]{2,1,0:T(8,128)}) custom-call(f32[5,3,8,8,720]{4,3,2,1,0:T(8,128)} %state_ref.1, f32[5,3,8,8,720]{4,3,2,1,0:T(8,128)} %state_ref.1, f32[3,8,8,720]{3,2,1,0:T(8,128)} %far_cx_ref.1), custom_call_target="tpu_custom_call" | custom-call | flops 100000 | bytes 1200000 | tf_op jit(solution)/shard_map/edges/pallas_call | solution.py:115
  12.1 1.7 %collective-permute-start.1 = (f32[3,8,128]{2,1,0:T(8,128)}, f32[3,8,128]{2,1,0:T(8,128)S(1)}, u32[]{:S(2)}, u32[]{:S(2)}) collective-permute-start(f32[3,8,128]{2,1,0:T(8,128)} %get-tuple-element.19), channel_id=1, source_target_pairs={{1,0},{2,1},{3,2},{0,3},{5,4},{6,5},{7,6},{4,7},{9,8},{10,9},{11,1... | collective-permute-start | bytes 36872 | tf_op jit(solution)/shard_map/ppermute | solution.py:751
  13.9 0.1 pad_add_fusion.place_ref
  14.0 1.5 %collective-permute-done.west_ref = f32[3,8,128]{2,1,0:T(8,128)S(1)} collective-permute-done((f32[3,8,128]{2,1,0:T(8,128)}, f32[3,8,128]{2,1,0:T(8,128)S(1)}, u32[]{:S(2)}, u32[]{:S(2)}) %collective-permute-start) | collective-permute-done | bytes 12320 | tf_op jit(solution)/shard_map/ppermute | solution.py:750
  15.5 0.0 collective-permute-done.1.east_ref
  15.5 0.0 copy-start.4
  15.5 1.1 %copy-done.4 = bf16[720,512]{1,0:T(8,128)(2,1)S(1)} copy-done((bf16[720,512]{1,0:T(8,128)(2,1)S(1)}, bf16[720,512]{1,0:T(8,128)(2,1)}, u32[]{:S(2)}) %copy-start.4) | copy-done | bytes 737304
  16.6 1.1 %copy-done.5 = bf16[720,512]{1,0:T(8,128)(2,1)S(1)} copy-done((bf16[720,512]{1,0:T(8,128)(2,1)S(1)}, bf16[720,512]{1,0:T(8,128)(2,1)}, u32[]{:S(2)}) %copy-start.5) | copy-done | bytes 737304
  17.8 13.5 %tendency.1 = (f32[5,3,8,8,720]{4,3,2,1,0:T(8,128)}, f32[320,512]{1,0:T(8,128)S(1)}, f32[320,512]{1,0:T(8,128)}) custom-call(f32[5,3,8,8,720]{4,3,2,1,0:T(8,128)} %state_ref.1, f32[3,8,8,720]{3,2,1,0:T(8,128)S(1)} %copy-done.3, f32[3,8,8,720]{3,2,1,0:T(8,128)S(1)} %copy-done.2, bf16[720,512]{1,0:T(8,128)(2,1)S(1)} %copy-done.5, ...), custom_call_target="tpu_custom_call" | custom-call | flops 1415577600 | bytes 9000000 | tf_op jit(solution)/shard_map/tendency/pallas_call | solution.py:470
  31.3 1.9 %collective-permute-start.2 = (f32[320,512]{1,0:T(8,128)}, f32[320,512]{1,0:T(8,128)}, u32[]{:S(2)}, u32[]{:S(2)}) collective-permute-start(f32[320,512]{1,0:T(8,128)} %get-tuple-element.23), channel_id=1, source_target_pairs={{0,1},{1,0},{2,3},{3,2},{4,5},{5,4},{6,7},{7,6},{8,9},{9,8},{10,11... | collective-permute-start | bytes 1966088 | tf_op jit(solution)/shard_map/ppermute | solution.py:721
  33.2 3.4 %faces.1 = (f32[8,176,128]{2,1,0:T(8,128)S(1)}, f32[320,512]{1,0:T(8,128)S(1)}) custom-call(f32[8,192,128]{2,1,0:T(8,128)S(1)} %all-to-all-done.got_ref, s32[192]{0:T(256)S(1)} %copy-done.8, f32[320,512]{1,0:T(8,128)S(1)} %get-tuple-element.21.later_in_ref), custom_call_target="tpu_custom_call", output_to_operand_aliasing={{1}: (2, {})} | custom-call | flops 100000 | bytes 1600000 | tf_op jit(solution)/shard_map/faces/pallas_call | solution.py:278
  36.7 0.9 %copy-done.6 = f32[8,176,128]{2,1,0:T(8,128)} copy-done((f32[8,176,128]{2,1,0:T(8,128)}, f32[8,176,128]{2,1,0:T(8,128)S(1)}, u32[]{:S(2)}) %copy-start.6) | copy-done | bytes 720920
  37.6 6.1 %all-to-all-start.1 = ((f32[8,176,128]{2,1,0:T(8,128)}), f32[8,176,128]{2,1,0:T(8,128)S(1)}, u32[]{:S(2)}, u32[]{:S(2)}) async-start(f32[8,176,128]{2,1,0:T(8,128)} %copy-done.6), calls=%async_computation.1 | async-start | bytes 1441792 | tf_op jit(solution)/shard_map/all_to_all | solution.py:757
  43.7 1.2 %add.27 = f32[320,512]{1,0:T(8,128)S(1)} add(f32[320,512]{1,0:T(8,128)S(1)} %get-tuple-element.22, f32[320,512]{1,0:T(8,128)} %collective-permute-done.2) | non-fusion elementwise | flops 163840 | bytes 1966080 | tf_op jit(solution)/shard_map/add | solution.py:725
  44.9 0.6 collective-permute-start.3
  45.5 15.8 %collective-permute-done.3 = f32[320,512]{1,0:T(8,128)S(1)} collective-permute-done((f32[320,512]{1,0:T(8,128)S(1)}, f32[320,512]{1,0:T(8,128)S(1)}, u32[]{:S(2)}, u32[]{:S(2)}) %collective-permute-start.3) | collective-permute-done | bytes 655392 | tf_op jit(solution)/shard_map/ppermute | solution.py:721
  61.3 0.1 add.28.mine_ref
  61.5 0.1 collective-permute-start.4
  61.5 1.1 %all-to-all-done.1 = f32[8,176,128]{2,1,0:T(8,128)S(1)} async-done(((f32[8,176,128]{2,1,0:T(8,128)}), f32[8,176,128]{2,1,0:T(8,128)S(1)}, u32[]{:S(2)}, u32[]{:S(2)}) %all-to-all-start.1) | async-done | bytes 720928 | tf_op jit(solution)/shard_map/all_to_all | solution.py:757
  62.6 1.6 %rim_spectra.1 = (f32[2,2,5,8,720]{4,3,2,1,0:T(8,128)S(1)}, f32[80,512]{1,0:T(8,128)S(1)}, f32[80,512]{1,0:T(8,128)S(1)}, f32[8,128]{1,0:T(8,128)S(1)}) custom-call(f32[1408,128]{1,0:T(8,128)S(1)} %bitcast.5, bf16[512,720]{1,0:T(8,128)(2,1)S(1)} %copy-done.1, bf16[512,720]{1,0:T(8,128)(2,1)S(1)} %copy-done, f32[4,1,512]{2,1,0:T(1,128)S(1)} %copy-done.7, ...), custom_call_target="tpu_custom_call" | custom-call | flops 353894400 | bytes 3000000 | tf_op jit(solution)/shard_map/rim_spectra/pallas_call | solution.py:620
  64.2 0.1 collective-permute-start.5
  64.3 1.4 %collective-permute-done.5 = f32[80,512]{1,0:T(8,128)S(1)} collective-permute-done((f32[80,512]{1,0:T(8,128)S(1)}, f32[80,512]{1,0:T(8,128)S(1)}, u32[]{:S(2)}, u32[]{:S(2)}) %collective-permute-start.5) | collective-permute-done | bytes 163872 | tf_op jit(solution)/shard_map/ppermute | solution.py:721
  65.7 0.6 collective-permute-start.6
  66.3 5.3 %main.1 = (f32[5,3,8,8,720]{4,3,2,1,0:T(8,128)}, f32[1,512]{1,0:T(1,128)S(1)}) custom-call(s32[2]{0:T(128)S(1)} %pad_add_fusion.place_ref, s32[3]{0:T(128)S(1)} %copy-done.9, s32[192]{0:T(256)S(1)} %copy-done.8, f32[5,3,8,8,720]{4,3,2,1,0:T(8,128)} %state_ref.1, f32[5,3,8,8,720]{4,3,2,1,0:T(8,128)} %get-tuple-element.20.base_ref, ...), custom_call_target="tpu_custom_call", output_to_operand_aliasing={{0}: (4, {})} | custom-call | flops 1415577600 | bytes 6000000 | tf_op jit(solution)/shard_map/main/pallas_call | solution.py:542
  71.6 0.4 collective-permute-done.6
  72.0 0.1 collective-permute-start.7
  72.1 1.4 %collective-permute-done.7.away_ref = f32[80,512]{1,0:T(8,128)S(1)} collective-permute-done((f32[80,512]{1,0:T(8,128)S(1)}, f32[80,512]{1,0:T(8,128)S(1)}, u32[]{:S(2)}, u32[]{:S(2)}) %collective-permute-start.7) | collective-permute-done | bytes 163872 | tf_op jit(solution)/shard_map/ppermute | solution.py:721
  73.5 2.6 %final.1 = f32[5,3,8,8,720]{4,3,2,1,0:T(8,128)} custom-call(f32[5,3,8,8,720]{4,3,2,1,0:T(8,128)} %get-tuple-element.26.main_ref, f32[2,2,5,8,720]{4,3,2,1,0:T(8,128)S(1)} %get-tuple-element.27.pair_ref, f32[1408,128]{1,0:T(8,128)S(1)} %bitcast.6, f32[80,512]{1,0:T(8,128)S(1)} %add_add_fusion.mine_ref, ...), custom_call_target="tpu_custom_call", output_to_operand_aliasing={{}: (0, {})} | custom-call | flops 353894400 | bytes 4000000 | tf_op jit(solution)/shard_map/final/pallas_call | solution.py:701
  (20 shorter events, 0.1 us)
Async XLA Ops:
  2.5 30.8 %all-to-all-start = ((f32[8,192,128]{2,1,0:T(8,128)}), f32[8,192,128]{2,1,0:T(8,128)S(1)}, u32[]{:S(2)}, u32[]{:S(2)}) async-start(f32[8,192,128]{2,1,0:T(8,128)} %bitcast.8), calls=%async_computation | async-start | bytes 1572864 | tf_op jit(solution)/shard_map/all_to_all | solution.py:747
  9.8 5.7 %copy-start.2 = (f32[3,8,8,720]{3,2,1,0:T(8,128)S(1)}, f32[3,8,8,720]{3,2,1,0:T(8,128)}, u32[]{:S(2)}) copy-start(f32[3,8,8,720]{3,2,1,0:T(8,128)} %wind_ref.3) | copy-start | bytes 1658884
  9.8 5.7 %copy-start.3 = (f32[3,8,8,720]{3,2,1,0:T(8,128)S(1)}, f32[3,8,8,720]{3,2,1,0:T(8,128)}, u32[]{:S(2)}) copy-start(f32[3,8,8,720]{3,2,1,0:T(8,128)} %far_cx_ref.1) | copy-start | bytes 1658884
  9.8 5.7 %copy-start.7 = (f32[4,1,512]{2,1,0:T(1,128)S(1)}, f32[4,1,512]{2,1,0:T(1,128)}, u32[]{:S(2)}) copy-start(f32[4,1,512]{2,1,0:T(1,128)} %constant.31.clone.turn_ref) | copy-start | bytes 24580
  9.8 5.7 %copy-start.8 = (s32[192]{0:T(256)S(1)}, s32[192]{0:T(256)}, u32[]{:S(2)}) copy-start(s32[192]{0:T(256)} %cutoff_ref.7) | copy-start | bytes 2308
  9.8 5.7 %copy-start.9 = (s32[3]{0:T(128)S(1)}, s32[3]{0:T(128)}, u32[]{:S(2)}) copy-start(s32[3]{0:T(128)} %block_ref.7) | copy-start | bytes 40
  12.1 3.3 %collective-permute-start = (f32[3,8,128]{2,1,0:T(8,128)}, f32[3,8,128]{2,1,0:T(8,128)S(1)}, u32[]{:S(2)}, u32[]{:S(2)}) collective-permute-start(f32[3,8,128]{2,1,0:T(8,128)} %get-tuple-element.18), channel_id=1, source_target_pairs={{0,1},{1,2},{2,3},{3,0},{4,5},{5,6},{6,7},{7,4},{8,9},{9,10},{10,1... | collective-permute-start | bytes 36872 | tf_op jit(solution)/shard_map/ppermute | solution.py:750
  12.1 3.4 %collective-permute-start.1 = (f32[3,8,128]{2,1,0:T(8,128)}, f32[3,8,128]{2,1,0:T(8,128)S(1)}, u32[]{:S(2)}, u32[]{:S(2)}) collective-permute-start(f32[3,8,128]{2,1,0:T(8,128)} %get-tuple-element.19), channel_id=1, source_target_pairs={{1,0},{2,1},{3,2},{0,3},{5,4},{6,5},{7,6},{4,7},{9,8},{10,9},{11,1... | collective-permute-start | bytes 36872 | tf_op jit(solution)/shard_map/ppermute | solution.py:751
  15.5 1.1 %copy-start.4 = (bf16[720,512]{1,0:T(8,128)(2,1)S(1)}, bf16[720,512]{1,0:T(8,128)(2,1)}, u32[]{:S(2)}) copy-start(bf16[720,512]{1,0:T(8,128)(2,1)} %constant.28.clone.far_low_ref) | copy-start | bytes 2211844
  16.6 1.1 %copy-start.5 = (bf16[720,512]{1,0:T(8,128)(2,1)S(1)}, bf16[720,512]{1,0:T(8,128)(2,1)}, u32[]{:S(2)}) copy-start(bf16[720,512]{1,0:T(8,128)(2,1)} %constant.27.clone.far_high_ref) | copy-start | bytes 2211844
  31.3 12.4 %collective-permute-start.2 = (f32[320,512]{1,0:T(8,128)}, f32[320,512]{1,0:T(8,128)}, u32[]{:S(2)}, u32[]{:S(2)}) collective-permute-start(f32[320,512]{1,0:T(8,128)} %get-tuple-element.23), channel_id=1, source_target_pairs={{0,1},{1,0},{2,3},{3,2},{4,5},{5,4},{6,7},{7,6},{8,9},{9,8},{10,11... | collective-permute-start | bytes 1966088 | tf_op jit(solution)/shard_map/ppermute | solution.py:721
  36.7 0.9 %copy-start.6 = (f32[8,176,128]{2,1,0:T(8,128)}, f32[8,176,128]{2,1,0:T(8,128)S(1)}, u32[]{:S(2)}) copy-start(f32[8,176,128]{2,1,0:T(8,128)S(1)} %get-tuple-element.24) | copy-start | bytes 2162692
  37.5 25.1 %copy-start = (bf16[512,720]{1,0:T(8,128)(2,1)S(1)}, bf16[512,720]{1,0:T(8,128)(2,1)}, u32[]{:S(2)}) copy-start(bf16[512,720]{1,0:T(8,128)(2,1)} %constant.30.clone.low_ref) | copy-start | bytes 2211844
  37.5 25.1 %copy-start.1 = (bf16[512,720]{1,0:T(8,128)(2,1)S(1)}, bf16[512,720]{1,0:T(8,128)(2,1)}, u32[]{:S(2)}) copy-start(bf16[512,720]{1,0:T(8,128)(2,1)} %constant.29.clone.high_ref) | copy-start | bytes 2211844
  37.6 25.0 %all-to-all-start.1 = ((f32[8,176,128]{2,1,0:T(8,128)}), f32[8,176,128]{2,1,0:T(8,128)S(1)}, u32[]{:S(2)}, u32[]{:S(2)}) async-start(f32[8,176,128]{2,1,0:T(8,128)} %copy-done.6), calls=%async_computation.1 | async-start | bytes 1441792 | tf_op jit(solution)/shard_map/all_to_all | solution.py:757
  44.9 16.4 %collective-permute-start.3 = (f32[320,512]{1,0:T(8,128)S(1)}, f32[320,512]{1,0:T(8,128)S(1)}, u32[]{:S(2)}, u32[]{:S(2)}) collective-permute-start(f32[320,512]{1,0:T(8,128)S(1)} %add.27), channel_id=1, source_target_pairs={{0,2},{1,3},{2,0},{3,1},{4,6},{5,7},{6,4},{7,5},{8,10},{9,11},{10,... | collective-permute-start | bytes 1966088 | tf_op jit(solution)/shard_map/ppermute | solution.py:721
  61.5 4.8 %collective-permute-start.4 = (f32[320,512]{1,0:T(8,128)S(1)}, f32[320,512]{1,0:T(8,128)}, u32[]{:S(2)}, u32[]{:S(2)}) collective-permute-start(f32[320,512]{1,0:T(8,128)S(1)} %add.28.mine_ref), channel_id=1, source_target_pairs={{0,1},{1,0},{2,3},{3,2},{4,5},{5,4},{6,7},{7,6},{8,9},{9,8},{10,11... | collective-permute-start | bytes 1966088 | tf_op jit(solution)/shard_map/ppermute | solution.py:721
  64.2 1.5 %collective-permute-start.5 = (f32[80,512]{1,0:T(8,128)S(1)}, f32[80,512]{1,0:T(8,128)S(1)}, u32[]{:S(2)}, u32[]{:S(2)}) collective-permute-start(f32[80,512]{1,0:T(8,128)S(1)} %get-tuple-element.29), channel_id=1, source_target_pairs={{0,1},{1,0},{2,3},{3,2},{4,5},{5,4},{6,7},{7,6},{8,9},{9,8},{10,11... | collective-permute-start | bytes 491528 | tf_op jit(solution)/shard_map/ppermute | solution.py:721
  65.7 6.3 %collective-permute-start.6 = (f32[80,512]{1,0:T(8,128)S(1)}, f32[80,512]{1,0:T(8,128)S(1)}, u32[]{:S(2)}, u32[]{:S(2)}) collective-permute-start(f32[80,512]{1,0:T(8,128)S(1)} %add.29), channel_id=1, source_target_pairs={{0,2},{1,3},{2,0},{3,1},{4,6},{5,7},{6,4},{7,5},{8,10},{9,11},{10,... | collective-permute-start | bytes 491528 | tf_op jit(solution)/shard_map/ppermute | solution.py:721
  72.0 1.5 %collective-permute-start.7 = (f32[80,512]{1,0:T(8,128)S(1)}, f32[80,512]{1,0:T(8,128)S(1)}, u32[]{:S(2)}, u32[]{:S(2)}) collective-permute-start(f32[80,512]{1,0:T(8,128)S(1)} %add_add_fusion.mine_ref), channel_id=1, source_target_pairs={{0,1},{1,0},{2,3},{3,2},{4,5},{5,4},{6,7},{7,6},{8,9},{9,8},{10,11... | collective-permute-start | bytes 491528 | tf_op jit(solution)/shard_map/ppermute | solution.py:721

commit v5 on v3

--- a/solution.py
+++ b/solution.py
@@ -437,7 +437,7 @@
             pltpu.VMEM(state.shape, F32),
             pltpu.SemaphoreType.DMA((slots,)),
         ],
-        compiler_params=pltpu.CompilerParams(vmem_limit_bytes=50 * MIB),
+        compiler_params=pltpu.CompilerParams(vmem_limit_bytes=60 * MIB),
         cost_estimate=pl.CostEstimate(
             flops=6 * count * 2 * KCUT * width * 2, bytes_accessed=9 * 10**6, transcendentals=0
         ),

time: 74.1 us -> 75.2 us (1.015)
  Pallas kernels: 28.8 us -> 30.7 us
    pallas_call x1, Pallas kernels: 12.6 us -> 13.6 us  [local_tendency(): pl.pallas_call(tendency_kernel, in_specs=vmem(8) + smem(3), out_specs=[pl...]
    pallas_call x1, Pallas kernels: 1.95 us -> 2.82 us  [faces_of_pieces(): pl.pallas_call(face_kernel, in_specs=vmem(1) + smem(1) + [pl.BlockSpec(me...]
  transfers between devices with their start and end apart: 10 -> 10, of which waited for: 6 -> 6; matrix products, arithmetic and copies ran while one was open for 2% -> 3% of each run, Pallas kernels for 32% -> 34%
where the time goes in v5:
time: 75.2 us; the launch traced here: 74.8 us
  Pallas kernels  30.7 us (41%)
  waiting for transfers between devices  20.9 us (28%)
  starting transfers between devices  18.1 us (24%)
  local copies, waits for them, and re-layouts  3.1 us (4%)
  other arithmetic  1.98 us (3%)
    ppermute x6, waiting for transfers between devices, swap(): return lax.ppermute(array, 'lon', [(i, i ^ bit) for i in range(size)])  18.8 us
    pallas_call x1, Pallas kernels, local_tendency(): pl.pallas_call(tendency_kernel, in_specs=vmem(8) + smem(3), out_specs=[pl...  13.6 us
    all_to_all x1, starting transfers between devices, shards(): got = lax.all_to_all(sent, 'lat', 0, 0, tiled=True)  7.28 us
    all_to_all x1, starting transfers between devices, shards(): back = lax.all_to_all(back, 'lat', 0, 0, tiled=True)  6.14 us
    pallas_call x1, Pallas kernels, main_part(): pl.pallas_call(main_kernel, grid_spec=pltpu.PrefetchScalarGridSpec(num_sc...  5.41 us
    unnamed x20, local copies, waits for them, and re-layouts  3.1 us
    ppermute x6, starting transfers between devices, swap(): return lax.ppermute(array, 'lon', [(i, i ^ bit) for i in range(size)])  2.9 us
    pallas_call x1, Pallas kernels, faces_of_pieces(): pl.pallas_call(face_kernel, in_specs=vmem(1) + smem(1) + [pl.BlockSpec(me...  2.82 us
  transfers between devices with their start and end apart: 10, of which 6 were waited for; matrix products, arithmetic and copies ran while one was open for 3% of the time, Pallas kernels for 34%

profile of v5, /device:TPU:0, one launch (start us, length us, event | category | flops | bytes accessed | tf_op | source)
XLA Modules:
  0.0 74.8 jit_solution(710257278556942362)
XLA Ops:
  0.0 2.5 %pack.1 = f32[1536,128]{1,0:T(8,128)} custom-call(f32[5,3,8,8,720]{4,3,2,1,0:T(8,128)} %state_ref.3, f32[5,3,8,8,720]{4,3,2,1,0:T(8,128)} %state_ref.3, f32[3,8,8,720]{3,2,1,0:T(8,128)} %wind_ref.3, s32[3]{0:T(128)} %block_ref.7), custom_call_target="tpu_custom_call" | custom-call | flops 100000 | bytes 1700000 | tf_op jit(solution)/shard_map/pack/pallas_call | solution.py:171
  2.5 7.3 %all-to-all-start = ((f32[8,192,128]{2,1,0:T(8,128)}), f32[8,192,128]{2,1,0:T(8,128)S(1)}, u32[]{:S(2)}, u32[]{:S(2)}) async-start(f32[8,192,128]{2,1,0:T(8,128)} %bitcast.8), calls=%async_computation | async-start | bytes 1572864 | tf_op jit(solution)/shard_map/all_to_all | solution.py:700
  9.8 2.2 %edges.1 = (f32[3,8,128]{2,1,0:T(8,128)}, f32[3,8,128]{2,1,0:T(8,128)}) custom-call(f32[5,3,8,8,720]{4,3,2,1,0:T(8,128)} %state_ref.3, f32[5,3,8,8,720]{4,3,2,1,0:T(8,128)} %state_ref.3, f32[3,8,8,720]{3,2,1,0:T(8,128)} %cx_ref.1), custom_call_target="tpu_custom_call" | custom-call | flops 100000 | bytes 1200000 | tf_op jit(solution)/shard_map/edges/pallas_call | solution.py:111
  12.0 0.0 collective-permute-start
  12.0 1.7 %collective-permute-start.1 = (f32[3,8,128]{2,1,0:T(8,128)}, f32[3,8,128]{2,1,0:T(8,128)S(1)}, u32[]{:S(2)}, u32[]{:S(2)}) collective-permute-start(f32[3,8,128]{2,1,0:T(8,128)} %get-tuple-element.19), channel_id=1, source_target_pairs={{1,0},{2,1},{3,2},{0,3},{5,4},{6,5},{7,6},{4,7},{9,8},{10,9},{11,1... | collective-permute-start | bytes 36872 | tf_op jit(solution)/shard_map/ppermute | solution.py:704
  13.7 0.6 pad_add_fusion.place_ref
  14.3 1.0 %collective-permute-done.west_ref = f32[3,8,128]{2,1,0:T(8,128)S(1)} collective-permute-done((f32[3,8,128]{2,1,0:T(8,128)}, f32[3,8,128]{2,1,0:T(8,128)S(1)}, u32[]{:S(2)}, u32[]{:S(2)}) %collective-permute-start) | collective-permute-done | bytes 12320 | tf_op jit(solution)/shard_map/ppermute | solution.py:703
  15.3 0.0 collective-permute-done.1.east_ref
  15.4 0.6 copy-done.8
  15.9 0.6 copy-done.9
  16.5 13.6 %tendency.1 = (f32[5,3,8,8,720]{4,3,2,1,0:T(8,128)}, f32[320,512]{1,0:T(8,128)}, f32[320,512]{1,0:T(8,128)}) custom-call(f32[5,3,8,8,720]{4,3,2,1,0:T(8,128)} %state_ref.3, f32[3,8,8,720]{3,2,1,0:T(8,128)} %cx_ref.1, f32[3,8,8,720]{3,2,1,0:T(8,128)} %wind_ref.3, f32[3,8,128]{2,1,0:T(8,128)} %copy-done.8, f32[3,8,128]{2,1,0:T(8,128)} %copy-done.9, ...), custom_call_target="tpu_custom_call" | custom-call | flops 1415577600 | bytes 9000000 | tf_op jit(solution)/shard_map/tendency/pallas_call | solution.py:430
  30.1 1.4 %collective-permute-start.2 = (f32[320,512]{1,0:T(8,128)}, f32[320,512]{1,0:T(8,128)S(1)}, u32[]{:S(2)}, u32[]{:S(2)}) collective-permute-start(f32[320,512]{1,0:T(8,128)} %get-tuple-element.23), channel_id=1, source_target_pairs={{0,1},{1,0},{2,3},{3,2},{4,5},{5,4},{6,7},{7,6},{8,9},{9,8},{10,11... | collective-permute-start | bytes 1966088 | tf_op jit(solution)/shard_map/ppermute | solution.py:674
  31.5 1.1 %copy-done.2 = f32[320,512]{1,0:T(8,128)S(1)} copy-done((f32[320,512]{1,0:T(8,128)S(1)}, f32[320,512]{1,0:T(8,128)}, u32[]{:S(2)}) %copy-start.2) | copy-done | bytes 655384
  32.6 2.8 %faces.1 = (f32[8,176,128]{2,1,0:T(8,128)}, f32[320,512]{1,0:T(8,128)S(1)}) custom-call(f32[8,192,128]{2,1,0:T(8,128)S(1)} %all-to-all-done.got_ref, s32[192]{0:T(256)S(1)} %copy-done.5, f32[320,512]{1,0:T(8,128)S(1)} %copy-done.2), custom_call_target="tpu_custom_call", output_to_operand_aliasing={{1}: (2, {})} | custom-call | flops 100000 | bytes 1600000 | tf_op jit(solution)/shard_map/faces/pallas_call | solution.py:266
  35.5 0.8 %copy-done.3 = f32[320,512]{1,0:T(8,128)} copy-done((f32[320,512]{1,0:T(8,128)}, f32[320,512]{1,0:T(8,128)S(1)}, u32[]{:S(2)}) %copy-start.3) | copy-done | bytes 655384
  36.3 6.1 %all-to-all-start.1 = ((f32[8,176,128]{2,1,0:T(8,128)}), f32[8,176,128]{2,1,0:T(8,128)S(1)}, u32[]{:S(2)}, u32[]{:S(2)}) async-start(f32[8,176,128]{2,1,0:T(8,128)} %get-tuple-element.24), calls=%async_computation.1 | async-start | bytes 1441792 | tf_op jit(solution)/shard_map/all_to_all | solution.py:710
  42.4 0.0 copy-start.6
  42.4 1.2 %add.27 = f32[320,512]{1,0:T(8,128)S(1)} add(f32[320,512]{1,0:T(8,128)} %copy-done.3, f32[320,512]{1,0:T(8,128)S(1)} %collective-permute-done.2) | non-fusion elementwise | flops 163840 | bytes 1966080 | tf_op jit(solution)/shard_map/add | solution.py:678
  43.7 0.6 collective-permute-start.3
  44.3 15.8 %collective-permute-done.3 = f32[320,512]{1,0:T(8,128)S(1)} collective-permute-done((f32[320,512]{1,0:T(8,128)S(1)}, f32[320,512]{1,0:T(8,128)S(1)}, u32[]{:S(2)}, u32[]{:S(2)}) %collective-permute-start.3) | collective-permute-done | bytes 655392 | tf_op jit(solution)/shard_map/ppermute | solution.py:674
  60.1 0.1 add.28.mine_ref
  60.2 0.1 collective-permute-start.4
  60.3 1.0 %all-to-all-done.1 = f32[8,176,128]{2,1,0:T(8,128)S(1)} async-done(((f32[8,176,128]{2,1,0:T(8,128)}), f32[8,176,128]{2,1,0:T(8,128)S(1)}, u32[]{:S(2)}, u32[]{:S(2)}) %all-to-all-start.1) | async-done | bytes 720928 | tf_op jit(solution)/shard_map/all_to_all | solution.py:710
  61.4 1.6 %rim_spectra.1 = (f32[2,2,5,8,720]{4,3,2,1,0:T(8,128)S(1)}, f32[80,512]{1,0:T(8,128)S(1)}, f32[80,512]{1,0:T(8,128)S(1)}, f32[8,128]{1,0:T(8,128)S(1)}) custom-call(f32[1408,128]{1,0:T(8,128)S(1)} %bitcast.5, bf16[512,720]{1,0:T(8,128)(2,1)S(1)} %copy-done.1, bf16[512,720]{1,0:T(8,128)(2,1)S(1)} %copy-done, f32[4,1,512]{2,1,0:T(1,128)S(1)} %copy-done.4, ...), custom_call_target="tpu_custom_call" | custom-call | flops 353894400 | bytes 3000000 | tf_op jit(solution)/shard_map/rim_spectra/pallas_call | solution.py:573
  63.0 0.1 collective-permute-start.5
  63.0 1.4 %collective-permute-done.5 = f32[80,512]{1,0:T(8,128)S(1)} collective-permute-done((f32[80,512]{1,0:T(8,128)S(1)}, f32[80,512]{1,0:T(8,128)S(1)}, u32[]{:S(2)}, u32[]{:S(2)}) %collective-permute-start.5) | collective-permute-done | bytes 163872 | tf_op jit(solution)/shard_map/ppermute | solution.py:674
  64.4 0.7 collective-permute-start.6
  65.2 5.4 %main.1 = (f32[5,3,8,8,720]{4,3,2,1,0:T(8,128)}, f32[1,512]{1,0:T(1,128)S(1)}) custom-call(s32[2]{0:T(128)S(1)} %copy-done.7, s32[3]{0:T(128)S(1)} %copy-done.6, s32[192]{0:T(256)S(1)} %copy-done.5, f32[5,3,8,8,720]{4,3,2,1,0:T(8,128)} %state_ref.3, f32[5,3,8,8,720]{4,3,2,1,0:T(8,128)} %get-tuple-element.20.base_ref, ...), custom_call_target="tpu_custom_call", output_to_operand_aliasing={{0}: (4, {})} | custom-call | flops 1415577600 | bytes 6000000 | tf_op jit(solution)/shard_map/main/pallas_call | solution.py:495
  70.6 0.2 collective-permute-done.6
  70.8 0.1 collective-permute-start.7
  70.9 1.4 %collective-permute-done.7.away_ref = f32[80,512]{1,0:T(8,128)S(1)} collective-permute-done((f32[80,512]{1,0:T(8,128)S(1)}, f32[80,512]{1,0:T(8,128)S(1)}, u32[]{:S(2)}, u32[]{:S(2)}) %collective-permute-start.7) | collective-permute-done | bytes 163872 | tf_op jit(solution)/shard_map/ppermute | solution.py:674
  72.2 2.6 %final.1 = f32[5,3,8,8,720]{4,3,2,1,0:T(8,128)} custom-call(f32[5,3,8,8,720]{4,3,2,1,0:T(8,128)} %get-tuple-element.26.main_ref, f32[2,2,5,8,720]{4,3,2,1,0:T(8,128)S(1)} %get-tuple-element.27.pair_ref, f32[1408,128]{1,0:T(8,128)S(1)} %bitcast.6, f32[80,512]{1,0:T(8,128)S(1)} %add_add_fusion.mine_ref, ...), custom_call_target="tpu_custom_call", output_to_operand_aliasing={{}: (0, {})} | custom-call | flops 353894400 | bytes 4000000 | tf_op jit(solution)/shard_map/final/pallas_call | solution.py:654
  (20 shorter events, 0.1 us)
Async XLA Ops:
  2.5 29.0 %all-to-all-start = ((f32[8,192,128]{2,1,0:T(8,128)}), f32[8,192,128]{2,1,0:T(8,128)S(1)}, u32[]{:S(2)}, u32[]{:S(2)}) async-start(f32[8,192,128]{2,1,0:T(8,128)} %bitcast.8), calls=%async_computation | async-start | bytes 1572864 | tf_op jit(solution)/shard_map/all_to_all | solution.py:700
  12.0 19.5 %copy-start.5 = (s32[192]{0:T(256)S(1)}, s32[192]{0:T(256)}, u32[]{:S(2)}) copy-start(s32[192]{0:T(256)} %cutoff_ref.7) | copy-start | bytes 2308
  12.0 3.3 %collective-permute-start = (f32[3,8,128]{2,1,0:T(8,128)}, f32[3,8,128]{2,1,0:T(8,128)S(1)}, u32[]{:S(2)}, u32[]{:S(2)}) collective-permute-start(f32[3,8,128]{2,1,0:T(8,128)} %get-tuple-element.18), channel_id=1, source_target_pairs={{0,1},{1,2},{2,3},{3,0},{4,5},{5,6},{6,7},{7,4},{8,9},{9,10},{10,1... | collective-permute-start | bytes 36872 | tf_op jit(solution)/shard_map/ppermute | solution.py:703
  12.0 3.4 %collective-permute-start.1 = (f32[3,8,128]{2,1,0:T(8,128)}, f32[3,8,128]{2,1,0:T(8,128)S(1)}, u32[]{:S(2)}, u32[]{:S(2)}) collective-permute-start(f32[3,8,128]{2,1,0:T(8,128)} %get-tuple-element.19), channel_id=1, source_target_pairs={{1,0},{2,1},{3,2},{0,3},{5,4},{6,5},{7,6},{4,7},{9,8},{10,9},{11,1... | collective-permute-start | bytes 36872 | tf_op jit(solution)/shard_map/ppermute | solution.py:704
  15.3 0.6 copy-start.8
  15.9 0.6 copy-start.9
  30.1 12.3 %collective-permute-start.2 = (f32[320,512]{1,0:T(8,128)}, f32[320,512]{1,0:T(8,128)S(1)}, u32[]{:S(2)}, u32[]{:S(2)}) collective-permute-start(f32[320,512]{1,0:T(8,128)} %get-tuple-element.23), channel_id=1, source_target_pairs={{0,1},{1,0},{2,3},{3,2},{4,5},{5,4},{6,7},{7,6},{8,9},{9,8},{10,11... | collective-permute-start | bytes 1966088 | tf_op jit(solution)/shard_map/ppermute | solution.py:674
  31.5 1.1 %copy-start.2 = (f32[320,512]{1,0:T(8,128)S(1)}, f32[320,512]{1,0:T(8,128)}, u32[]{:S(2)}) copy-start(f32[320,512]{1,0:T(8,128)} %get-tuple-element.21.later_in_ref) | copy-start | bytes 1966084
  35.4 0.8 %copy-start.3 = (f32[320,512]{1,0:T(8,128)}, f32[320,512]{1,0:T(8,128)S(1)}, u32[]{:S(2)}) copy-start(f32[320,512]{1,0:T(8,128)S(1)} %get-tuple-element.22) | copy-start | bytes 1966084
  36.3 25.1 %copy-start = (bf16[512,720]{1,0:T(8,128)(2,1)S(1)}, bf16[512,720]{1,0:T(8,128)(2,1)}, u32[]{:S(2)}) copy-start(bf16[512,720]{1,0:T(8,128)(2,1)} %constant.30.clone.low_ref) | copy-start | bytes 2211844
  36.3 25.1 %copy-start.1 = (bf16[512,720]{1,0:T(8,128)(2,1)S(1)}, bf16[512,720]{1,0:T(8,128)(2,1)}, u32[]{:S(2)}) copy-start(bf16[512,720]{1,0:T(8,128)(2,1)} %constant.29.clone.high_ref) | copy-start | bytes 2211844
  36.3 25.1 %copy-start.4 = (f32[4,1,512]{2,1,0:T(1,128)S(1)}, f32[4,1,512]{2,1,0:T(1,128)}, u32[]{:S(2)}) copy-start(f32[4,1,512]{2,1,0:T(1,128)} %constant.31.clone.turn_ref) | copy-start | bytes 24580
  36.3 25.1 %copy-start.7 = (s32[2]{0:T(128)S(1)}, s32[2]{0:T(128)}, u32[]{:S(2)}) copy-start(s32[2]{0:T(128)} %pad_add_fusion.place_ref) | copy-start | bytes 28
  36.3 25.1 %all-to-all-start.1 = ((f32[8,176,128]{2,1,0:T(8,128)}), f32[8,176,128]{2,1,0:T(8,128)S(1)}, u32[]{:S(2)}, u32[]{:S(2)}) async-start(f32[8,176,128]{2,1,0:T(8,128)} %get-tuple-element.24), calls=%async_computation.1 | async-start | bytes 1441792 | tf_op jit(solution)/shard_map/all_to_all | solution.py:710
  42.4 22.7 %copy-start.6 = (s32[3]{0:T(128)S(1)}, s32[3]{0:T(128)}, u32[]{:S(2)}) copy-start(s32[3]{0:T(128)} %block_ref.7) | copy-start | bytes 40
  43.7 16.4 %collective-permute-start.3 = (f32[320,512]{1,0:T(8,128)S(1)}, f32[320,512]{1,0:T(8,128)S(1)}, u32[]{:S(2)}, u32[]{:S(2)}) collective-permute-start(f32[320,512]{1,0:T(8,128)S(1)} %add.27), channel_id=1, source_target_pairs={{0,2},{1,3},{2,0},{3,1},{4,6},{5,7},{6,4},{7,5},{8,10},{9,11},{10,... | collective-permute-start | bytes 1966088 | tf_op jit(solution)/shard_map/ppermute | solution.py:674
  60.2 4.9 %collective-permute-start.4 = (f32[320,512]{1,0:T(8,128)S(1)}, f32[320,512]{1,0:T(8,128)}, u32[]{:S(2)}, u32[]{:S(2)}) collective-permute-start(f32[320,512]{1,0:T(8,128)S(1)} %add.28.mine_ref), channel_id=1, source_target_pairs={{0,1},{1,0},{2,3},{3,2},{4,5},{5,4},{6,7},{7,6},{8,9},{9,8},{10,11... | collective-permute-start | bytes 1966088 | tf_op jit(solution)/shard_map/ppermute | solution.py:674
  63.0 1.5 %collective-permute-start.5 = (f32[80,512]{1,0:T(8,128)S(1)}, f32[80,512]{1,0:T(8,128)S(1)}, u32[]{:S(2)}, u32[]{:S(2)}) collective-permute-start(f32[80,512]{1,0:T(8,128)S(1)} %get-tuple-element.29), channel_id=1, source_target_pairs={{0,1},{1,0},{2,3},{3,2},{4,5},{5,4},{6,7},{7,6},{8,9},{9,8},{10,11... | collective-permute-start | bytes 491528 | tf_op jit(solution)/shard_map/ppermute | solution.py:674
  64.4 6.3 %collective-permute-start.6 = (f32[80,512]{1,0:T(8,128)S(1)}, f32[80,512]{1,0:T(8,128)S(1)}, u32[]{:S(2)}, u32[]{:S(2)}) collective-permute-start(f32[80,512]{1,0:T(8,128)S(1)} %add.29), channel_id=1, source_target_pairs={{0,2},{1,3},{2,0},{3,1},{4,6},{5,7},{6,4},{7,5},{8,10},{9,11},{10,... | collective-permute-start | bytes 491528 | tf_op jit(solution)/shard_map/ppermute | solution.py:674
  70.8 1.5 %collective-permute-start.7 = (f32[80,512]{1,0:T(8,128)S(1)}, f32[80,512]{1,0:T(8,128)S(1)}, u32[]{:S(2)}, u32[]{:S(2)}) collective-permute-start(f32[80,512]{1,0:T(8,128)S(1)} %add_add_fusion.mine_ref), channel_id=1, source_target_pairs={{0,1},{1,0},{2,3},{3,2},{4,5},{5,4},{6,7},{7,6},{8,9},{9,8},{10,11... | collective-permute-start | bytes 491528 | tf_op jit(solution)/shard_map/ppermute | solution.py:674

commit v6 on v2

--- a/solution.py
+++ b/solution.py
@@ -123,7 +123,7 @@
     )(state, state, courant_x)
 
 
-PIECE = 192
+PIECE = 200
 BACK = 176
 TAIL = 80
 SPARE = LANES - TAIL
@@ -145,25 +145,24 @@
     def put(row, tile):
         out_ref[pl.ds(row, 8, stride=PIECE), :] = tile
 
-    tails = []
     for j in range(slots):
         half = wind_ref[j, 0] * 0.5
-        north = [last_ref[f, j, 0] * half for f in range(fields)]
-        south = [first_ref[f, j, 0] for f in range(fields)]
-        for t in range(tiles - 1):
-            put(55 * j + 25 + t, tile_of(half, t, width))
-            for f in range(fields):
-                put(55 * j + t * fields + f, tile_of(north[f], t, width))
-                put(55 * j + 30 + t * fields + f, tile_of(south[f], t, width))
-        tails.append([tile_of(slab, tiles - 1, width) for slab in (*north, half, *south)])
-    for u, (a, b, c) in enumerate(zip(*tails)):
-        put(165 + u, jnp.where(lane < TAIL, a, pltpu.roll(c, TAIL, 1)))
-        put(176 + u, jnp.where(lane < TAIL, b, pltpu.roll(c, LANES - 2 * SPARE, 1)))
+        for t in range(tiles):
+            row = {0: 192 + 2 * j, 1: 193 + 2 * j, 2: 64 * j + 62, 3: 64 * j + 63}.get(
+                t, 64 * j + 26 + t
+            )
+            put(row, tile_of(half, t, width))
+        for f in range(fields):
+            north = last_ref[f, j, 0] * half
+            south = first_ref[f, j, 0]
+            for t in range(tiles):
+                put(64 * j + t * fields + f, tile_of(north, t, width))
+                put(64 * j + 32 + t * fields + f, tile_of(south, t, width))
     table = jnp.zeros((8, LANES), jnp.int32)
     for j in range(slots):
         table = jnp.where(lane == j, block_ref[j], table)
-    for row in range(187, PIECE):
-        put(row, table.astype(F32))
+    put(198, table.astype(F32))
+    put(199, table.astype(F32))
 
 
 def pack(state, courant_y, block):
@@ -191,8 +190,6 @@
     out_ref,
     later_ref,
     face_ref,
-    south_ref,
-    half_ref,
     whole_ref,
     table_ref,
     slot_ref,
@@ -202,38 +199,35 @@
     parts = got_ref.shape[0]
     slots = face_ref.shape[0] // parts
     count = parts * slots
-    whole_ref[...] = got_ref[:, 184:192, :].astype(jnp.int32)
+    whole_ref[...] = got_ref[:, 192:200, :].astype(jnp.int32)
     copy = pltpu.make_async_copy(whole_ref, table_ref, sem)
     copy.start()
     lane = lax.broadcasted_iota(jnp.int32, (8, LANES), 1)
-    wide = lax.broadcasted_iota(jnp.int32, (16, LANES), 1)
-    tails = []
-    for s in range(count):
-        src, j = divmod(s, slots)
-        if j < 2:
-            tail = got_ref[src, 165 + 11 * j : 176 + 11 * j, :]
-        else:
-            one = pltpu.roll(got_ref[src, 165:181, :], SPARE, 1)
-            two = pltpu.roll(got_ref[src, 176:192, :], 2 * SPARE, 1)
-            tail = jnp.where(wide < SPARE, one, two)[:11]
-        south_ref[s, :25] = got_ref[src, 55 * j + 30 : 55 * j + 55, :]
-        south_ref[s, 25:30] = tail[6:]
-        face_ref[s, :25] = got_ref[src, 55 * j : 55 * j + 25, :]
-        face_ref[s, 25:30] = tail[:5]
-        half_ref[s, :5] = got_ref[src, 55 * j + 25 : 55 * j + 30, :]
-        half_ref[s, 5:6] = tail[5:6]
     copy.wait()
-    blocks = [table_ref[s // slots, 3, s % slots] for s in range(count)]
+    blocks = [table_ref[s // slots, 6, s % slots] for s in range(count)]
     slot_ref[0] = -1
     slot_ref[count + 1] = -1
     for s in range(count):
         slot_ref[blocks[s] + 1] = s
     for s in range(count):
+        src, j = divmod(s, slots)
         south = slot_ref[blocks[s] + 2]
-        half = jnp.concatenate(
-            [jnp.broadcast_to(half_ref[s, t : t + 1], (5, LANES)) for t in range(6)], axis=0
-        )
-        face = face_ref[s, :30] + half * south_ref[jnp.maximum(south, 0), :30]
+        safe = jnp.maximum(south, 0)
+        from_src = lax.div(safe, slots)
+        from_slot = safe - from_src * slots
+        half = [
+            jnp.broadcast_to(got_ref[src, row : row + 1, :], (5, LANES))
+            for row in (
+                192 + 2 * j,
+                193 + 2 * j,
+                64 * j + 62,
+                64 * j + 63,
+                64 * j + 30,
+                64 * j + 31,
+            )
+        ]
+        other = got_ref[from_src, pl.ds(pl.multiple_of(64 * from_slot + 32, 32), 32), :]
+        face = got_ref[src, 64 * j : 64 * j + 30, :] + jnp.concatenate(half, axis=0) * other[:30]
         face_ref[s, :30] = jnp.where(south >= 0, face, 0.0)
     for d in range(parts):
         first, second, rest = pick_slots(blocks[slots * d : slots * d + slots], cutoff_ref, 8)
@@ -274,8 +268,6 @@
         input_output_aliases={2: 1},
         scratch_shapes=[
             pltpu.VMEM((parts * slots, 32, LANES), F32),
-            pltpu.VMEM((parts * slots, 32, LANES), F32),
-            pltpu.VMEM((parts * slots, 8, LANES), F32),
             pltpu.VMEM((parts, 8, LANES), jnp.int32),
             pltpu.SMEM((parts, 8, LANES), jnp.int32),
             pltpu.SMEM((parts * slots + 2,), jnp.int32),

time: 74.2 us -> 73.2 us (0.987)
  local copies, waits for them, and re-layouts: 1.79 us -> 0.91 us
    unnamed x24 -> x22, local copies, waits for them, and re-layouts: 1.79 us -> 0.91 us
  transfers between devices with their start and end apart: 10 -> 10, of which waited for: 6 -> 6; matrix products, arithmetic and copies ran while one was open for 2% -> 2% of each run, Pallas kernels for 34% -> 35%
where the time goes in v6:
time: 73.2 us; the launch traced here: 72.8 us
  Pallas kernels  30.1 us (41%)
  waiting for transfers between devices  21.6 us (30%)
  starting transfers between devices  18.5 us (25%)
  other arithmetic  1.4 us (2%)
  local copies, waits for them, and re-layouts  0.91 us (1%)
    ppermute x6, waiting for transfers between devices, swap(): return lax.ppermute(array, 'lon', [(i, i ^ bit) for i in range(size)])  19 us
    pallas_call x1, Pallas kernels, local_tendency(): pl.pallas_call(tendency_kernel, in_specs=vmem(8) + smem(3), out_specs=[pl...  12.6 us
    all_to_all x1, starting transfers between devices, shards(): got = lax.all_to_all(sent, 'lat', 0, 0, tiled=True)  7.28 us
    all_to_all x1, starting transfers between devices, shards(): back = lax.all_to_all(back, 'lat', 0, 0, tiled=True)  6.12 us
    pallas_call x1, Pallas kernels, main_part(): pl.pallas_call(main_kernel, grid_spec=pltpu.PrefetchScalarGridSpec(num_sc...  5.36 us
    pallas_call x1, Pallas kernels, faces_of_pieces(): pl.pallas_call(face_kernel, in_specs=vmem(1) + smem(1) + [pl.BlockSpec(me...  3.45 us
    ppermute x6, starting transfers between devices, swap(): return lax.ppermute(array, 'lon', [(i, i ^ bit) for i in range(size)])  3.39 us
    pallas_call x1, Pallas kernels, final_part(): pl.pallas_call(functools.partial(final_kernel, back.ndim == 2), grid=(2,)...  2.57 us
  transfers between devices with their start and end apart: 10, of which 6 were waited for; matrix products, arithmetic and copies ran while one was open for 2% of the time, Pallas kernels for 35%

profile of v6, /device:TPU:0, one launch (start us, length us, event | category | flops | bytes accessed | tf_op | source)
XLA Modules:
  0.0 72.8 jit_solution(8861822551013684199)
XLA Ops:
  0.0 2.2 %pack.1 = f32[1600,128]{1,0:T(8,128)} custom-call(f32[5,3,8,8,720]{4,3,2,1,0:T(8,128)} %state_ref.3, f32[5,3,8,8,720]{4,3,2,1,0:T(8,128)} %state_ref.3, f32[3,8,8,720]{3,2,1,0:T(8,128)} %wind_ref.3, s32[3]{0:T(128)} %block_ref.7), custom_call_target="tpu_custom_call" | custom-call | flops 100000 | bytes 1700000 | tf_op jit(solution)/shard_map/pack/pallas_call | solution.py:170
  2.2 7.3 %all-to-all-start = ((f32[8,200,128]{2,1,0:T(8,128)}), f32[8,200,128]{2,1,0:T(8,128)}, u32[]{:S(2)}, u32[]{:S(2)}) async-start(f32[8,200,128]{2,1,0:T(8,128)} %bitcast.8), calls=%async_computation | async-start | bytes 1638400 | tf_op jit(solution)/shard_map/all_to_all | solution.py:691
  9.5 0.0 copy-start.5
  9.5 0.0 copy-start.6
  9.5 0.0 copy-start.7
  9.6 2.4 %edges.1 = (f32[3,8,128]{2,1,0:T(8,128)}, f32[3,8,128]{2,1,0:T(8,128)}) custom-call(f32[5,3,8,8,720]{4,3,2,1,0:T(8,128)} %state_ref.3, f32[5,3,8,8,720]{4,3,2,1,0:T(8,128)} %state_ref.3, f32[3,8,8,720]{3,2,1,0:T(8,128)} %cx_ref.1), custom_call_target="tpu_custom_call" | custom-call | flops 100000 | bytes 1200000 | tf_op jit(solution)/shard_map/edges/pallas_call | solution.py:111
  12.0 1.7 %collective-permute-start.1 = (f32[3,8,128]{2,1,0:T(8,128)}, f32[3,8,128]{2,1,0:T(8,128)S(1)}, u32[]{:S(2)}, u32[]{:S(2)}) collective-permute-start(f32[3,8,128]{2,1,0:T(8,128)} %get-tuple-element.19), channel_id=1, source_target_pairs={{1,0},{2,1},{3,2},{0,3},{5,4},{6,5},{7,6},{4,7},{9,8},{10,9},{11,1... | collective-permute-start | bytes 36872 | tf_op jit(solution)/shard_map/ppermute | solution.py:695
  13.7 0.1 pad_add_fusion.place_ref
  13.8 1.5 %collective-permute-done.west_ref = f32[3,8,128]{2,1,0:T(8,128)S(1)} collective-permute-done((f32[3,8,128]{2,1,0:T(8,128)}, f32[3,8,128]{2,1,0:T(8,128)S(1)}, u32[]{:S(2)}, u32[]{:S(2)}) %collective-permute-start) | collective-permute-done | bytes 12320 | tf_op jit(solution)/shard_map/ppermute | solution.py:694
  15.3 0.0 collective-permute-done.1.east_ref
  15.4 12.6 %tendency.1 = (f32[5,3,8,8,720]{4,3,2,1,0:T(8,128)}, f32[320,512]{1,0:T(8,128)S(1)}, f32[320,512]{1,0:T(8,128)}) custom-call(f32[5,3,8,8,720]{4,3,2,1,0:T(8,128)} %state_ref.3, f32[3,8,8,720]{3,2,1,0:T(8,128)S(1)} %copy-done.3, f32[3,8,8,720]{3,2,1,0:T(8,128)S(1)} %copy-done.4, f32[3,8,128]{2,1,0:T(8,128)S(1)} %collective-permute-done.west_ref, ...), custom_call_target="tpu_custom_call" | custom-call | flops 1415577600 | bytes 9000000 | tf_op jit(solution)/shard_map/tendency/pallas_call | solution.py:421
  28.0 0.8 %copy-done.2 = f32[320,512]{1,0:T(8,128)} copy-done((f32[320,512]{1,0:T(8,128)}, f32[320,512]{1,0:T(8,128)S(1)}, u32[]{:S(2)}) %copy-start.2) | copy-done | bytes 655384
  28.8 2.0 %collective-permute-start.2 = (f32[320,512]{1,0:T(8,128)}, f32[320,512]{1,0:T(8,128)S(1)}, u32[]{:S(2)}, u32[]{:S(2)}) collective-permute-start(f32[320,512]{1,0:T(8,128)} %get-tuple-element.23), channel_id=1, source_target_pairs={{0,1},{1,0},{2,3},{3,2},{4,5},{5,4},{6,7},{7,6},{8,9},{9,8},{10,11... | collective-permute-start | bytes 1966088 | tf_op jit(solution)/shard_map/ppermute | solution.py:665
  30.8 3.4 %faces.1 = (f32[8,176,128]{2,1,0:T(8,128)}, f32[320,512]{1,0:T(8,128)}) custom-call(f32[8,200,128]{2,1,0:T(8,128)} %all-to-all-done.got_ref, s32[192]{0:T(256)} %cutoff_ref.7, f32[320,512]{1,0:T(8,128)} %copy-done.2), custom_call_target="tpu_custom_call", output_to_operand_aliasing={{1}: (2, {})} | custom-call | flops 100000 | bytes 1600000 | tf_op jit(solution)/shard_map/faces/pallas_call | solution.py:260
  34.3 0.0 copy-start
  34.3 0.0 copy-start.1
  34.3 6.1 %all-to-all-start.1 = ((f32[8,176,128]{2,1,0:T(8,128)}), f32[8,176,128]{2,1,0:T(8,128)S(1)}, u32[]{:S(2)}, u32[]{:S(2)}) async-start(f32[8,176,128]{2,1,0:T(8,128)} %get-tuple-element.24), calls=%async_computation.1 | async-start | bytes 1441792 | tf_op jit(solution)/shard_map/all_to_all | solution.py:701
  40.5 1.2 %add.27 = f32[320,512]{1,0:T(8,128)S(1)} add(f32[320,512]{1,0:T(8,128)} %get-tuple-element.22, f32[320,512]{1,0:T(8,128)S(1)} %collective-permute-done.2) | non-fusion elementwise | flops 163840 | bytes 1966080 | tf_op jit(solution)/shard_map/add | solution.py:669
  41.6 0.6 collective-permute-start.3
  42.2 15.8 %collective-permute-done.3 = f32[320,512]{1,0:T(8,128)S(1)} collective-permute-done((f32[320,512]{1,0:T(8,128)S(1)}, f32[320,512]{1,0:T(8,128)S(1)}, u32[]{:S(2)}, u32[]{:S(2)}) %collective-permute-start.3) | collective-permute-done | bytes 655392 | tf_op jit(solution)/shard_map/ppermute | solution.py:665
  58.1 0.1 add.28.mine_ref
  58.2 0.1 collective-permute-start.4
  58.3 1.1 %all-to-all-done.1 = f32[8,176,128]{2,1,0:T(8,128)S(1)} async-done(((f32[8,176,128]{2,1,0:T(8,128)}), f32[8,176,128]{2,1,0:T(8,128)S(1)}, u32[]{:S(2)}, u32[]{:S(2)}) %all-to-all-start.1) | async-done | bytes 720928 | tf_op jit(solution)/shard_map/all_to_all | solution.py:701
  59.4 1.6 %rim_spectra.1 = (f32[2,2,5,8,720]{4,3,2,1,0:T(8,128)S(1)}, f32[80,512]{1,0:T(8,128)S(1)}, f32[80,512]{1,0:T(8,128)S(1)}, f32[8,128]{1,0:T(8,128)S(1)}) custom-call(f32[1408,128]{1,0:T(8,128)S(1)} %bitcast.5, bf16[512,720]{1,0:T(8,128)(2,1)S(1)} %copy-done.1, bf16[512,720]{1,0:T(8,128)(2,1)S(1)} %copy-done, f32[4,1,512]{2,1,0:T(1,128)S(1)} %copy-done.7, ...), custom_call_target="tpu_custom_call" | custom-call | flops 353894400 | bytes 3000000 | tf_op jit(solution)/shard_map/rim_spectra/pallas_call | solution.py:564
  60.9 0.1 collective-permute-start.5
  61.0 1.4 %collective-permute-done.5 = f32[80,512]{1,0:T(8,128)S(1)} collective-permute-done((f32[80,512]{1,0:T(8,128)S(1)}, f32[80,512]{1,0:T(8,128)S(1)}, u32[]{:S(2)}, u32[]{:S(2)}) %collective-permute-start.5) | collective-permute-done | bytes 163872 | tf_op jit(solution)/shard_map/ppermute | solution.py:665
  62.4 0.6 collective-permute-start.6
  63.0 5.4 %main.1 = (f32[5,3,8,8,720]{4,3,2,1,0:T(8,128)}, f32[1,512]{1,0:T(1,128)S(1)}) custom-call(s32[2]{0:T(128)S(1)} %pad_add_fusion.place_ref, s32[3]{0:T(128)S(1)} %copy-done.10, s32[192]{0:T(256)S(1)} %copy-done.9, f32[5,3,8,8,720]{4,3,2,1,0:T(8,128)} %state_ref.3, f32[5,3,8,8,720]{4,3,2,1,0:T(8,128)} %get-tuple-element.20.base_ref, ...), custom_call_target="tpu_custom_call", output_to_operand_aliasing={{0}: (4, {})} | custom-call | flops 1415577600 | bytes 6000000 | tf_op jit(solution)/shard_map/main/pallas_call | solution.py:486
  68.4 0.4 collective-permute-done.6
  68.8 0.1 collective-permute-start.7
  68.8 1.4 %collective-permute-done.7.away_ref = f32[80,512]{1,0:T(8,128)S(1)} collective-permute-done((f32[80,512]{1,0:T(8,128)S(1)}, f32[80,512]{1,0:T(8,128)S(1)}, u32[]{:S(2)}, u32[]{:S(2)}) %collective-permute-start.7) | collective-permute-done | bytes 163872 | tf_op jit(solution)/shard_map/ppermute | solution.py:665
  70.2 2.6 %final.1 = f32[5,3,8,8,720]{4,3,2,1,0:T(8,128)} custom-call(f32[5,3,8,8,720]{4,3,2,1,0:T(8,128)} %get-tuple-element.26.main_ref, f32[2,2,5,8,720]{4,3,2,1,0:T(8,128)S(1)} %get-tuple-element.27.pair_ref, f32[1408,128]{1,0:T(8,128)S(1)} %bitcast.6, f32[80,512]{1,0:T(8,128)S(1)} %add_add_fusion.mine_ref, ...), custom_call_target="tpu_custom_call", output_to_operand_aliasing={{}: (0, {})} | custom-call | flops 353894400 | bytes 4000000 | tf_op jit(solution)/shard_map/final/pallas_call | solution.py:645
  (22 shorter events, 0.1 us)
Async XLA Ops:
  2.2 28.6 %all-to-all-start = ((f32[8,200,128]{2,1,0:T(8,128)}), f32[8,200,128]{2,1,0:T(8,128)}, u32[]{:S(2)}, u32[]{:S(2)}) async-start(f32[8,200,128]{2,1,0:T(8,128)} %bitcast.8), calls=%async_computation | async-start | bytes 1638400 | tf_op jit(solution)/shard_map/all_to_all | solution.py:691
  9.5 5.8 %copy-start.3 = (f32[3,8,8,720]{3,2,1,0:T(8,128)S(1)}, f32[3,8,8,720]{3,2,1,0:T(8,128)}, u32[]{:S(2)}) copy-start(f32[3,8,8,720]{3,2,1,0:T(8,128)} %cx_ref.1) | copy-start | bytes 1658884
  9.5 5.8 %copy-start.4 = (f32[3,8,8,720]{3,2,1,0:T(8,128)S(1)}, f32[3,8,8,720]{3,2,1,0:T(8,128)}, u32[]{:S(2)}) copy-start(f32[3,8,8,720]{3,2,1,0:T(8,128)} %wind_ref.3) | copy-start | bytes 1658884
  9.5 5.8 %copy-start.5 = (bf16[720,512]{1,0:T(8,128)(2,1)S(1)}, bf16[720,512]{1,0:T(8,128)(2,1)}, u32[]{:S(2)}) copy-start(bf16[720,512]{1,0:T(8,128)(2,1)} %constant.28.clone.low_ref) | copy-start | bytes 2211844
  9.5 5.8 %copy-start.6 = (bf16[720,512]{1,0:T(8,128)(2,1)S(1)}, bf16[720,512]{1,0:T(8,128)(2,1)}, u32[]{:S(2)}) copy-start(bf16[720,512]{1,0:T(8,128)(2,1)} %constant.27.clone.high_ref) | copy-start | bytes 2211844
  9.5 5.8 %copy-start.7 = (f32[4,1,512]{2,1,0:T(1,128)S(1)}, f32[4,1,512]{2,1,0:T(1,128)}, u32[]{:S(2)}) copy-start(f32[4,1,512]{2,1,0:T(1,128)} %constant.31.clone.turn_ref) | copy-start | bytes 24580
  9.5 5.8 %copy-start.8 = (s32[192]{0:T(256)S(1)}, s32[192]{0:T(256)}, u32[]{:S(2)}) copy-start(s32[192]{0:T(256)} %cutoff_ref.7) | copy-start | bytes 2308
  9.6 5.8 %copy-start.10 = (s32[3]{0:T(128)S(1)}, s32[3]{0:T(128)}, u32[]{:S(2)}) copy-start(s32[3]{0:T(128)} %block_ref.7) | copy-start | bytes 40
  12.0 3.3 %collective-permute-start = (f32[3,8,128]{2,1,0:T(8,128)}, f32[3,8,128]{2,1,0:T(8,128)S(1)}, u32[]{:S(2)}, u32[]{:S(2)}) collective-permute-start(f32[3,8,128]{2,1,0:T(8,128)} %get-tuple-element.18), channel_id=1, source_target_pairs={{0,1},{1,2},{2,3},{3,0},{4,5},{5,6},{6,7},{7,4},{8,9},{9,10},{10,1... | collective-permute-start | bytes 36872 | tf_op jit(solution)/shard_map/ppermute | solution.py:694
  12.0 3.4 %collective-permute-start.1 = (f32[3,8,128]{2,1,0:T(8,128)}, f32[3,8,128]{2,1,0:T(8,128)S(1)}, u32[]{:S(2)}, u32[]{:S(2)}) collective-permute-start(f32[3,8,128]{2,1,0:T(8,128)} %get-tuple-element.19), channel_id=1, source_target_pairs={{1,0},{2,1},{3,2},{0,3},{5,4},{6,5},{7,6},{4,7},{9,8},{10,9},{11,1... | collective-permute-start | bytes 36872 | tf_op jit(solution)/shard_map/ppermute | solution.py:695
  28.0 0.9 %copy-start.2 = (f32[320,512]{1,0:T(8,128)}, f32[320,512]{1,0:T(8,128)S(1)}, u32[]{:S(2)}) copy-start(f32[320,512]{1,0:T(8,128)S(1)} %get-tuple-element.21.later_in_ref) | copy-start | bytes 1966084
  28.8 11.6 %collective-permute-start.2 = (f32[320,512]{1,0:T(8,128)}, f32[320,512]{1,0:T(8,128)S(1)}, u32[]{:S(2)}, u32[]{:S(2)}) collective-permute-start(f32[320,512]{1,0:T(8,128)} %get-tuple-element.23), channel_id=1, source_target_pairs={{0,1},{1,0},{2,3},{3,2},{4,5},{5,4},{6,7},{7,6},{8,9},{9,8},{10,11... | collective-permute-start | bytes 1966088 | tf_op jit(solution)/shard_map/ppermute | solution.py:665
  34.3 25.1 %copy-start = (bf16[512,720]{1,0:T(8,128)(2,1)S(1)}, bf16[512,720]{1,0:T(8,128)(2,1)}, u32[]{:S(2)}) copy-start(bf16[512,720]{1,0:T(8,128)(2,1)} %constant.30.clone.low_ref) | copy-start | bytes 2211844
  34.3 25.1 %copy-start.1 = (bf16[512,720]{1,0:T(8,128)(2,1)S(1)}, bf16[512,720]{1,0:T(8,128)(2,1)}, u32[]{:S(2)}) copy-start(bf16[512,720]{1,0:T(8,128)(2,1)} %constant.29.clone.high_ref) | copy-start | bytes 2211844
  34.3 25.0 %all-to-all-start.1 = ((f32[8,176,128]{2,1,0:T(8,128)}), f32[8,176,128]{2,1,0:T(8,128)S(1)}, u32[]{:S(2)}, u32[]{:S(2)}) async-start(f32[8,176,128]{2,1,0:T(8,128)} %get-tuple-element.24), calls=%async_computation.1 | async-start | bytes 1441792 | tf_op jit(solution)/shard_map/all_to_all | solution.py:701
  40.4 22.6 %copy-start.9 = (s32[192]{0:T(256)S(1)}, s32[192]{0:T(256)}, u32[]{:S(2)}) copy-start(s32[192]{0:T(256)} %cutoff_ref.7) | copy-start | bytes 2308
  41.6 16.4 %collective-permute-start.3 = (f32[320,512]{1,0:T(8,128)S(1)}, f32[320,512]{1,0:T(8,128)S(1)}, u32[]{:S(2)}, u32[]{:S(2)}) collective-permute-start(f32[320,512]{1,0:T(8,128)S(1)} %add.27), channel_id=1, source_target_pairs={{0,2},{1,3},{2,0},{3,1},{4,6},{5,7},{6,4},{7,5},{8,10},{9,11},{10,... | collective-permute-start | bytes 1966088 | tf_op jit(solution)/shard_map/ppermute | solution.py:665
  58.2 4.8 %collective-permute-start.4 = (f32[320,512]{1,0:T(8,128)S(1)}, f32[320,512]{1,0:T(8,128)}, u32[]{:S(2)}, u32[]{:S(2)}) collective-permute-start(f32[320,512]{1,0:T(8,128)S(1)} %add.28.mine_ref), channel_id=1, source_target_pairs={{0,1},{1,0},{2,3},{3,2},{4,5},{5,4},{6,7},{7,6},{8,9},{9,8},{10,11... | collective-permute-start | bytes 1966088 | tf_op jit(solution)/shard_map/ppermute | solution.py:665
  60.9 1.5 %collective-permute-start.5 = (f32[80,512]{1,0:T(8,128)S(1)}, f32[80,512]{1,0:T(8,128)S(1)}, u32[]{:S(2)}, u32[]{:S(2)}) collective-permute-start(f32[80,512]{1,0:T(8,128)S(1)} %get-tuple-element.29), channel_id=1, source_target_pairs={{0,1},{1,0},{2,3},{3,2},{4,5},{5,4},{6,7},{7,6},{8,9},{9,8},{10,11... | collective-permute-start | bytes 491528 | tf_op jit(solution)/shard_map/ppermute | solution.py:665
  62.4 6.3 %collective-permute-start.6 = (f32[80,512]{1,0:T(8,128)S(1)}, f32[80,512]{1,0:T(8,128)S(1)}, u32[]{:S(2)}, u32[]{:S(2)}) collective-permute-start(f32[80,512]{1,0:T(8,128)S(1)} %add.29), channel_id=1, source_target_pairs={{0,2},{1,3},{2,0},{3,1},{4,6},{5,7},{6,4},{7,5},{8,10},{9,11},{10,... | collective-permute-start | bytes 491528 | tf_op jit(solution)/shard_map/ppermute | solution.py:665
  68.8 1.5 %collective-permute-start.7 = (f32[80,512]{1,0:T(8,128)S(1)}, f32[80,512]{1,0:T(8,128)S(1)}, u32[]{:S(2)}, u32[]{:S(2)}) collective-permute-start(f32[80,512]{1,0:T(8,128)S(1)} %add_add_fusion.mine_ref), channel_id=1, source_target_pairs={{0,1},{1,0},{2,3},{3,2},{4,5},{5,4},{6,7},{7,6},{8,9},{9,8},{10,11... | collective-permute-start | bytes 491528 | tf_op jit(solution)/shard_map/ppermute | solution.py:665

commit v7 on v6

--- a/solution.py
+++ b/solution.py
@@ -186,16 +186,15 @@
 def face_kernel(
     got_ref,
     cutoff_ref,
-    later_in_ref,
     out_ref,
-    later_ref,
+    token_ref,
     face_ref,
     whole_ref,
     table_ref,
     slot_ref,
     sem,
 ):
-    del later_in_ref, later_ref
+    token_ref[...] = jnp.zeros_like(token_ref)
     parts = got_ref.shape[0]
     slots = face_ref.shape[0] // parts
     count = parts * slots
@@ -255,17 +254,16 @@
         out_ref[d, 170:BACK] = jnp.zeros((BACK - 170, LANES), F32)
 
 
-def faces_of_pieces(got, slots, cutoff, later):
+def faces_of_pieces(got, slots, cutoff):
     parts = got.shape[0]
     return pl.pallas_call(
         face_kernel,
-        in_specs=vmem(1) + smem(1) + [pl.BlockSpec(memory_space=pl.ANY)],
-        out_specs=vmem(1) + [pl.BlockSpec(memory_space=pl.ANY)],
+        in_specs=vmem(1) + smem(1),
+        out_specs=vmem(2),
         out_shape=[
             jax.ShapeDtypeStruct((parts, BACK, LANES), F32),
-            jax.ShapeDtypeStruct(later.shape, F32),
+            jax.ShapeDtypeStruct((1, 2 * KCUT), F32),
         ],
-        input_output_aliases={2: 1},
         scratch_shapes=[
             pltpu.VMEM((parts * slots, 32, LANES), F32),
             pltpu.VMEM((parts, 8, LANES), jnp.int32),
@@ -275,7 +273,7 @@
         ],
         cost_estimate=pl.CostEstimate(flops=10**5, bytes_accessed=1600000, transcendentals=0),
         name="faces",
-    )(got, cutoff, later)
+    )(got, cutoff)
 
 
 def to_pieces(units, parts):
@@ -697,7 +695,8 @@
         state, courant_x, courant_y, west, east, forward, *tables
     )
     if packed:
-        back, mine = faces_of_pieces(got, slots, cutoff, mine)
+        back, token = faces_of_pieces(got, slots, cutoff)
+        mine = mine + token
         back = lax.all_to_all(back, "lat", 0, 0, tiled=True)
         pair = rest = back.reshape(lat * BACK, LANES)
     else:

time: 73.2 us -> 72.3 us (0.988)
  local copies, waits for them, and re-layouts: 0.91 us -> 0.06 us
    unnamed x22 -> x20, local copies, waits for them, and re-layouts: 0.91 us -> 0.06 us
  transfers between devices with their start and end apart: 10 -> 10, of which waited for: 6 -> 7; matrix products, arithmetic and copies ran while one was open for 2% -> 2% of each run, Pallas kernels for 35% -> 35%
where the time goes in v7:
time: 72.3 us; the launch traced here: 71.9 us
  Pallas kernels  30 us (41%)
  waiting for transfers between devices  22.2 us (31%)
  starting transfers between devices  18 us (25%)
  other arithmetic  1.46 us (2%)
    ppermute x6, waiting for transfers between devices, swap(): return lax.ppermute(array, 'lon', [(i, i ^ bit) for i in range(size)])  19.1 us
    pallas_call x1, Pallas kernels, local_tendency(): pl.pallas_call(tendency_kernel, in_specs=vmem(8) + smem(3), out_specs=[pl...  12.5 us
    all_to_all x1, starting transfers between devices, shards(): got = lax.all_to_all(sent, 'lat', 0, 0, tiled=True)  7.28 us
    all_to_all x1, starting transfers between devices, shards(): back = lax.all_to_all(back, 'lat', 0, 0, tiled=True)  5.48 us
    pallas_call x1, Pallas kernels, main_part(): pl.pallas_call(main_kernel, grid_spec=pltpu.PrefetchScalarGridSpec(num_sc...  5.3 us
    ppermute x6, starting transfers between devices, swap(): return lax.ppermute(array, 'lon', [(i, i ^ bit) for i in range(size)])  3.47 us
    pallas_call x1, Pallas kernels, faces_of_pieces(): pl.pallas_call(face_kernel, in_specs=vmem(1) + smem(1), out_specs=vmem(2)...  3.44 us
    pallas_call x1, Pallas kernels, final_part(): pl.pallas_call(functools.partial(final_kernel, back.ndim == 2), grid=(2,)...  2.56 us
  transfers between devices with their start and end apart: 10, of which 7 were waited for; matrix products, arithmetic and copies ran while one was open for 2% of the time, Pallas kernels for 35%

profile of v7, /device:TPU:0, one launch (start us, length us, event | category | flops | bytes accessed | tf_op | source)
XLA Modules:
  0.0 71.9 jit_solution(10784743228660061555)
XLA Ops:
  0.0 2.2 %pack.1 = f32[1600,128]{1,0:T(8,128)} custom-call(f32[5,3,8,8,720]{4,3,2,1,0:T(8,128)} %state_ref.3, f32[5,3,8,8,720]{4,3,2,1,0:T(8,128)} %state_ref.3, f32[3,8,8,720]{3,2,1,0:T(8,128)} %wind_ref.3, s32[3]{0:T(128)} %block_ref.7), custom_call_target="tpu_custom_call" | custom-call | flops 100000 | bytes 1700000 | tf_op jit(solution)/shard_map/pack/pallas_call | solution.py:170
  2.2 7.3 %all-to-all-start = ((f32[8,200,128]{2,1,0:T(8,128)}), f32[8,200,128]{2,1,0:T(8,128)}, u32[]{:S(2)}, u32[]{:S(2)}) async-start(f32[8,200,128]{2,1,0:T(8,128)} %bitcast.9), calls=%async_computation | async-start | bytes 1638400 | tf_op jit(solution)/shard_map/all_to_all | solution.py:689
  9.5 0.0 copy-start.4
  9.5 0.0 copy-start.5
  9.5 0.0 copy-start.6
  9.6 2.4 %edges.1 = (f32[3,8,128]{2,1,0:T(8,128)}, f32[3,8,128]{2,1,0:T(8,128)}) custom-call(f32[5,3,8,8,720]{4,3,2,1,0:T(8,128)} %state_ref.3, f32[5,3,8,8,720]{4,3,2,1,0:T(8,128)} %state_ref.3, f32[3,8,8,720]{3,2,1,0:T(8,128)} %cx_ref.1), custom_call_target="tpu_custom_call" | custom-call | flops 100000 | bytes 1200000 | tf_op jit(solution)/shard_map/edges/pallas_call | solution.py:111
  12.0 1.7 %collective-permute-start.1 = (f32[3,8,128]{2,1,0:T(8,128)}, f32[3,8,128]{2,1,0:T(8,128)S(1)}, u32[]{:S(2)}, u32[]{:S(2)}) collective-permute-start(f32[3,8,128]{2,1,0:T(8,128)} %get-tuple-element.19), channel_id=1, source_target_pairs={{1,0},{2,1},{3,2},{0,3},{5,4},{6,5},{7,6},{4,7},{9,8},{10,9},{11,1... | collective-permute-start | bytes 36872 | tf_op jit(solution)/shard_map/ppermute | solution.py:693
  13.7 0.1 pad_add_fusion.place_ref
  13.8 1.5 %collective-permute-done.west_ref = f32[3,8,128]{2,1,0:T(8,128)S(1)} collective-permute-done((f32[3,8,128]{2,1,0:T(8,128)}, f32[3,8,128]{2,1,0:T(8,128)S(1)}, u32[]{:S(2)}, u32[]{:S(2)}) %collective-permute-start) | collective-permute-done | bytes 12320 | tf_op jit(solution)/shard_map/ppermute | solution.py:692
  15.3 0.0 collective-permute-done.1.east_ref
  15.4 12.5 %tendency.1 = (f32[5,3,8,8,720]{4,3,2,1,0:T(8,128)}, f32[320,512]{1,0:T(8,128)S(1)}, f32[320,512]{1,0:T(8,128)}) custom-call(f32[5,3,8,8,720]{4,3,2,1,0:T(8,128)} %state_ref.3, f32[3,8,8,720]{3,2,1,0:T(8,128)S(1)} %copy-done.2, f32[3,8,8,720]{3,2,1,0:T(8,128)S(1)} %copy-done.3, f32[3,8,128]{2,1,0:T(8,128)S(1)} %collective-permute-done.west_ref, ...), custom_call_target="tpu_custom_call" | custom-call | flops 1415577600 | bytes 9000000 | tf_op jit(solution)/shard_map/tendency/pallas_call | solution.py:419
  27.9 0.0 copy-start
  27.9 0.0 copy-start.1
  27.9 2.0 %collective-permute-start.2 = (f32[320,512]{1,0:T(8,128)}, f32[320,512]{1,0:T(8,128)}, u32[]{:S(2)}, u32[]{:S(2)}) collective-permute-start(f32[320,512]{1,0:T(8,128)} %get-tuple-element.23), channel_id=1, source_target_pairs={{0,1},{1,0},{2,3},{3,2},{4,5},{5,4},{6,7},{7,6},{8,9},{9,8},{10,11... | collective-permute-start | bytes 1966088 | tf_op jit(solution)/shard_map/ppermute | solution.py:663
  30.0 0.5 all-to-all-done.got_ref
  30.5 3.4 %faces.1 = (f32[8,176,128]{2,1,0:T(8,128)}, f32[1,512]{1,0:T(1,128)}) custom-call(f32[8,200,128]{2,1,0:T(8,128)} %all-to-all-done.got_ref, s32[192]{0:T(256)} %cutoff_ref.7), custom_call_target="tpu_custom_call" | custom-call | flops 100000 | bytes 1600000 | tf_op jit(solution)/shard_map/faces/pallas_call | solution.py:259
  33.9 5.5 %all-to-all-start.1 = ((f32[8,176,128]{2,1,0:T(8,128)}), f32[8,176,128]{2,1,0:T(8,128)S(1)}, u32[]{:S(2)}, u32[]{:S(2)}) async-start(f32[8,176,128]{2,1,0:T(8,128)} %get-tuple-element.24), calls=%async_computation.1 | async-start | bytes 1441792 | tf_op jit(solution)/shard_map/all_to_all | solution.py:700
  39.4 1.2 %add_add_fusion = f32[320,512]{1,0:T(8,128)S(1)} fusion(f32[320,512]{1,0:T(8,128)} %collective-permute-done.2, f32[320,512]{1,0:T(8,128)S(1)} %get-tuple-element.21, f32[512]{0:T(512)} %bitcast.10), kind=kLoop, calls=%fused_computation | loop fusion | flops 327680 | bytes 1968128 | tf_op jit(solution)/shard_map/add | solution.py:667
  40.7 0.6 collective-permute-start.3
  41.3 15.9 %collective-permute-done.3 = f32[320,512]{1,0:T(8,128)S(1)} collective-permute-done((f32[320,512]{1,0:T(8,128)S(1)}, f32[320,512]{1,0:T(8,128)S(1)}, u32[]{:S(2)}, u32[]{:S(2)}) %collective-permute-start.3) | collective-permute-done | bytes 655392 | tf_op jit(solution)/shard_map/ppermute | solution.py:663
  57.2 0.1 add.41.mine_ref
  57.3 0.1 collective-permute-start.4
  57.4 1.0 %all-to-all-done.1 = f32[8,176,128]{2,1,0:T(8,128)S(1)} async-done(((f32[8,176,128]{2,1,0:T(8,128)}), f32[8,176,128]{2,1,0:T(8,128)S(1)}, u32[]{:S(2)}, u32[]{:S(2)}) %all-to-all-start.1) | async-done | bytes 720928 | tf_op jit(solution)/shard_map/all_to_all | solution.py:700
  58.5 1.6 %rim_spectra.1 = (f32[2,2,5,8,720]{4,3,2,1,0:T(8,128)S(1)}, f32[80,512]{1,0:T(8,128)S(1)}, f32[80,512]{1,0:T(8,128)S(1)}, f32[8,128]{1,0:T(8,128)S(1)}) custom-call(f32[1408,128]{1,0:T(8,128)S(1)} %bitcast.6, bf16[512,720]{1,0:T(8,128)(2,1)S(1)} %copy-done.1, bf16[512,720]{1,0:T(8,128)(2,1)S(1)} %copy-done, f32[4,1,512]{2,1,0:T(1,128)S(1)} %copy-done.6, ...), custom_call_target="tpu_custom_call" | custom-call | flops 353894400 | bytes 3000000 | tf_op jit(solution)/shard_map/rim_spectra/pallas_call | solution.py:562
  60.0 0.1 collective-permute-start.5
  60.1 1.4 %collective-permute-done.5 = f32[80,512]{1,0:T(8,128)S(1)} collective-permute-done((f32[80,512]{1,0:T(8,128)S(1)}, f32[80,512]{1,0:T(8,128)S(1)}, u32[]{:S(2)}, u32[]{:S(2)}) %collective-permute-start.5) | collective-permute-done | bytes 163872 | tf_op jit(solution)/shard_map/ppermute | solution.py:663
  61.5 0.6 collective-permute-start.6
  62.1 5.3 %main.1 = (f32[5,3,8,8,720]{4,3,2,1,0:T(8,128)}, f32[1,512]{1,0:T(1,128)S(1)}) custom-call(s32[2]{0:T(128)S(1)} %pad_add_fusion.place_ref, s32[3]{0:T(128)S(1)} %copy-done.9, s32[192]{0:T(256)S(1)} %copy-done.8, f32[5,3,8,8,720]{4,3,2,1,0:T(8,128)} %state_ref.3, f32[5,3,8,8,720]{4,3,2,1,0:T(8,128)} %get-tuple-element.20.base_ref, ...), custom_call_target="tpu_custom_call", output_to_operand_aliasing={{0}: (4, {})} | custom-call | flops 1415577600 | bytes 6000000 | tf_op jit(solution)/shard_map/main/pallas_call | solution.py:484
  67.4 0.4 collective-permute-done.6
  67.9 0.1 collective-permute-start.7
  67.9 1.4 %collective-permute-done.7.away_ref = f32[80,512]{1,0:T(8,128)S(1)} collective-permute-done((f32[80,512]{1,0:T(8,128)S(1)}, f32[80,512]{1,0:T(8,128)S(1)}, u32[]{:S(2)}, u32[]{:S(2)}) %collective-permute-start.7) | collective-permute-done | bytes 163872 | tf_op jit(solution)/shard_map/ppermute | solution.py:663
  69.3 2.6 %final.1 = f32[5,3,8,8,720]{4,3,2,1,0:T(8,128)} custom-call(f32[5,3,8,8,720]{4,3,2,1,0:T(8,128)} %get-tuple-element.26.main_ref, f32[2,2,5,8,720]{4,3,2,1,0:T(8,128)S(1)} %get-tuple-element.27.pair_ref, f32[1408,128]{1,0:T(8,128)S(1)} %bitcast.7, f32[80,512]{1,0:T(8,128)S(1)} %add_add_fusion.1.mine_ref, ...), custom_call_target="tpu_custom_call", output_to_operand_aliasing={{}: (0, {})} | custom-call | flops 353894400 | bytes 4000000 | tf_op jit(solution)/shard_map/final/pallas_call | solution.py:643
  (20 shorter events, 0.1 us)
Async XLA Ops:
  2.2 28.3 %all-to-all-start = ((f32[8,200,128]{2,1,0:T(8,128)}), f32[8,200,128]{2,1,0:T(8,128)}, u32[]{:S(2)}, u32[]{:S(2)}) async-start(f32[8,200,128]{2,1,0:T(8,128)} %bitcast.9), calls=%async_computation | async-start | bytes 1638400 | tf_op jit(solution)/shard_map/all_to_all | solution.py:689
  9.5 5.8 %copy-start.2 = (f32[3,8,8,720]{3,2,1,0:T(8,128)S(1)}, f32[3,8,8,720]{3,2,1,0:T(8,128)}, u32[]{:S(2)}) copy-start(f32[3,8,8,720]{3,2,1,0:T(8,128)} %cx_ref.1) | copy-start | bytes 1658884
  9.5 5.8 %copy-start.3 = (f32[3,8,8,720]{3,2,1,0:T(8,128)S(1)}, f32[3,8,8,720]{3,2,1,0:T(8,128)}, u32[]{:S(2)}) copy-start(f32[3,8,8,720]{3,2,1,0:T(8,128)} %wind_ref.3) | copy-start | bytes 1658884
  9.5 5.8 %copy-start.4 = (bf16[720,512]{1,0:T(8,128)(2,1)S(1)}, bf16[720,512]{1,0:T(8,128)(2,1)}, u32[]{:S(2)}) copy-start(bf16[720,512]{1,0:T(8,128)(2,1)} %constant.28.clone.low_ref) | copy-start | bytes 2211844
  9.5 5.8 %copy-start.5 = (bf16[720,512]{1,0:T(8,128)(2,1)S(1)}, bf16[720,512]{1,0:T(8,128)(2,1)}, u32[]{:S(2)}) copy-start(bf16[720,512]{1,0:T(8,128)(2,1)} %constant.27.clone.high_ref) | copy-start | bytes 2211844
  9.5 5.8 %copy-start.6 = (f32[4,1,512]{2,1,0:T(1,128)S(1)}, f32[4,1,512]{2,1,0:T(1,128)}, u32[]{:S(2)}) copy-start(f32[4,1,512]{2,1,0:T(1,128)} %constant.31.clone.turn_ref) | copy-start | bytes 24580
  9.5 5.8 %copy-start.7 = (s32[192]{0:T(256)S(1)}, s32[192]{0:T(256)}, u32[]{:S(2)}) copy-start(s32[192]{0:T(256)} %cutoff_ref.7) | copy-start | bytes 2308
  9.6 5.8 %copy-start.9 = (s32[3]{0:T(128)S(1)}, s32[3]{0:T(128)}, u32[]{:S(2)}) copy-start(s32[3]{0:T(128)} %block_ref.7) | copy-start | bytes 40
  12.0 3.3 %collective-permute-start = (f32[3,8,128]{2,1,0:T(8,128)}, f32[3,8,128]{2,1,0:T(8,128)S(1)}, u32[]{:S(2)}, u32[]{:S(2)}) collective-permute-start(f32[3,8,128]{2,1,0:T(8,128)} %get-tuple-element.18), channel_id=1, source_target_pairs={{0,1},{1,2},{2,3},{3,0},{4,5},{5,6},{6,7},{7,4},{8,9},{9,10},{10,1... | collective-permute-start | bytes 36872 | tf_op jit(solution)/shard_map/ppermute | solution.py:692
  12.0 3.4 %collective-permute-start.1 = (f32[3,8,128]{2,1,0:T(8,128)}, f32[3,8,128]{2,1,0:T(8,128)S(1)}, u32[]{:S(2)}, u32[]{:S(2)}) collective-permute-start(f32[3,8,128]{2,1,0:T(8,128)} %get-tuple-element.19), channel_id=1, source_target_pairs={{1,0},{2,1},{3,2},{0,3},{5,4},{6,5},{7,6},{4,7},{9,8},{10,9},{11,1... | collective-permute-start | bytes 36872 | tf_op jit(solution)/shard_map/ppermute | solution.py:693
  27.9 30.6 %copy-start = (bf16[512,720]{1,0:T(8,128)(2,1)S(1)}, bf16[512,720]{1,0:T(8,128)(2,1)}, u32[]{:S(2)}) copy-start(bf16[512,720]{1,0:T(8,128)(2,1)} %constant.30.clone.low_ref) | copy-start | bytes 2211844
  27.9 30.5 %copy-start.1 = (bf16[512,720]{1,0:T(8,128)(2,1)S(1)}, bf16[512,720]{1,0:T(8,128)(2,1)}, u32[]{:S(2)}) copy-start(bf16[512,720]{1,0:T(8,128)(2,1)} %constant.29.clone.high_ref) | copy-start | bytes 2211844
  27.9 11.5 %collective-permute-start.2 = (f32[320,512]{1,0:T(8,128)}, f32[320,512]{1,0:T(8,128)}, u32[]{:S(2)}, u32[]{:S(2)}) collective-permute-start(f32[320,512]{1,0:T(8,128)} %get-tuple-element.23), channel_id=1, source_target_pairs={{0,1},{1,0},{2,3},{3,2},{4,5},{5,4},{6,7},{7,6},{8,9},{9,8},{10,11... | collective-permute-start | bytes 1966088 | tf_op jit(solution)/shard_map/ppermute | solution.py:663
  33.9 24.5 %all-to-all-start.1 = ((f32[8,176,128]{2,1,0:T(8,128)}), f32[8,176,128]{2,1,0:T(8,128)S(1)}, u32[]{:S(2)}, u32[]{:S(2)}) async-start(f32[8,176,128]{2,1,0:T(8,128)} %get-tuple-element.24), calls=%async_computation.1 | async-start | bytes 1441792 | tf_op jit(solution)/shard_map/all_to_all | solution.py:700
  39.4 22.7 %copy-start.8 = (s32[192]{0:T(256)S(1)}, s32[192]{0:T(256)}, u32[]{:S(2)}) copy-start(s32[192]{0:T(256)} %cutoff_ref.7) | copy-start | bytes 2308
  40.7 16.5 %collective-permute-start.3 = (f32[320,512]{1,0:T(8,128)S(1)}, f32[320,512]{1,0:T(8,128)S(1)}, u32[]{:S(2)}, u32[]{:S(2)}) collective-permute-start(f32[320,512]{1,0:T(8,128)S(1)} %add_add_fusion), channel_id=1, source_target_pairs={{0,2},{1,3},{2,0},{3,1},{4,6},{5,7},{6,4},{7,5},{8,10},{9,11},{10,... | collective-permute-start | bytes 1966088 | tf_op jit(solution)/shard_map/ppermute | solution.py:663
  57.3 4.8 %collective-permute-start.4 = (f32[320,512]{1,0:T(8,128)S(1)}, f32[320,512]{1,0:T(8,128)}, u32[]{:S(2)}, u32[]{:S(2)}) collective-permute-start(f32[320,512]{1,0:T(8,128)S(1)} %add.41.mine_ref), channel_id=1, source_target_pairs={{0,1},{1,0},{2,3},{3,2},{4,5},{5,4},{6,7},{7,6},{8,9},{9,8},{10,11... | collective-permute-start | bytes 1966088 | tf_op jit(solution)/shard_map/ppermute | solution.py:663
  60.0 1.5 %collective-permute-start.5 = (f32[80,512]{1,0:T(8,128)S(1)}, f32[80,512]{1,0:T(8,128)S(1)}, u32[]{:S(2)}, u32[]{:S(2)}) collective-permute-start(f32[80,512]{1,0:T(8,128)S(1)} %get-tuple-element.29), channel_id=1, source_target_pairs={{0,1},{1,0},{2,3},{3,2},{4,5},{5,4},{6,7},{7,6},{8,9},{9,8},{10,11... | collective-permute-start | bytes 491528 | tf_op jit(solution)/shard_map/ppermute | solution.py:663
  61.5 6.3 %collective-permute-start.6 = (f32[80,512]{1,0:T(8,128)S(1)}, f32[80,512]{1,0:T(8,128)S(1)}, u32[]{:S(2)}, u32[]{:S(2)}) collective-permute-start(f32[80,512]{1,0:T(8,128)S(1)} %add.42), channel_id=1, source_target_pairs={{0,2},{1,3},{2,0},{3,1},{4,6},{5,7},{6,4},{7,5},{8,10},{9,11},{10,... | collective-permute-start | bytes 491528 | tf_op jit(solution)/shard_map/ppermute | solution.py:663
  67.9 1.5 %collective-permute-start.7 = (f32[80,512]{1,0:T(8,128)S(1)}, f32[80,512]{1,0:T(8,128)S(1)}, u32[]{:S(2)}, u32[]{:S(2)}) collective-permute-start(f32[80,512]{1,0:T(8,128)S(1)} %add_add_fusion.1.mine_ref), channel_id=1, source_target_pairs={{0,1},{1,0},{2,3},{3,2},{4,5},{5,4},{6,7},{7,6},{8,9},{9,8},{10,11... | collective-permute-start | bytes 491528 | tf_op jit(solution)/shard_map/ppermute | solution.py:663
